TPU v7x, 32 devices: a whole 2x2x4 slice. The times are simulated.
32 devices in a mesh: tm: 4 (over x, core), space: 8 (over z, y).
Axes of the slice: x: 2, y: 2, z: 4, core: 2. Of those that a mesh axis runs over, the one named last changes fastest.
Arguments:
- adjoint_field: float32 [512, 24, 9216], P('tm', 'space'), may hold values from -6 to 6
- absorption: float32 [24, 9216], P('space'), may hold values from 0.25 to 2
- mode_rates: float32 [16], replicated, may hold values from 0.1 to 40
- mode_weights: float32 [16], replicated, may hold values from 0.1 to 0.5
Outputs:
- adjoint_image: float32 [512, 24, 9216], P('tm', 'space')
All inputs are finite; a program needn't handle non-finite values.
Results may differ from a plain program's by a relative error of at most 0.0001.
Values sent between devices are 32-bit elements; how exact they have to be, the bound alone decides.
No kernel may reach another device: no remote copies, remote signals or barrier semaphores. Data moves between devices by JAX's collectives and lax.ppermute only.
A program may use at most 192 MiB of HBM per device.

v0:
```python
import jax
import jax.numpy as jnp
from jax import lax
from jax.sharding import PartitionSpec as P

NY = 96
BAND = 16


DIFFUSION = 0.2
ORDER_EXP = 0.4
STENCIL = (-1.0 / 12.0, 16.0 / 12.0, -30.0 / 12.0, 16.0 / 12.0, -1.0 / 12.0)


def shifted(block, axis, distance):
    devices = range(lax.axis_size(axis))
    route = [(i - distance, i) for i in devices if i - distance in devices]
    return lax.ppermute(block, axis, route)


def with_halo(cells, sides, width):
    for axis, dim in sides:
        count = lax.axis_size(axis)
        ends = count - 1
        head = lax.slice_in_dim(cells, 0, width, axis=dim)
        tail = lax.slice_in_dim(cells, cells.shape[dim] - width, cells.shape[dim], axis=dim)
        cells = jnp.concatenate(
            [
                lax.ppermute(tail, axis, [(i, (i + 1) % count) for i in range(ends)]),
                cells,
                lax.ppermute(head, axis, [((i + 1) % count, i) for i in range(ends)]),
            ],
            axis=dim,
        )
    return cells


def caputo_weights(count):
    steps_idx = jnp.arange(count, dtype=jnp.float32)
    increments = (steps_idx + 1.0) ** ORDER_EXP - steps_idx**ORDER_EXP
    earlier = jnp.concatenate([jnp.zeros((1,), jnp.float32), increments[:-1]])
    return increments - earlier


def mode_tables(mode_rates, mode_weights, total_steps):
    scaled = mode_rates / total_steps
    decays = jnp.exp(-scaled)
    mode_gain = mode_weights * jnp.sqrt(-jnp.expm1(-2.0 * scaled))
    return (scaled, decays, mode_gain)


def plane_masks(row_len, plane_len):
    column = jnp.arange(plane_len, dtype=jnp.int32) % row_len
    return [
        ((column + offset >= 0) & (column + offset < row_len)).astype(jnp.float32)
        for offset in (-2, -1, 1, 2)
    ]


def laplacian(padded, slab_depth, row_len):
    plane_len = padded.shape[-1]
    center = padded[..., 2 : 2 + slab_depth, :]
    summed = 3.0 * STENCIL[2] * center
    for offset in (-2, -1, 1, 2):
        summed = summed + STENCIL[offset + 2] * padded[..., 2 + offset : 2 + offset + slab_depth, :]
    widths = [(0, 0)] * (center.ndim - 1) + [(2 * row_len, 2 * row_len)]
    spread = jnp.pad(center, widths)
    y_masks = plane_masks(row_len, plane_len)
    for position, offset in enumerate((-2, -1, 1, 2)):
        weight = STENCIL[offset + 2]
        anchor = 2 * row_len + offset * row_len
        summed = summed + weight * spread[..., anchor : anchor + plane_len]
        anchor = 2 * row_len + offset
        summed = summed + weight * y_masks[position] * spread[..., anchor : anchor + plane_len]
    return summed


def per_device(adjoint_field, absorption, mode_rates, mode_weights):
    steps_dev, slab_depth, plane_len = adjoint_field.shape
    group_count = lax.axis_size("tm")
    total_steps = steps_dev * group_count
    scaled, decays, mode_gain = mode_tables(mode_rates, mode_weights, total_steps)
    cell_count = slab_depth * plane_len
    next_head = shifted(adjoint_field[: BAND - 1], "tm", -1)
    extended = jnp.concatenate([adjoint_field, next_head], axis=0)
    span_len = steps_dev + BAND - 1
    row_idx = jnp.arange(steps_dev, dtype=jnp.int32)[:, None]
    col_idx = jnp.arange(span_len, dtype=jnp.int32)[None, :]
    lag_steps = col_idx - row_idx
    lag_clip = jnp.clip(lag_steps, 0, span_len).astype(jnp.float32)
    far_table = jnp.sum(
        mode_gain[:, None, None] * jnp.exp(-scaled[:, None, None] * lag_clip[None]), axis=0
    )
    band_onehot = (
        lag_steps[None, :, :] == jnp.arange(BAND, dtype=jnp.int32)[:, None, None]
    ).astype(jnp.float32)
    near_part = jnp.sum(caputo_weights(BAND)[:, None, None] * band_onehot, axis=0)
    inside = col_idx < steps_dev
    in_band = (lag_steps >= 0) & (lag_steps < BAND)
    kernel = jnp.where(
        inside,
        near_part + jnp.where(lag_steps >= BAND, far_table, 0.0),
        jnp.where(in_band, near_part - far_table, 0.0),
    )
    flat_field = extended.reshape(span_len, cell_count)
    history = jnp.dot(
        kernel, flat_field, precision=lax.Precision.HIGHEST, preferred_element_type=jnp.float32
    )
    step_pos = jnp.arange(steps_dev, dtype=jnp.float32)
    projector = jnp.exp(-scaled[:, None] * step_pos[None, :])
    block_sums = jnp.dot(
        projector,
        flat_field[:steps_dev],
        precision=lax.Precision.HIGHEST,
        preferred_element_type=jnp.float32,
    )
    block_decay = jnp.exp(-scaled * steps_dev)[:, None]

    def relay_step(turn_idx, carried):
        return shifted(block_sums + block_decay * carried, "tm", -1)

    carried = lax.fori_loop(0, group_count - 1, relay_step, jnp.zeros_like(block_sums))
    remote_gain = mode_gain[None, :] * jnp.exp(-scaled[None, :] * (steps_dev - step_pos)[:, None])
    history = history + jnp.dot(
        remote_gain, carried, precision=lax.Precision.HIGHEST, preferred_element_type=jnp.float32
    )
    padded = with_halo(adjoint_field, (("space", 1),), 2)
    diffusion_term = laplacian(padded, slab_depth, NY)
    outcome = (
        history.reshape(adjoint_field.shape)
        + absorption[None] * adjoint_field
        - DIFFUSION * diffusion_term
    )
    return outcome


def solution(mesh):
    return jax.shard_map(
        per_device,
        mesh=mesh,
        in_specs=(P("tm", "space", None), P("space", None), P(), P()),
        out_specs=P("tm", "space", None),
        check_vma=False,
    )
```

profile of v0, /device:TPU:0, one launch (start us, length us, event | category | flops | bytes accessed | tf_op | source)
XLA Modules:
  0.0 525.0 jit_solution(1414531785541494756)
XLA Ops:
  0.0 1.6 slice.57
  1.6 1.3 collective-permute-start.1
  2.9 15.1 %copy.29 = f32[128,3,9216]{0,2,1:T(8,128)} copy(f32[128,3,9216]{2,0,1:T(8,128)} %param.6) | data formatting | bytes 28311552 | tf_op args[0]
  18.0 13.2 %fusion.82 = (f32[128,2,9216]{0,2,1:T(8,128)}, f32[128,2,9216]{0,2,1:T(8,128)}) fusion(f32[128,3,9216]{0,2,1:T(8,128)} %copy.29), kind=kLoop, calls=%fused_computation.109 | loop fusion | bytes 37748736 | tf_op jit(solution)/shard_map/slice | solution.py:26
  31.2 8.5 %collective-permute-start.2 = (f32[128,2,9216]{0,2,1:T(8,128)}, f32[128,2,9216]{0,2,1:T(8,128)}, u32[]{:S(2)}, u32[]{:S(2)}) collective-permute-start(f32[128,2,9216]{0,2,1:T(8,128)} %get-tuple-element.36), channel_id=1, source_target_pairs={{0,1},{1,2},{2,3},{3,4},{4,5},{5,6},{6,7},{8,9},{9,10},{10,11},{11... | collective-permute-start | bytes 28311560 | tf_op jit(solution)/shard_map/ppermute | solution.py:29
  39.7 1.3 collective-permute-start.3
  44.0 14.2 %fusion.66 = f32[16,27648]{1,0:T(8,128)S(1)} fusion(f32[128,27648]{0,1:T(8,128)} %bitcast.14, f32[16]{0:T(128)S(1)} %get-tuple-element.39), kind=kOutput, calls=%fused_computation.85 | convolution fusion | flops 679479296 | bytes 15925312 | tf_op jit(solution)/shard_map/dot_general | solution.py:111
  58.2 6.8 %pad_maximum_fusion = f32[143,3,9216]{2,0,1:T(8,128)S(1)} fusion(f32[15,3,9216]{2,0,1:T(8,128)} %collective-permute-done.1, f32[128,3,9216]{2,0,1:T(8,128)} %param.6), kind=kLoop, calls=%fused_computation.6 | loop fusion | flops 3953664 | bytes 31629312 | tf_op jit(solution)/shard_map/concatenate | solution.py:85
  65.1 28.9 %copy.28 = f32[143,3,9216]{2,1,0:T(4,128)} copy(f32[143,3,9216]{2,0,1:T(8,128)S(1)} %pad_maximum_fusion) | data formatting | bytes 31629312 | tf_op jit(solution)/shard_map/concatenate | solution.py:85
  94.0 12.4 %pad.17 = f32[144,3,9216]{2,1,0:T(4,128)S(1)} pad(f32[143,3,9216]{2,1,0:T(4,128)} %copy.28, f32[]{:T(128)} %constant.18.clone.1), padding=0_1x0_0x0_0 | pad | bytes 31739908
  106.4 13.5 %copy.39 = f32[18,8,3,9216]{3,1,2,0:T(8,128)} copy(f32[18,8,3,9216]{3,2,1,0:T(4,128)S(1)} %bitcast.15) | data formatting | bytes 31850496
  119.9 19.6 %fusion.26 = f32[128,27648]{1,0:T(8,128)} fusion(f32[143,27648]{1,0:T(8,128)} %bitcast.16, f32[128,143]{0,1:T(8,128)S(1)} %get-tuple-element.42, f32[128,143]{0,1:T(8,128)S(1)} %get-tuple-element.41, pred[143]{0:T(512)(128)(4,1)S(1)} %copy-done.7), kind=kOutput, calls=%fused_computation.44 | convolution fusion | flops 6073011200 | bytes 30117008 | tf_op jit(solution)/shard_map/dot_general | solution.py:106
  139.7 59.4 %while.10 = (s32[]{:T(128)}, f32[16,27648]{1,0:T(8,128)S(1)}, f32[16,1]{0,1:T(1,128)S(1)}, f32[16,27648]{1,0:T(8,128)S(1)}, s32[]{:T(128)}) while((s32[]{:T(128)}, f32[16,27648]{1,0:T(8,128)S(1)}, f32[16,1]{0,1:T(1,128)S(1)}, f32[16,27648]{1,0:T(8,128)S(1)}, s32[]{:T(128)}) %tuple.24), condition=%wide.region_3.4_spmd, body=%wide.region_2.3_spmd.sunk | while | flops 884738 | bytes 12386469 | solution.py:122
  139.7 1.5 multiply_add_fusion.2
  142.4 4.8 collective-permute-done
  147.3 1.5 multiply_add_fusion.2
  150.0 23.1 %collective-permute-done = f32[16,27648]{1,0:T(8,128)S(1)} collective-permute-done((f32[16,27648]{1,0:T(8,128)}, f32[16,27648]{1,0:T(8,128)S(1)}, u32[]{:S(2)}, u32[]{:S(2)}) %collective-permute-start) | collective-permute-done | bytes 1769504 | tf_op jit(solution)/shard_map/while/body/eval_jaxpr/ppermute | solution.py:18
  173.2 1.5 multiply_add_fusion.2
  175.9 23.1 %collective-permute-done = f32[16,27648]{1,0:T(8,128)S(1)} collective-permute-done((f32[16,27648]{1,0:T(8,128)}, f32[16,27648]{1,0:T(8,128)S(1)}, u32[]{:S(2)}, u32[]{:S(2)}) %collective-permute-start) | collective-permute-done | bytes 1769504 | tf_op jit(solution)/shard_map/while/body/eval_jaxpr/ppermute | solution.py:18
  199.1 16.3 %convolution_add_fusion = f32[128,27648]{1,0:T(8,128)} fusion(f32[128,27648]{1,0:T(8,128)} %fusion.26, f32[16,27648]{1,0:T(8,128)S(1)} %get-tuple-element.27, f32[128]{0:T(128)S(1)} %iota_subtract_fusion.1, f32[16]{0:T(128)S(1)} %get-tuple-element.39, f32[16]{0:T(128)S(1)} %get-tuple-element.40), kind=kOutput, calls=%fused_computation.1 | convolution fusion | flops 683020288 | bytes 30081664 | tf_op jit(solution)/shard_map/dot_general | solution.py:124
  215.3 15.2 %copy.30 = f32[128,27648]{0,1:T(8,128)} copy(f32[128,27648]{1,0:T(8,128)} %convolution_add_fusion) | data formatting | bytes 28311552 | tf_op jit(solution)/shard_map/add | solution.py:124
  230.5 211.3 %collective-permute-done.2 = f32[128,2,9216]{0,2,1:T(8,128)} collective-permute-done((f32[128,2,9216]{0,2,1:T(8,128)}, f32[128,2,9216]{0,2,1:T(8,128)}, u32[]{:S(2)}, u32[]{:S(2)}) %collective-permute-start.2) | collective-permute-done | bytes 9437216 | tf_op jit(solution)/shard_map/ppermute | solution.py:29
  441.8 68.1 %fusion.13 = f32[128,3,9216]{0,2,1:T(8,128)} fusion(f32[128,3,9216]{0,2,1:T(8,128)} %copy.29, f32[128,2,9216]{0,2,1:T(8,128)} %collective-permute-done.3, f32[128,2,9216]{0,2,1:T(8,128)} %collective-permute-done.2, f32[128,3,9216]{0,2,1:T(8,128)} %bitcast.17, f32[9216]{0:T(1024)S(1)} %copy-done.3, f32[9216]{0:T(1024)S(1)} %copy-done.4, ...), kind=kLoop, calls=%fused_computation.20 | loop fusion | flops 116785152 | bytes 61599744 | tf_op jit(solution)/shard_map/sub | solution.py:130
  509.9 15.1 %copy.38 = f32[128,3,9216]{2,0,1:T(8,128)} copy(f32[128,3,9216]{0,2,1:T(8,128)} %fusion.13) | data formatting | bytes 28311552 | tf_op jit(solution)/shard_map/sub | solution.py:130
  (32 shorter events, 6.9 us)
Async XLA Ops:
  1.6 56.6 %collective-permute-start.1 = (f32[15,3,9216]{2,0,1:T(8,128)S(1)}, f32[15,3,9216]{2,0,1:T(8,128)}, u32[]{:S(2)}, u32[]{:S(2)}) collective-permute-start(f32[15,3,9216]{2,0,1:T(8,128)S(1)} %slice.57), channel_id=1, source_target_pairs={{8,0},{16,8},{24,16},{9,1},{17,9},{25,17},{10,2},{18,10},{26,18},{... | collective-permute-start | bytes 4976648 | tf_op jit(solution)/shard_map/ppermute | solution.py:18
  18.0 23.8 %copy-start.5 = (f32[16]{0:T(128)S(1)}, f32[16]{0:T(128)}, u32[]{:S(2)}) copy-start(f32[16]{0:T(128)} %param.8) | copy-start | bytes 196
  18.0 23.8 %copy-start.6 = (f32[16]{0:T(128)S(1)}, f32[16]{0:T(128)}, u32[]{:S(2)}) copy-start(f32[16]{0:T(128)} %param.9) | copy-start | bytes 196
  31.2 410.6 %collective-permute-start.2 = (f32[128,2,9216]{0,2,1:T(8,128)}, f32[128,2,9216]{0,2,1:T(8,128)}, u32[]{:S(2)}, u32[]{:S(2)}) collective-permute-start(f32[128,2,9216]{0,2,1:T(8,128)} %get-tuple-element.36), channel_id=1, source_target_pairs={{0,1},{1,2},{2,3},{3,4},{4,5},{5,6},{6,7},{8,9},{9,10},{10,11},{11... | collective-permute-start | bytes 28311560 | tf_op jit(solution)/shard_map/ppermute | solution.py:29
  39.7 402.0 %collective-permute-start.3 = (f32[128,2,9216]{0,2,1:T(8,128)}, f32[128,2,9216]{0,2,1:T(8,128)}, u32[]{:S(2)}, u32[]{:S(2)}) collective-permute-start(f32[128,2,9216]{0,2,1:T(8,128)} %get-tuple-element.37), channel_id=1, source_target_pairs={{1,0},{2,1},{3,2},{4,3},{5,4},{6,5},{7,6},{9,8},{10,9},{11,10},{12... | collective-permute-start | bytes 28311560 | tf_op jit(solution)/shard_map/ppermute | solution.py:31
  106.4 13.6 %copy-start.7 = (pred[143]{0:T(512)(128)(4,1)S(1)}, pred[143]{0:T(512)(128)(4,1)}, u32[]{:S(2)}) copy-start(pred[143]{0:T(512)(128)(4,1)} %iota_compare_fusion.1) | copy-start | bytes 433
  141.2 6.1 %collective-permute-start = (f32[16,27648]{1,0:T(8,128)}, f32[16,27648]{1,0:T(8,128)S(1)}, u32[]{:S(2)}, u32[]{:S(2)}) collective-permute-start(f32[16,27648]{1,0:T(8,128)} %multiply_add_fusion.2), channel_id=1, source_target_pairs={{8,0},{16,8},{24,16},{9,1},{17,9},{25,17},{10,2},{18,10},{26,18},{... | collective-permute-start | bytes 5308424 | tf_op jit(solution)/shard_map/while/body/eval_jaxpr/ppermute | solution.py:18
  148.7 24.4 %collective-permute-start = (f32[16,27648]{1,0:T(8,128)}, f32[16,27648]{1,0:T(8,128)S(1)}, u32[]{:S(2)}, u32[]{:S(2)}) collective-permute-start(f32[16,27648]{1,0:T(8,128)} %multiply_add_fusion.2), channel_id=1, source_target_pairs={{8,0},{16,8},{24,16},{9,1},{17,9},{25,17},{10,2},{18,10},{26,18},{... | collective-permute-start | bytes 5308424 | tf_op jit(solution)/shard_map/while/body/eval_jaxpr/ppermute | solution.py:18
  174.6 24.4 %collective-permute-start = (f32[16,27648]{1,0:T(8,128)}, f32[16,27648]{1,0:T(8,128)S(1)}, u32[]{:S(2)}, u32[]{:S(2)}) collective-permute-start(f32[16,27648]{1,0:T(8,128)} %multiply_add_fusion.2), channel_id=1, source_target_pairs={{8,0},{16,8},{24,16},{9,1},{17,9},{25,17},{10,2},{18,10},{26,18},{... | collective-permute-start | bytes 5308424 | tf_op jit(solution)/shard_map/while/body/eval_jaxpr/ppermute | solution.py:18
  215.3 226.5 %copy-start = (f32[3,9216]{1,0:T(4,128)S(1)}, f32[3,9216]{1,0:T(4,128)}, u32[]{:S(2)}) copy-start(f32[3,9216]{1,0:T(4,128)} %param.7) | copy-start | bytes 331780
  215.3 226.5 %copy-start.1 = (f32[9216]{0:T(1024)S(1)}, f32[9216]{0:T(1024)}, u32[]{:S(2)}) copy-start(f32[9216]{0:T(1024)} %get-tuple-element.45) | copy-start | bytes 110596
  215.3 226.5 %copy-start.2 = (f32[9216]{0:T(1024)S(1)}, f32[9216]{0:T(1024)}, u32[]{:S(2)}) copy-start(f32[9216]{0:T(1024)} %get-tuple-element.46) | copy-start | bytes 110596
  215.3 226.5 %copy-start.3 = (f32[9216]{0:T(1024)S(1)}, f32[9216]{0:T(1024)}, u32[]{:S(2)}) copy-start(f32[9216]{0:T(1024)} %get-tuple-element.43) | copy-start | bytes 110596
  215.3 226.5 %copy-start.4 = (f32[9216]{0:T(1024)S(1)}, f32[9216]{0:T(1024)}, u32[]{:S(2)}) copy-start(f32[9216]{0:T(1024)} %get-tuple-element.44) | copy-start | bytes 110596
where the time goes:
time: 527 us; the launch traced here: 525 us
  waiting for transfers between devices  262 us (50%)
  local copies, waits for them, and re-layouts  115 us (22%)
  other arithmetic  82.2 us (16%)
  matrix products  50.1 us (10%)
  starting transfers between devices  14.9 us (3%)
    ppermute x1, waiting for transfers between devices, with_halo(): lax.ppermute(tail, axis, [(i, (i + 1) % count) for i in range(ends)])  211 us
    sub x1, other arithmetic, per_device(): history.reshape(adjoint_field.shape) + absorption[None] * adjoint_field  68.1 us
    ppermute x4, waiting for transfers between devices, shifted(): return lax.ppermute(block, axis, route)  51.1 us
    unnamed x19, local copies, waits for them, and re-layouts  41 us
    concatenate x1, local copies, waits for them, and re-layouts, per_device(): extended = jnp.concatenate([adjoint_field, next_head], axis=0)  28.9 us
    dot_general x1, matrix products, per_device(): jnp.dot(kernel, flat_field, precision=lax.Precision.HIGHEST, preferred_el...  19.6 us
    dot_general x1, matrix products, per_device(): jnp.dot(remote_gain, carried, precision=lax.Precision.HIGHEST, preferred_...  16.3 us
    add x1, local copies, waits for them, and re-layouts, per_device(): history + jnp.dot(remote_gain, carried, precision=lax.Precision.HIGHEST,...  15.2 us
  transfers between devices with their start and end apart: 6, of which 4 were waited for; matrix products, arithmetic and copies ran while one was open for 31% of the time, Pallas kernels for 0%

commit v1 on v0

v1 whole, which is shorter than its diff:
```python
import functools

import jax
import jax.numpy as jnp
from jax import lax
from jax.experimental import pallas as pl
from jax.experimental.pallas import tpu as pltpu
from jax.sharding import PartitionSpec as P

NY = 96
BAND = 16

DIFFUSION = 0.2
ORDER_EXP = 0.4
STENCIL = (-1.0 / 12.0, 16.0 / 12.0, -30.0 / 12.0, 16.0 / 12.0, -1.0 / 12.0)
NEAR = -DIFFUSION * STENCIL[1]
FAR = -DIFFUSION * STENCIL[0]
OFFSETS = (-2, -1, 1, 2)
ROWS = 8
VMEM_LIMIT = 48 * 1024 * 1024


def tied(value, *others):
    return lax.optimization_barrier((value, *others))[0]


def caputo_weights(count):
    steps_idx = jnp.arange(count, dtype=jnp.float32)
    increments = (steps_idx + 1.0) ** ORDER_EXP - steps_idx**ORDER_EXP
    earlier = jnp.concatenate([jnp.zeros((1,), jnp.float32), increments[:-1]])
    return increments - earlier


def mode_tables(mode_rates, mode_weights, total_steps):
    scaled = mode_rates / total_steps
    mode_gain = mode_weights * jnp.sqrt(-jnp.expm1(-2.0 * scaled))
    return scaled, mode_gain


def history_tables(scaled, mode_gain, steps):
    span = steps + BAND
    lag = jnp.arange(span, dtype=jnp.int32)[None, :] - jnp.arange(steps, dtype=jnp.int32)[:, None]
    lag_clip = jnp.maximum(lag, 0).astype(jnp.float32)
    far = jnp.sum(
        mode_gain[:, None, None] * jnp.exp(-scaled[:, None, None] * lag_clip[None]), axis=0
    )
    onehot = (lag[None] == jnp.arange(BAND, dtype=jnp.int32)[:, None, None]).astype(jnp.float32)
    near = jnp.sum(caputo_weights(BAND)[:, None, None] * onehot, axis=0)
    own = near + jnp.where(lag >= BAND, far, 0.0)
    ahead = jnp.where((lag >= 0) & (lag < BAND), near - far, 0.0)
    pos = jnp.arange(steps, dtype=jnp.float32)
    projector = jnp.exp(-scaled[:, None] * pos[None, :])
    remote_gain = mode_gain[None, :] * jnp.exp(-scaled[None, :] * (steps - pos)[:, None])
    return own[:, :steps], ahead[:, steps:], projector, remote_gain


def dot(a, b):
    return jnp.dot(a, b, precision=lax.Precision.HIGHEST, preferred_element_type=jnp.float32)


def tile_of(plane):
    for count in range(4, plane + 1):
        if plane % count == 0 and (plane // count) % 128 == 0:
            return plane // count
    return plane


def sums_kernel(projector, field, sums):
    sums[...] = dot(projector[...], field[...])


def mode_sums(projector, field):
    depth, steps, plane = field.shape
    modes = projector.shape[0]
    tile = tile_of(plane)
    return pl.pallas_call(
        sums_kernel,
        grid=(depth, plane // tile),
        in_specs=[
            pl.BlockSpec((modes, steps), lambda p, c: (0, 0)),
            pl.BlockSpec((None, steps, tile), lambda p, c: (p, 0, c)),
        ],
        out_specs=pl.BlockSpec((None, modes, tile), lambda p, c: (p, 0, c)),
        out_shape=jax.ShapeDtypeStruct((depth, modes, plane), jnp.float32),
        compiler_params=pltpu.CompilerParams(vmem_limit_bytes=VMEM_LIMIT),
        cost_estimate=pl.CostEstimate(
            flops=12 * field.size * modes, bytes_accessed=4 * field.size, transcendentals=0
        ),
        name="mode_sums",
    )(projector, field)


def history_kernel(inner, outer, gain, field, head, later, history):
    history[...] = (
        dot(inner[...], field[...]) + dot(outer[...], head[...]) + dot(gain[...], later[...])
    )


def history_of(inner, outer, gain, field, head, later):
    depth, steps, plane = field.shape
    tile = tile_of(plane)
    whole = lambda p, c: (0, 0)
    part = lambda p, c: (p, 0, c)
    return pl.pallas_call(
        history_kernel,
        grid=(depth, plane // tile),
        in_specs=[
            pl.BlockSpec(inner.shape, whole),
            pl.BlockSpec(outer.shape, whole),
            pl.BlockSpec(gain.shape, whole),
            pl.BlockSpec((None, steps, tile), part),
            pl.BlockSpec((None, head.shape[1], tile), part),
            pl.BlockSpec((None, later.shape[1], tile), part),
        ],
        out_specs=pl.BlockSpec((None, steps, tile), part),
        out_shape=jax.ShapeDtypeStruct(field.shape, jnp.float32),
        compiler_params=pltpu.CompilerParams(vmem_limit_bytes=VMEM_LIMIT),
        cost_estimate=pl.CostEstimate(
            flops=12 * field.size * (steps + 2 * BAND),
            bytes_accessed=8 * field.size,
            transcendentals=0,
        ),
        name="history",
    )(inner, outer, gain, field, head, later)


def local_kernel(depth, shifts, outer_plane, masks, absorption, field, near, out_side, beyond, history, image):
    plane = field.shape[-1]
    first = outer_plane[0] == 0
    for p in range(depth):
        cells = field[p]
        total = history[p] + (absorption[p][None, :] - 3.0 * DIFFUSION * STENCIL[2]) * cells
        for row, shift in enumerate(shifts):
            total = total + masks[row][None, :] * pltpu.roll(cells, (-shift) % plane, 1)
        for offset in OFFSETS:
            if 0 <= p + offset < depth:
                total = total + (-DIFFUSION * STENCIL[offset + 2]) * field[p + offset]
        image[p] = total
    inner_plane = depth - 1 - outer_plane[0]
    image[outer_plane[0]] += NEAR * beyond[...] + FAR * out_side[...]
    middle = jnp.where(first, 1, depth - 2)
    image[middle] += FAR * beyond[...]
    image[inner_plane] += FAR * near[...]


def local_terms(outer_plane, masks, absorption, field, near, out_side, beyond, history, shifts):
    depth, steps, plane = field.shape
    slab = pl.BlockSpec((depth, ROWS, plane), lambda t, s: (0, t, 0))
    single = pl.BlockSpec((ROWS, plane), lambda t, s: (t, 0))
    return pl.pallas_call(
        functools.partial(local_kernel, depth, shifts),
        grid_spec=pltpu.PrefetchScalarGridSpec(
            num_scalar_prefetch=1,
            grid=(steps // ROWS,),
            in_specs=[
                pl.BlockSpec(masks.shape, lambda t, s: (0, 0)),
                pl.BlockSpec(absorption.shape, lambda t, s: (0, 0)),
                slab,
                single,
                single,
                single,
                slab,
            ],
            out_specs=slab,
        ),
        out_shape=jax.ShapeDtypeStruct(field.shape, jnp.float32),
        input_output_aliases={7: 0},
        compiler_params=pltpu.CompilerParams(vmem_limit_bytes=VMEM_LIMIT),
        cost_estimate=pl.CostEstimate(
            flops=40 * field.size, bytes_accessed=16 * field.size, transcendentals=0
        ),
        name="local_terms",
    )(outer_plane, masks, absorption, field, near, out_side, beyond, history)


def inner_kernel(planes, beside, image, out):
    weight = jnp.where(pl.program_id(1) == 0, NEAR, FAR)
    out[...] = image[...] + weight * beside[...]


def add_inner(planes, beside, image, start):
    depth, steps, plane = image.shape
    count = beside.shape[0]
    at = pl.BlockSpec((None, ROWS, plane), lambda t, g, s: (s[g], start // ROWS + t, 0))
    return pl.pallas_call(
        inner_kernel,
        grid_spec=pltpu.PrefetchScalarGridSpec(
            num_scalar_prefetch=1,
            grid=(count // ROWS, 2),
            in_specs=[pl.BlockSpec((ROWS, plane), lambda t, g, s: (t, 0)), at],
            out_specs=at,
        ),
        out_shape=jax.ShapeDtypeStruct(image.shape, jnp.float32),
        input_output_aliases={2: 0},
        compiler_params=pltpu.CompilerParams(vmem_limit_bytes=VMEM_LIMIT),
        cost_estimate=pl.CostEstimate(
            flops=4 * beside.size, bytes_accessed=20 * beside.size, transcendentals=0
        ),
        name="add_inner",
    )(planes, beside, image)


def cuts(steps, pieces):
    marks = [ROWS * round(steps * i / pieces / ROWS) for i in range(pieces + 1)]
    return list(zip(marks[:-1], marks[1:]))


def per_device(adjoint_field, absorption, mode_rates, mode_weights):
    steps, depth, plane = adjoint_field.shape
    groups = lax.axis_size("tm")
    slabs = lax.axis_size("space")
    pairs = slabs // 2
    me = lax.axis_index("space")
    odd = me % 2
    field = adjoint_field.transpose(1, 0, 2)

    swap = [(i, i ^ 1) for i in range(slabs)]
    outward = [(i, i - 2 if i % 2 == 0 else i + 2) for i in range(slabs)]
    outward = [(a, b) for a, b in outward if 0 <= b < slabs]
    onward = [(i, i + 2 if i % 2 == 0 else i - 2) for i in range(slabs)]
    onward = [(a, b) for a, b in onward if 0 <= b < slabs]

    def rank(i):
        return i // 2 if i % 2 == 0 else pairs - 1 - i // 2

    my_rank = jnp.where(odd == 0, me // 2, pairs - 1 - me // 2)
    partner_rank = jnp.where(odd == 1, me // 2, pairs - 1 - me // 2)

    outer_at = jnp.where(odd == 0, 0, depth - 1).astype(jnp.int32)
    inner_at = depth - 1 - outer_at

    def piece(at, lo, hi):
        return lax.dynamic_slice(field, (at, lo, 0), (1, hi - lo, plane))[0]

    halves = cuts(steps, 2)
    quarters = cuts(steps, pairs)
    relay_end = quarters[-1][0]

    mid = [lax.slice(field, (1, lo, 0), (2, hi, plane))[0] for lo, hi in halves]
    y_mid0 = lax.ppermute(mid[0], "space", swap)
    outer_part = piece(outer_at, 0, relay_end)
    outer_part = tied(outer_part, mid[0])
    relayed = lax.ppermute(outer_part, "space", outward)
    mid1 = tied(mid[1], outer_part)
    y_mid1 = lax.ppermute(mid1, "space", swap)
    head = lax.slice(field, (0, 0, 0), (depth, BAND, plane))
    head = tied(head, mid1)
    back = [(i, i - 1) for i in range(1, groups)]
    next_head = lax.ppermute(head, "tm", back)

    rates, weights = lax.optimization_barrier((mode_rates, mode_weights, head))[:2]
    scaled, mode_gain = mode_tables(rates, weights, steps * groups)
    inner, outer, projector, remote_gain = history_tables(scaled, mode_gain, steps)
    sums = mode_sums(projector, field)
    block_decay = jnp.exp(-scaled * steps)[None, :, None]
    later = lax.ppermute(sums, "tm", back)

    y_mid0 = tied(y_mid0, sums)
    z_mid0 = lax.ppermute(y_mid0, "space", onward)

    def outer_send(q, *after):
        lo, hi = quarters[q]
        own = piece(outer_at, lo, hi)
        if q < pairs - 1:
            own = jnp.where(q < pairs - 1 - my_rank, relayed[lo:hi], own)
        own = tied(own, *after)
        route = [(i, i ^ 1) for i in range(slabs) if q != pairs - 1 - rank(i)]
        return lax.ppermute(own, "space", route)

    def outer_onward(q, got):
        route = [
            (a, b) for a, b in onward if q > pairs - 1 - rank(a ^ 1)
        ]
        return lax.ppermute(got, "space", route) if route else jnp.zeros_like(got)

    y_out = [outer_send(0, y_mid0)]
    for _ in range(groups - 2):
        later = lax.ppermute(sums + block_decay * later, "tm", back)
    z_mid1 = lax.ppermute(y_mid1, "space", onward)
    y_out.append(outer_send(1, y_mid1))
    history = history_of(inner, outer, remote_gain, field, next_head, later)
    z_out = []
    for q in range(2, pairs):
        y_out.append(outer_send(q, y_out[q - 2]))
    for q in range(pairs):
        z_out.append(outer_onward(q, y_out[q]))
    inner_cuts = [(0, steps // 2), (steps // 2, steps - 2 * ROWS), (steps - 2 * ROWS, steps)]
    y_in = []
    waits = [y_out[pairs - 2], y_out[pairs - 1]]
    for (lo, hi) in inner_cuts:
        src = tied(piece(inner_at, lo, hi), waits[len(y_in)])
        y_in.append(lax.ppermute(src, "space", swap))
        waits.append(y_in[-1])

    near = jnp.concatenate([y_mid0, y_mid1], axis=0)
    out_side = jnp.concatenate([z_mid0, z_mid1], axis=0)
    beyond = jnp.concatenate(
        [jnp.where(q < pairs - 1 - partner_rank, y_out[q], z_out[q]) for q in range(pairs)], axis=0
    )
    column = jnp.arange(plane, dtype=jnp.int32)
    row_pos = column % NY
    masks = [
        jnp.where((row_pos + o >= 0) & (row_pos + o < NY), -DIFFUSION * STENCIL[o + 2], 0.0) for o in OFFSETS
    ] + [
        jnp.where((column + o * NY >= 0) & (column + o * NY < plane), -DIFFUSION * STENCIL[o + 2], 0.0)
        for o in OFFSETS
    ]
    masks = jnp.stack(masks).astype(jnp.float32)
    shifts = tuple(OFFSETS) + tuple(o * NY for o in OFFSETS)
    image = local_terms(
        outer_at[None], masks, absorption, field, near, out_side, beyond, history, shifts
    )
    planes = jnp.stack([inner_at, jnp.where(odd == 0, depth - 2, 1).astype(jnp.int32)])
    for (lo, hi), beside in zip(inner_cuts, y_in):
        image = add_inner(planes, beside, image, lo)
    return image.transpose(1, 0, 2)


def solution(mesh):
    return jax.shard_map(
        per_device,
        mesh=mesh,
        in_specs=(P("tm", "space", None), P("space", None), P(), P()),
        out_specs=P("tm", "space", None),
        check_vma=False,
    )
```

time: 527 us -> 347 us (0.66)
  waiting for transfers between devices: 262 us -> 123 us
  Pallas kernels: 0 us -> 110 us
  local copies, waits for them, and re-layouts: 115 us -> 37.3 us
  other arithmetic: 82.2 us -> 27.6 us
  matrix products: 50.1 us -> 0 us
  starting transfers between devices: 14.9 us -> 45.4 us
    ppermute x6 -> x19, waiting for transfers between devices: 262 us -> 123 us  [the longest x4 46.6 us: outer_send(): return lax.ppermute(own, 'space', route)]
    pallas_call x0 -> x6, Pallas kernels: none -> 110 us  [the longest x1 37.5 us: history_of(): pl.pallas_call(history_kernel, grid=(depth, plane // tile), in_specs=[pl....]
    sub x3 -> x2, other arithmetic: 68.1 us -> 1.27 us  [the longest x1 0.67 us: history_tables(): jnp.arange(span, dtype=jnp.int32)[None, :]]
    dot_general x3 -> x0, matrix products: 50.1 us -> none  [the longest x1 19.6 us: per_device(): jnp.dot(kernel, flat_field, precision=lax.Precision.HIGHEST, preferred_el...]
    unnamed x19 -> x36, local copies, waits for them, and re-layouts: 41 us -> 6.58 us
    ppermute x6 -> x19, starting transfers between devices: 14.9 us -> 45.4 us  [the longest x4 13.1 us: outer_send(): return lax.ppermute(own, 'space', route)]
    concatenate x1 -> x0, local copies, waits for them, and re-layouts: 28.9 us -> none  [per_device(): extended = jnp.concatenate([adjoint_field, next_head], axis=0)]
    squeeze x0 -> x6, local copies, waits for them, and re-layouts: none -> 19.5 us  [the longest x5 14.4 us: piece(): return lax.dynamic_slice(field, (at, lo, 0), (1, hi - lo, plane))[0]]
  transfers between devices with their start and end apart: 6 -> 19, of which waited for: 4 -> 7; matrix products, arithmetic and copies ran while one was open for 31% -> 17% of each run, Pallas kernels for 0% -> 31%
where the time goes in v1:
time: 347 us; the launch traced here: 343 us
  waiting for transfers between devices  123 us (35%)
  Pallas kernels  110 us (32%)
  starting transfers between devices  45.4 us (13%)
  local copies, waits for them, and re-layouts  37.3 us (11%)
  other arithmetic  27.6 us (8%)
    ppermute x4, waiting for transfers between devices, outer_send(): return lax.ppermute(own, 'space', route)  46.6 us
    ppermute x3, waiting for transfers between devices, outer_onward(): return lax.ppermute(got, 'space', route) if route else jnp.zeros_like(got)  42.3 us
    pallas_call x1, Pallas kernels, history_of(): pl.pallas_call(history_kernel, grid=(depth, plane // tile), in_specs=[pl....  37.5 us
    pallas_call x1, Pallas kernels, local_terms(): pl.pallas_call(functools.partial(local_kernel, depth, shifts), grid_spec=...  36.6 us
    ppermute x1, waiting for transfers between devices, per_device(): y_mid1 = lax.ppermute(mid1, 'space', swap)  33 us
    pallas_call x3, Pallas kernels, add_inner(): pl.pallas_call(inner_kernel, grid_spec=pltpu.PrefetchScalarGridSpec(num_s...  23.7 us
    squeeze x5, local copies, waits for them, and re-layouts, piece(): return lax.dynamic_slice(field, (at, lo, 0), (1, hi - lo, plane))[0]  14.4 us
    ppermute x4, starting transfers between devices, outer_send(): return lax.ppermute(own, 'space', route)  13.1 us
  transfers between devices with their start and end apart: 19, of which 7 were waited for; matrix products, arithmetic and copies ran while one was open for 17% of the time, Pallas kernels for 31%

profile of v1, /device:TPU:0, one launch (start us, length us, event | category | flops | bytes accessed | tf_op | source)
XLA Modules:
  0.0 343.3 jit_solution(1544899565144017848)
XLA Ops:
  0.0 5.1 %slice_bitcast_fusion = (f32[64,9216]{1,0:T(8,128)}, f32[64,9216]{1,0:T(8,128)}) fusion(f32[3,128,9216]{2,1,0:T(8,128)} %bitcast.25), kind=kLoop, calls=%fused_computation.4 | loop fusion | bytes 9437184 | tf_op jit(solution)/shard_map/squeeze | solution.py:239
  5.1 3.0 collective-permute-start.1
  8.0 4.0 %dynamic-slice_bitcast_fusion = f32[96,9216]{1,0:T(8,128)} fusion(f32[128,3,9216]{2,0,1:T(8,128)} %param.4, s32[]{:T(128)} %select_n.199), kind=kLoop, calls=%fused_computation.3 | loop fusion | bytes 7077892 | tf_op jit(solution)/shard_map/squeeze | solution.py:233
  13.4 4.4 %collective-permute-start.6 = (f32[64,9216]{1,0:T(8,128)}, f32[64,9216]{1,0:T(8,128)}, u32[]{:S(2)}, u32[]{:S(2)}) collective-permute-start(f32[64,9216]{1,0:T(8,128)} %get-tuple-element.19), channel_id=1, source_target_pairs={{0,1},{1,0},{2,3},{3,2},{4,5},{5,4},{6,7},{7,6},{8,9},{9,8},{10,11... | collective-permute-start | bytes 7077896 | tf_op jit(solution)/shard_map/ppermute | solution.py:245
  22.0 12.2 %mode_sums.1 = f32[3,16,9216]{2,1,0:T(8,128)S(1)} custom-call(f32[16,128]{1,0:T(8,128)S(1)} %multiply_exponential_fusion.projector, f32[3,128,9216]{2,1,0:T(8,128)} %bitcast.27), custom_call_target="tpu_custom_call" | custom-call | flops 679477248 | bytes 14155776 | tf_op jit(solution)/shard_map/mode_sums/pallas_call | solution.py:76
  42.3 2.8 dynamic-slice_bitcast_fusion.2
  66.1 3.2 dynamic-slice_bitcast_fusion.1
  77.2 33.0 %collective-permute-done.6 = f32[64,9216]{1,0:T(8,128)} collective-permute-done((f32[64,9216]{1,0:T(8,128)}, f32[64,9216]{1,0:T(8,128)}, u32[]{:S(2)}, u32[]{:S(2)}) %collective-permute-start.6) | collective-permute-done | bytes 2359328 | tf_op jit(solution)/shard_map/ppermute | solution.py:245
  110.1 3.8 %collective-permute-start.11 = (f32[64,9216]{1,0:T(8,128)}, f32[64,9216]{1,0:T(8,128)S(1)}, u32[]{:S(2)}, u32[]{:S(2)}) collective-permute-start(f32[64,9216]{1,0:T(8,128)} %collective-permute-done.6), channel_id=1, source_target_pairs={{0,2},{2,4},{3,1},{4,6},{5,3},{7,5},{8,10},{10,12},{11,9},{12,14},... | collective-permute-start | bytes 7077896 | tf_op jit(solution)/shard_map/ppermute | solution.py:279
  116.8 4.5 %slice_select_fusion = (f32[32,9216]{1,0:T(8,128)S(1)}, f32[32,9216]{1,0:T(8,128)S(1)}, f32[32,9216]{1,0:T(8,128)}) fusion(f32[96,9216]{1,0:T(8,128)} %collective-permute-done, f32[128,3,9216]{2,0,1:T(8,128)} %param.4, s32[]{:T(128)} %select_n.199, pred[]{:T(512)S(6)} %gt.23, pred[]{:T(512)S(6)} %gt.22, pred[]{:T(512)S(6)} %gt.21), kind=kLoop, calls=%fused_computation.10 | loop fusion | flops 884736 | bytes 10616839 | tf_op jit(solution)/shard_map/jit(_where)/select_n | solution.py:265
  123.2 4.1 %collective-permute-start.2 = (f32[32,9216]{1,0:T(8,128)S(1)}, f32[32,9216]{1,0:T(8,128)S(1)}, u32[]{:S(2)}, u32[]{:S(2)}) collective-permute-start(f32[32,9216]{1,0:T(8,128)S(1)} %get-tuple-element.23), channel_id=1, source_target_pairs={{0,1},{2,3},{3,2},{4,5},{5,4},{7,6},{8,9},{10,11},{11,10},{12,13},... | collective-permute-start | bytes 3538952 | tf_op jit(solution)/shard_map/ppermute | solution.py:268
  127.7 22.0 %collective-permute-done.7 = f32[32,9216]{1,0:T(8,128)S(1)} collective-permute-done((f32[32,9216]{1,0:T(8,128)S(1)}, f32[32,9216]{1,0:T(8,128)S(1)}, u32[]{:S(2)}, u32[]{:S(2)}) %collective-permute-start.7) | collective-permute-done | bytes 1179680 | tf_op jit(solution)/shard_map/ppermute | solution.py:268
  151.0 21.8 %collective-permute-done.2 = f32[32,9216]{1,0:T(8,128)S(1)} collective-permute-done((f32[32,9216]{1,0:T(8,128)S(1)}, f32[32,9216]{1,0:T(8,128)S(1)}, u32[]{:S(2)}, u32[]{:S(2)}) %collective-permute-start.2) | collective-permute-done | bytes 1179680 | tf_op jit(solution)/shard_map/ppermute | solution.py:268
  174.2 5.8 %collective-permute-start.3 = (f32[32,9216]{1,0:T(8,128)}, f32[32,9216]{1,0:T(8,128)}, u32[]{:S(2)}, u32[]{:S(2)}) collective-permute-start(f32[32,9216]{1,0:T(8,128)} %get-tuple-element.24), channel_id=1, source_target_pairs={{0,1},{1,0},{3,2},{4,5},{6,7},{7,6},{8,9},{9,8},{11,10},{12,13},{1... | collective-permute-start | bytes 3538952 | tf_op jit(solution)/shard_map/ppermute | solution.py:268
  180.0 3.3 collective-permute-start.12
  185.9 37.5 %history.1 = f32[3,128,9216]{2,1,0:T(8,128)} custom-call(f32[128,128]{1,0:T(8,128)S(1)} %copy-done.1, f32[128,16]{1,0:T(8,128)S(1)} %copy-done.2, f32[128,16]{1,0:T(8,128)S(1)} %exponential_multiply_fusion.gain, f32[3,128,9216]{2,1,0:T(8,128)} %bitcast.28, f32[3,16,9216]{2,1,0:T(8,128)S(1)} %collective-permute-done.15.head, ...), custom_call_target="tpu_custom_call" | custom-call | flops 6794772480 | bytes 28311552 | tf_op jit(solution)/shard_map/history/pallas_call | solution.py:104
  228.2 4.0 %collective-permute-start.14 = (f32[32,9216]{1,0:T(8,128)}, f32[32,9216]{1,0:T(8,128)S(1)}, u32[]{:S(2)}, u32[]{:S(2)}) collective-permute-start(f32[32,9216]{1,0:T(8,128)} %collective-permute-done.8), channel_id=1, source_target_pairs={{0,2},{2,4},{3,1},{4,6},{5,3},{7,5},{8,10},{10,12},{11,9},{12,14},... | collective-permute-start | bytes 3538952 | tf_op jit(solution)/shard_map/ppermute | solution.py:274
  232.1 3.3 collective-permute-start.13
  237.0 21.8 %collective-permute-done.14 = f32[32,9216]{1,0:T(8,128)S(1)} collective-permute-done((f32[32,9216]{1,0:T(8,128)}, f32[32,9216]{1,0:T(8,128)S(1)}, u32[]{:S(2)}, u32[]{:S(2)}) %collective-permute-start.14) | collective-permute-done | bytes 1179680 | tf_op jit(solution)/shard_map/ppermute | solution.py:274
  258.9 20.6 %collective-permute-done.13 = f32[32,9216]{1,0:T(8,128)S(1)} collective-permute-done((f32[32,9216]{1,0:T(8,128)}, f32[32,9216]{1,0:T(8,128)S(1)}, u32[]{:S(2)}, u32[]{:S(2)}) %collective-permute-start.13) | collective-permute-done | bytes 1179680 | tf_op jit(solution)/shard_map/ppermute | solution.py:274
  282.9 36.6 %local_terms.1.image = f32[3,128,9216]{2,1,0:T(8,128)} custom-call(s32[1]{0:T(128)} %bitcast.12.outer_plane, f32[8,9216]{1,0:T(8,128)S(1)} %copy-done, f32[3,9216]{1,0:T(4,128)S(1)} %copy-done.3, f32[3,128,9216]{2,1,0:T(8,128)} %bitcast.29, f32[128,9216]{1,0:T(8,128)S(1)} %pad_maximum_fusion.near, ...), custom_call_target="tpu_custom_call", output_to_operand_aliasing={{}: (7, {})} | custom-call | flops 141557760 | bytes 56623104 | tf_op jit(solution)/shard_map/local_terms/pallas_call | solution.py:150
  319.5 11.0 %add_inner.3.image = f32[3,128,9216]{2,1,0:T(8,128)} custom-call(s32[2]{0:T(128)S(1)} %pad_add_fusion.planes, f32[64,9216]{1,0:T(8,128)S(1)} %collective-permute-done.4.beside, f32[3,128,9216]{2,1,0:T(8,128)} %local_terms.1.image), custom_call_target="tpu_custom_call", output_to_operand_aliasing={{}: (2, {})} | custom-call | flops 2359296 | bytes 11796480 | tf_op jit(solution)/shard_map/add_inner/pallas_call | solution.py:185
  330.5 8.8 %add_inner.4.image = f32[3,128,9216]{2,1,0:T(8,128)} custom-call(s32[2]{0:T(128)S(1)} %pad_add_fusion.planes, f32[48,9216]{1,0:T(8,128)S(1)} %collective-permute-done.9.beside, f32[3,128,9216]{2,1,0:T(8,128)} %add_inner.3.image), custom_call_target="tpu_custom_call", output_to_operand_aliasing={{}: (2, {})} | custom-call | flops 1769472 | bytes 8847360 | tf_op jit(solution)/shard_map/add_inner/pallas_call | solution.py:185
  339.3 4.0 %add_inner.5 = f32[3,128,9216]{2,1,0:T(8,128)} custom-call(s32[2]{0:T(128)S(1)} %pad_add_fusion.planes, f32[16,9216]{1,0:T(8,128)S(1)} %collective-permute-done.5.beside, f32[3,128,9216]{2,1,0:T(8,128)} %add_inner.4.image), custom_call_target="tpu_custom_call", output_to_operand_aliasing={{}: (2, {})} | custom-call | flops 589824 | bytes 2949120 | tf_op jit(solution)/shard_map/add_inner/pallas_call | solution.py:185
  (97 shorter events, 62.4 us)
Async XLA Ops:
  5.1 70.1 %collective-permute-start.1 = (f32[64,9216]{1,0:T(8,128)}, f32[64,9216]{1,0:T(8,128)}, u32[]{:S(2)}, u32[]{:S(2)}) collective-permute-start(f32[64,9216]{1,0:T(8,128)} %get-tuple-element.35), channel_id=1, source_target_pairs={{0,1},{1,0},{2,3},{3,2},{4,5},{5,4},{6,7},{7,6},{8,9},{9,8},{10,11... | collective-permute-start | bytes 7077896 | tf_op jit(solution)/shard_map/ppermute | solution.py:240
  12.0 104.8 %collective-permute-start = (f32[96,9216]{1,0:T(8,128)}, f32[96,9216]{1,0:T(8,128)}, u32[]{:S(2)}, u32[]{:S(2)}) collective-permute-start(f32[96,9216]{1,0:T(8,128)} %dynamic-slice_bitcast_fusion), channel_id=1, source_target_pairs={{1,3},{2,0},{3,5},{4,2},{5,7},{6,4},{9,11},{10,8},{11,13},{12,10},... | collective-permute-start | bytes 10616840 | tf_op jit(solution)/shard_map/ppermute | solution.py:243
  13.4 96.8 %collective-permute-start.6 = (f32[64,9216]{1,0:T(8,128)}, f32[64,9216]{1,0:T(8,128)}, u32[]{:S(2)}, u32[]{:S(2)}) collective-permute-start(f32[64,9216]{1,0:T(8,128)} %get-tuple-element.19), channel_id=1, source_target_pairs={{0,1},{1,0},{2,3},{3,2},{4,5},{5,4},{6,7},{7,6},{8,9},{9,8},{10,11... | collective-permute-start | bytes 7077896 | tf_op jit(solution)/shard_map/ppermute | solution.py:245
  20.6 165.3 %collective-permute-start.15 = (f32[3,16,9216]{2,1,0:T(8,128)}, f32[3,16,9216]{2,1,0:T(8,128)S(1)}, u32[]{:S(2)}, u32[]{:S(2)}) collective-permute-start(f32[3,16,9216]{2,1,0:T(8,128)} %slice.39), channel_id=1, source_target_pairs={{8,0},{16,8},{24,16},{9,1},{17,9},{25,17},{10,2},{18,10},{26,18},{... | collective-permute-start | bytes 5308424 | tf_op jit(solution)/shard_map/ppermute | solution.py:249
  21.9 26.8 %copy-start.10 = (f32[16]{0:T(128)}, f32[16]{0:T(128)S(1)}, u32[]{:S(2)}) copy-start(f32[16]{0:T(128)S(1)} %get-tuple-element.38) | copy-start | bytes 196
  21.9 26.8 %copy-start.12 = (f32[16]{0:T(128)}, f32[16]{0:T(128)S(1)}, u32[]{:S(2)}) copy-start(f32[16]{0:T(128)S(1)} %get-tuple-element.37) | copy-start | bytes 196
  34.2 38.0 %collective-permute-start.16 = (f32[3,16,9216]{2,1,0:T(8,128)S(1)}, f32[3,16,9216]{2,1,0:T(8,128)}, u32[]{:S(2)}, u32[]{:S(2)}) collective-permute-start(f32[3,16,9216]{2,1,0:T(8,128)S(1)} %mode_sums.1), channel_id=1, source_target_pairs={{8,0},{16,8},{24,16},{9,1},{17,9},{25,17},{10,2},{18,10},{26,18},{... | collective-permute-start | bytes 5308424 | tf_op jit(solution)/shard_map/ppermute | solution.py:256
  73.9 49.3 %collective-permute-start.17 = (f32[3,16,9216]{2,1,0:T(8,128)S(1)}, f32[3,16,9216]{2,1,0:T(8,128)S(1)}, u32[]{:S(2)}, u32[]{:S(2)}) collective-permute-start(f32[3,16,9216]{2,1,0:T(8,128)S(1)} %multiply_add_fusion.1), channel_id=1, source_target_pairs={{8,0},{16,8},{24,16},{9,1},{17,9},{25,17},{10,2},{18,10},{26,18},{... | collective-permute-start | bytes 5308424 | tf_op jit(solution)/shard_map/ppermute | solution.py:278
  75.2 99.0 %collective-permute-start.10 = (f32[64,9216]{1,0:T(8,128)}, f32[64,9216]{1,0:T(8,128)S(1)}, u32[]{:S(2)}, u32[]{:S(2)}) collective-permute-start(f32[64,9216]{1,0:T(8,128)} %collective-permute-done.1), channel_id=1, source_target_pairs={{0,2},{2,4},{3,1},{4,6},{5,3},{7,5},{8,10},{10,12},{11,9},{12,14},... | collective-permute-start | bytes 7077896 | tf_op jit(solution)/shard_map/ppermute | solution.py:259
  110.1 69.9 %collective-permute-start.11 = (f32[64,9216]{1,0:T(8,128)}, f32[64,9216]{1,0:T(8,128)S(1)}, u32[]{:S(2)}, u32[]{:S(2)}) collective-permute-start(f32[64,9216]{1,0:T(8,128)} %collective-permute-done.6), channel_id=1, source_target_pairs={{0,2},{2,4},{3,1},{4,6},{5,3},{7,5},{8,10},{10,12},{11,9},{12,14},... | collective-permute-start | bytes 7077896 | tf_op jit(solution)/shard_map/ppermute | solution.py:279
  121.3 28.4 %collective-permute-start.7 = (f32[32,9216]{1,0:T(8,128)S(1)}, f32[32,9216]{1,0:T(8,128)S(1)}, u32[]{:S(2)}, u32[]{:S(2)}) collective-permute-start(f32[32,9216]{1,0:T(8,128)S(1)} %get-tuple-element.27), channel_id=1, source_target_pairs={{0,1},{1,0},{2,3},{5,4},{6,7},{7,6},{8,9},{9,8},{10,11},{13,12},{1... | collective-permute-start | bytes 3538952 | tf_op jit(solution)/shard_map/ppermute | solution.py:268
  123.2 49.6 %copy-start.6 = (f32[32,9216]{1,0:T(8,128)S(1)}, f32[32,9216]{1,0:T(8,128)}, u32[]{:S(2)}) copy-start(f32[32,9216]{1,0:T(8,128)} %dynamic-slice_bitcast_fusion.3) | copy-start | bytes 3538948
  123.2 49.6 %collective-permute-start.2 = (f32[32,9216]{1,0:T(8,128)S(1)}, f32[32,9216]{1,0:T(8,128)S(1)}, u32[]{:S(2)}, u32[]{:S(2)}) collective-permute-start(f32[32,9216]{1,0:T(8,128)S(1)} %get-tuple-element.23), channel_id=1, source_target_pairs={{0,1},{2,3},{3,2},{4,5},{5,4},{7,6},{8,9},{10,11},{11,10},{12,13},... | collective-permute-start | bytes 3538952 | tf_op jit(solution)/shard_map/ppermute | solution.py:268
  149.7 36.1 %collective-permute-start.18 = (f32[3,16,9216]{2,1,0:T(8,128)S(1)}, f32[3,16,9216]{2,1,0:T(8,128)S(1)}, u32[]{:S(2)}, u32[]{:S(2)}) collective-permute-start(f32[3,16,9216]{2,1,0:T(8,128)S(1)} %multiply_add_fusion), channel_id=1, source_target_pairs={{8,0},{16,8},{24,16},{9,1},{17,9},{25,17},{10,2},{18,10},{26,18},{... | collective-permute-start | bytes 5308424 | tf_op jit(solution)/shard_map/ppermute | solution.py:278
  172.8 53.3 %collective-permute-start.8 = (f32[32,9216]{1,0:T(8,128)S(1)}, f32[32,9216]{1,0:T(8,128)}, u32[]{:S(2)}, u32[]{:S(2)}) collective-permute-start(f32[32,9216]{1,0:T(8,128)S(1)} %copy-done.6), channel_id=1, source_target_pairs={{1,0},{2,3},{3,2},{4,5},{5,4},{6,7},{9,8},{10,11},{11,10},{12,13},... | collective-permute-start | bytes 3538952 | tf_op jit(solution)/shard_map/ppermute | solution.py:268
  174.2 51.9 %collective-permute-start.3 = (f32[32,9216]{1,0:T(8,128)}, f32[32,9216]{1,0:T(8,128)}, u32[]{:S(2)}, u32[]{:S(2)}) collective-permute-start(f32[32,9216]{1,0:T(8,128)} %get-tuple-element.24), channel_id=1, source_target_pairs={{0,1},{1,0},{3,2},{4,5},{6,7},{7,6},{8,9},{9,8},{11,10},{12,13},{1... | collective-permute-start | bytes 3538952 | tf_op jit(solution)/shard_map/ppermute | solution.py:268
  180.0 55.5 %collective-permute-start.12 = (f32[32,9216]{1,0:T(8,128)S(1)}, f32[32,9216]{1,0:T(8,128)}, u32[]{:S(2)}, u32[]{:S(2)}) collective-permute-start(f32[32,9216]{1,0:T(8,128)S(1)} %collective-permute-done.7), channel_id=1, source_target_pairs={{0,2},{7,5},{8,10},{15,13},{16,18},{23,21},{24,26},{31,29}} | collective-permute-start | bytes 3538952 | tf_op jit(solution)/shard_map/ppermute | solution.py:274
  185.8 40.3 %copy-start.4 = (f32[64,9216]{1,0:T(8,128)S(1)}, f32[64,9216]{1,0:T(8,128)}, u32[]{:S(2)}) copy-start(f32[64,9216]{1,0:T(8,128)} %dynamic-slice_bitcast_fusion.1) | copy-start | bytes 7077892
  185.8 40.3 %copy-start.5 = (f32[48,9216]{1,0:T(8,128)S(1)}, f32[48,9216]{1,0:T(8,128)}, u32[]{:S(2)}) copy-start(f32[48,9216]{1,0:T(8,128)} %dynamic-slice_bitcast_fusion.2) | copy-start | bytes 5308420
  226.1 54.2 %collective-permute-start.4 = (f32[64,9216]{1,0:T(8,128)S(1)}, f32[64,9216]{1,0:T(8,128)S(1)}, u32[]{:S(2)}, u32[]{:S(2)}) collective-permute-start(f32[64,9216]{1,0:T(8,128)S(1)} %copy-done.4), channel_id=1, source_target_pairs={{0,1},{1,0},{2,3},{3,2},{4,5},{5,4},{6,7},{7,6},{8,9},{9,8},{10,11... | collective-permute-start | bytes 7077896 | tf_op jit(solution)/shard_map/ppermute | solution.py:292
  226.2 104.3 %collective-permute-start.9 = (f32[48,9216]{1,0:T(8,128)S(1)}, f32[48,9216]{1,0:T(8,128)S(1)}, u32[]{:S(2)}, u32[]{:S(2)}) collective-permute-start(f32[48,9216]{1,0:T(8,128)S(1)} %copy-done.5), channel_id=1, source_target_pairs={{0,1},{1,0},{2,3},{3,2},{4,5},{5,4},{6,7},{7,6},{8,9},{9,8},{10,11... | collective-permute-start | bytes 5308424 | tf_op jit(solution)/shard_map/ppermute | solution.py:292
  228.2 30.6 %collective-permute-start.14 = (f32[32,9216]{1,0:T(8,128)}, f32[32,9216]{1,0:T(8,128)S(1)}, u32[]{:S(2)}, u32[]{:S(2)}) collective-permute-start(f32[32,9216]{1,0:T(8,128)} %collective-permute-done.8), channel_id=1, source_target_pairs={{0,2},{2,4},{3,1},{4,6},{5,3},{7,5},{8,10},{10,12},{11,9},{12,14},... | collective-permute-start | bytes 3538952 | tf_op jit(solution)/shard_map/ppermute | solution.py:274
  232.1 47.3 %collective-permute-start.13 = (f32[32,9216]{1,0:T(8,128)}, f32[32,9216]{1,0:T(8,128)S(1)}, u32[]{:S(2)}, u32[]{:S(2)}) collective-permute-start(f32[32,9216]{1,0:T(8,128)} %collective-permute-done.3), channel_id=1, source_target_pairs={{0,2},{2,4},{5,3},{7,5},{8,10},{10,12},{13,11},{15,13},{16,18},{18... | collective-permute-start | bytes 3538952 | tf_op jit(solution)/shard_map/ppermute | solution.py:274
  280.3 58.9 %collective-permute-start.5 = (f32[16,9216]{1,0:T(8,128)S(1)}, f32[16,9216]{1,0:T(8,128)S(1)}, u32[]{:S(2)}, u32[]{:S(2)}) collective-permute-start(f32[16,9216]{1,0:T(8,128)S(1)} %copy-done.7), channel_id=1, source_target_pairs={{0,1},{1,0},{2,3},{3,2},{4,5},{5,4},{6,7},{7,6},{8,9},{9,8},{10,11... | collective-permute-start | bytes 1769480 | tf_op jit(solution)/shard_map/ppermute | solution.py:292
  (11 other events, 80.2 us)

commit v2 on v1

v2 whole, which is shorter than its diff:
```python
import functools
import math

import jax
import jax.numpy as jnp
from jax import lax
from jax.experimental import pallas as pl
from jax.experimental.pallas import tpu as pltpu
from jax.sharding import PartitionSpec as P
import numpy as np

NY = 96
BAND = 16

DIFFUSION = 0.2
ORDER_EXP = 0.4
STENCIL = (-1.0 / 12.0, 16.0 / 12.0, -30.0 / 12.0, 16.0 / 12.0, -1.0 / 12.0)
NEAR = -DIFFUSION * STENCIL[1]
FAR = -DIFFUSION * STENCIL[0]
OFFSETS = (-2, -1, 1, 2)
ROWS = 8
VMEM_LIMIT = 48 * 1024 * 1024
SHORT = pl.CostEstimate(flops=1, bytes_accessed=1, transcendentals=0)

OUTER, INNER, MIDDLE, RANK, PARTNER_RANK = range(5)


def mode_tables(mode_rates, mode_weights, total_steps):
    scaled = mode_rates / total_steps
    mode_gain = mode_weights * jnp.sqrt(-jnp.expm1(-2.0 * scaled))
    return scaled, mode_gain


def caputo_weights():
    grown = np.arange(BAND + 1, dtype=np.float64) ** ORDER_EXP
    increments = grown[1:] - grown[:-1]
    return [float(w) for w in np.diff(increments, prepend=0.0)]


def dot(a, b):
    return jnp.dot(a, b, precision=lax.Precision.HIGHEST, preferred_element_type=jnp.float32)


def tile_of(plane):
    for count in range(4, plane + 1):
        if plane % count == 0 and (plane // count) % 128 == 0:
            return plane // count
    return plane


def sums_kernel(scaled, field, sums, projector):
    modes, steps = projector.shape

    @pl.when((pl.program_id(0) == 0) & (pl.program_id(1) == 0))
    def _():
        pos = lax.broadcasted_iota(jnp.int32, (1, steps), 1).astype(jnp.float32)
        for j in range(modes):
            projector[j : j + 1, :] = jnp.exp(-scaled[j] * pos)

    sums[...] = dot(projector[...], field[...])


def mode_sums(scaled, field):
    depth, steps, plane = field.shape
    modes = scaled.shape[0]
    tile = tile_of(plane)
    return pl.pallas_call(
        sums_kernel,
        grid=(depth, plane // tile),
        in_specs=[
            pl.BlockSpec(memory_space=pltpu.SMEM),
            pl.BlockSpec((None, steps, tile), lambda p, c: (p, 0, c)),
        ],
        out_specs=pl.BlockSpec((None, modes, tile), lambda p, c: (p, 0, c)),
        out_shape=jax.ShapeDtypeStruct((depth, modes, plane), jnp.float32),
        scratch_shapes=[pltpu.VMEM((modes, steps), jnp.float32)],
        compiler_params=pltpu.CompilerParams(vmem_limit_bytes=VMEM_LIMIT),
        cost_estimate=SHORT,
        name="mode_sums",
    )(scaled, field)


def carry_kernel(steps, scaled, sums, later, total):
    for j in range(total.shape[0]):
        decay = jnp.exp(jnp.full((1, total.shape[1]), -scaled[j] * steps, jnp.float32))
        total[j : j + 1, :] = sums[j : j + 1, :] + decay * later[j : j + 1, :]


def carried(scaled, steps, sums, later):
    depth, _, plane = sums.shape
    modes = scaled.shape[0]
    part = pl.BlockSpec((None, modes, plane), lambda p: (p, 0, 0))
    return pl.pallas_call(
        functools.partial(carry_kernel, steps),
        grid=(depth,),
        in_specs=[pl.BlockSpec(memory_space=pltpu.SMEM), part, part],
        out_specs=part,
        out_shape=jax.ShapeDtypeStruct((depth, modes, plane), jnp.float32),
        cost_estimate=SHORT,
        name="carried",
    )(scaled, sums, later)


def fill_tables(steps, aways, scaled, mode_gain, scaled_row, gain_row, table):
    near_weights = caputo_weights()
    modes = scaled.shape[0]

    def lags(columns, ahead):
        row = lax.broadcasted_iota(jnp.int32, (steps, columns), 0)
        return lax.broadcasted_iota(jnp.int32, (steps, columns), 1) - row + ahead

    def far_of(lag):
        distance = jnp.maximum(lag, 0).astype(jnp.float32)
        far = jnp.zeros(lag.shape, jnp.float32)
        for j in range(modes):
            far = far + mode_gain[j] * jnp.exp(-scaled[j] * distance)
        return far

    def near_of(lag):
        near = jnp.zeros(lag.shape, jnp.float32)
        for k, weight in enumerate(near_weights):
            near = jnp.where(lag == k, weight, near)
        return near

    lag = lags(steps, 0)
    table[:, :steps] = jnp.where(lag >= BAND, far_of(lag), near_of(lag))
    lag = lags(BAND, steps)
    table[:, steps : steps + BAND] = jnp.where(lag < BAND, near_of(lag) - far_of(lag), 0.0)
    row = lax.broadcasted_iota(jnp.int32, (steps, modes), 0)
    for k, away in enumerate(aways):
        at = steps + BAND + k * modes
        distance = (away * steps - row).astype(jnp.float32)
        table[:, at : at + modes] = gain_row[...] * jnp.exp(-scaled_row[...] * distance)


def history_kernel(aways, scaled, mode_gain, scaled_row, gain_row, field, *refs):
    parts, (before, image, table, stacked) = refs[: 1 + len(aways)], refs[1 + len(aways) :]
    steps = field.shape[0]

    @pl.when((pl.program_id(0) == 0) & (pl.program_id(1) == 0))
    def _():
        fill_tables(steps, aways, scaled, mode_gain, scaled_row, gain_row, table)

    stacked[:steps, :] = field[...]
    at = steps
    for part in parts:
        stacked[at : at + part.shape[0], :] = part[...]
        at += part.shape[0]
    image[...] = before[...] + dot(table[...], stacked[...])


def add_history(scaled, mode_gain, field, head, aways, later, image):
    depth, steps, plane = field.shape
    modes = scaled.shape[0]
    tile = tile_of(plane)
    operands = (field, head, *later)
    rows = sum(array.shape[1] for array in operands)
    smem = pl.BlockSpec(memory_space=pltpu.SMEM)
    whole = pl.BlockSpec((1, modes), lambda p, c: (0, 0))
    part = lambda p, c: (p, 0, c)
    return pl.pallas_call(
        functools.partial(history_kernel, aways),
        grid=(depth, plane // tile),
        in_specs=[
            smem,
            smem,
            whole,
            whole,
            *[pl.BlockSpec((None, array.shape[1], tile), part) for array in (*operands, image)],
        ],
        out_specs=pl.BlockSpec((None, steps, tile), part),
        out_shape=jax.ShapeDtypeStruct(field.shape, jnp.float32),
        input_output_aliases={4 + len(operands): 0},
        scratch_shapes=[pltpu.VMEM((steps, rows), jnp.float32), pltpu.VMEM((rows, tile), jnp.float32)],
        compiler_params=pltpu.CompilerParams(vmem_limit_bytes=VMEM_LIMIT),
        cost_estimate=SHORT,
        name="add_history",
    )(scaled, mode_gain, scaled[None], mode_gain[None], *operands, image)


def copy_rows(source, out, sems):
    pieces = [pl.ds(k * ROWS, ROWS) for k in range(out.shape[0] // ROWS)]
    copies = [
        pltpu.make_async_copy(source.at[rows], out.at[rows], sems.at[k]) for k, rows in enumerate(pieces)
    ]
    for copy in copies:
        copy.start()
    for copy in copies:
        copy.wait()


def staged(kernel, name, shape, device, *arrays):
    return pl.pallas_call(
        kernel,
        in_specs=[pl.BlockSpec(memory_space=pltpu.SMEM)]
        + [pl.BlockSpec(memory_space=pl.ANY)] * len(arrays),
        out_specs=pl.BlockSpec(memory_space=pltpu.VMEM),
        out_shape=pltpu.VMEM(shape, jnp.float32),
        scratch_shapes=[pltpu.SemaphoreType.DMA((math.prod(shape[:-1]) // ROWS,))],
        cost_estimate=SHORT,
        name=name,
    )(device, *arrays)


def rows_kernel(which, lo, device, field, out, sems):
    copy_rows(field.at[device[which], pl.ds(lo, out.shape[0])], out, sems)


def middle_kernel(lo, field, token, out, sems):
    copy_rows(field.at[1, pl.ds(lo, out.shape[0])], out, sems)


def middle_rows(field, token, lo, hi):
    shape = (hi - lo, field.shape[-1])
    return pl.pallas_call(
        functools.partial(middle_kernel, lo),
        in_specs=[pl.BlockSpec(memory_space=pl.ANY)] * 2,
        out_specs=pl.BlockSpec(memory_space=pltpu.VMEM),
        out_shape=pltpu.VMEM(shape, jnp.float32),
        scratch_shapes=[pltpu.SemaphoreType.DMA((shape[0] // ROWS,))],
        cost_estimate=SHORT,
        name="middle_rows",
    )(field, token)


def rows_of(device, which, field, lo, hi):
    kernel = functools.partial(rows_kernel, which, lo)
    return staged(kernel, "rows_of", (hi - lo, field.shape[-1]), device, field)


def pick_kernel(last, relayed_lo, own_lo, device, field, relayed, out, sems):
    count = out.shape[0]

    @pl.when(device[RANK] < last)
    def _():
        copy_rows(relayed.at[pl.ds(relayed_lo, count)], out, sems)

    @pl.when(device[RANK] >= last)
    def _():
        copy_rows(field.at[device[OUTER], pl.ds(own_lo, count)], out, sems)


def picked_rows(device, field, relayed, last, relayed_lo, own_lo, count):
    kernel = functools.partial(pick_kernel, last, relayed_lo, own_lo)
    return staged(kernel, "picked_rows", (count, field.shape[-1]), device, field, relayed)


def head_kernel(device, field, out, sems):
    per_plane = BAND // ROWS
    for p in range(out.shape[0]):
        copy_rows(field.at[p, pl.ds(0, BAND)], out.at[p], sems.at[pl.ds(p * per_plane, per_plane)])


def head_of(device, field):
    depth, _, plane = field.shape
    return staged(head_kernel, "head_of", (depth, BAND, plane), device, field)


def join_kernel(device, *refs):
    arrays, (out, sems) = refs[:-2], refs[-2:]
    at = 0
    for array in arrays:
        rows = array.shape[0]
        copy_rows(array, out.at[pl.ds(at, rows)], sems.at[pl.ds(at // ROWS, rows // ROWS)])
        at += rows


def joined(device, arrays):
    shape = (sum(array.shape[0] for array in arrays), arrays[0].shape[1])
    return staged(join_kernel, "joined", shape, device, *arrays)


def block_rows(*edges):
    return 2 * ROWS if all(edge % (2 * ROWS) == 0 for edge in edges) else ROWS


def plane_kernel(depth, shifts, absorption, field, *refs):
    image, masks = refs[-2:]
    plane = field.shape[-1]

    @pl.when(pl.program_id(0) == 0)
    def _():
        column = lax.broadcasted_iota(jnp.int32, (1, plane), 1)
        row_pos = column % NY
        for at, offset in enumerate(OFFSETS):
            weight = -DIFFUSION * STENCIL[offset + 2]
            moved = row_pos + offset
            masks[at : at + 1, :] = jnp.where((moved >= 0) & (moved < NY), weight, 0.0)
            at += len(OFFSETS)
            moved = column + offset * NY
            masks[at : at + 1, :] = jnp.where((moved >= 0) & (moved < plane), weight, 0.0)

    for p in range(depth):
        cells = field[p]
        total = (absorption[p][None, :] - 3.0 * DIFFUSION * STENCIL[2]) * cells
        for row, shift in enumerate(shifts):
            total = total + masks[row][None, :] * pltpu.roll(cells, (-shift) % plane, 1)
        for offset in OFFSETS:
            if 0 <= p + offset < depth:
                total = total + (-DIFFUSION * STENCIL[offset + 2]) * field[p + offset]
        image[p] = total


def plane_terms(token, absorption, field, image, start, end):
    depth, _, plane = field.shape
    shifts = tuple(OFFSETS) + tuple(offset * NY for offset in OFFSETS)
    first = start // ROWS
    slab = pl.BlockSpec((depth, ROWS, plane), lambda t: (0, first + t, 0))
    in_any = pl.BlockSpec(memory_space=pl.ANY)
    started = [] if image is None else [image]
    return pl.pallas_call(
        functools.partial(plane_kernel, depth, shifts),
        grid=((end - start) // ROWS,),
        in_specs=[pl.BlockSpec(absorption.shape, lambda t: (0, 0)), slab, in_any] + [in_any] * len(started),
        out_specs=slab,
        scratch_shapes=[pltpu.VMEM((len(shifts), plane), jnp.float32)],
        out_shape=jax.ShapeDtypeStruct(field.shape, jnp.float32),
        input_output_aliases={3: 0} if started else {},
        compiler_params=pltpu.CompilerParams(vmem_limit_bytes=VMEM_LIMIT),
        cost_estimate=SHORT,
        name="plane_terms",
    )(absorption, field, token, *started)


def halo_kernel(last, device, near, out_side, over_y, over_z, before, image):
    beyond = jnp.where(device[PARTNER_RANK] < last, over_y[...], over_z[...])
    outer, middle, inner = device[OUTER], device[MIDDLE], device[INNER]
    image[outer] = before[outer] + NEAR * beyond + FAR * out_side[...]
    image[middle] = before[middle] + FAR * beyond
    image[inner] = before[inner] + FAR * near[...]


def add_halo(device, near, out_side, over_y, over_z, image, last, start, end):
    depth, _, plane = image.shape
    beside = (near, out_side, over_y, over_z)
    rows = block_rows(start, end, *[row for _, row in beside])
    slab = pl.BlockSpec((depth, rows, plane), lambda t, s: (0, start // rows + t, 0))

    def single(row):
        return pl.BlockSpec((rows, plane), lambda t, s: (row // rows + t, 0))

    return pl.pallas_call(
        functools.partial(halo_kernel, last),
        grid_spec=pltpu.PrefetchScalarGridSpec(
            num_scalar_prefetch=1,
            grid=((end - start) // rows,),
            in_specs=[*[single(row) for _, row in beside], slab],
            out_specs=slab,
        ),
        out_shape=jax.ShapeDtypeStruct(image.shape, jnp.float32),
        input_output_aliases={5: 0},
        compiler_params=pltpu.CompilerParams(vmem_limit_bytes=VMEM_LIMIT),
        cost_estimate=SHORT,
        name="add_halo",
    )(device, *[array for array, _ in beside], image)


def inner_kernel(device, beside, image, token, out):
    weight = jnp.where(pl.program_id(1) == 0, NEAR, FAR)
    out[...] = image[...] + weight * beside[...]


def add_inner(device, beside, image, token, start):
    plane = image.shape[-1]
    count = beside.shape[0]
    rows = block_rows(start, count)

    def place(t, g, s):
        return jnp.where(g == 0, s[INNER], s[MIDDLE]), start // rows + t, 0

    at = pl.BlockSpec((None, rows, plane), place)
    return pl.pallas_call(
        inner_kernel,
        grid_spec=pltpu.PrefetchScalarGridSpec(
            num_scalar_prefetch=1,
            grid=(count // rows, 2),
            in_specs=[
                pl.BlockSpec((rows, plane), lambda t, g, s: (t, 0)),
                at,
                pl.BlockSpec(memory_space=pl.ANY),
            ],
            out_specs=at,
        ),
        out_shape=jax.ShapeDtypeStruct(image.shape, jnp.float32),
        input_output_aliases={2: 0},
        compiler_params=pltpu.CompilerParams(vmem_limit_bytes=VMEM_LIMIT),
        cost_estimate=SHORT,
        name="add_inner",
    )(device, beside, image, token)


def cuts(steps, pieces):
    marks = [ROWS * round(steps * i / pieces / ROWS) for i in range(pieces + 1)]
    return list(zip(marks[:-1], marks[1:]))


class Order:
    def __init__(self, token):
        self.token = token

    def __call__(self, value):
        value, self.token = lax.optimization_barrier((value, self.token))
        return value


def per_device(adjoint_field, absorption, mode_rates, mode_weights):
    steps, depth, plane = adjoint_field.shape
    groups = lax.axis_size("tm")
    slabs = lax.axis_size("space")
    pairs = slabs // 2
    me = lax.axis_index("space")
    odd = me % 2
    field = adjoint_field.transpose(1, 0, 2)
    order = Order(mode_rates)

    swap = [(i, i ^ 1) for i in range(slabs)]
    outward = [(i, i - 2 if i % 2 == 0 else i + 2) for i in range(slabs)]
    outward = [(a, b) for a, b in outward if 0 <= b < slabs]
    onward = [(i, i + 2 if i % 2 == 0 else i - 2) for i in range(slabs)]
    onward = [(a, b) for a, b in onward if 0 <= b < slabs]

    def back(distance):
        return [(i, i - distance) for i in range(distance, groups)]


    def rank(i):
        return i // 2 if i % 2 == 0 else pairs - 1 - i // 2

    device = jnp.stack(
        [
            jnp.where(odd == 0, 0, depth - 1),
            jnp.where(odd == 0, depth - 1, 0),
            jnp.where(odd == 0, depth - 2, 1),
            jnp.where(odd == 0, me // 2, pairs - 1 - me // 2),
            jnp.where(odd == 1, me // 2, pairs - 1 - me // 2),
        ]
    ).astype(jnp.int32)

    def send(value, axis, route):
        return lax.ppermute(order(value), axis, route)

    def whole_rows(share):
        return ROWS * round(steps * share / ROWS)

    def between(*marks):
        return list(zip(marks[:-1], marks[1:]))

    mid_cuts = between(0, whole_rows(1 / 2), steps)
    out_cuts = cuts(steps, pairs)
    in_cuts = between(0, whole_rows(5 / 8), whole_rows(7 / 8), steps - ROWS, steps)
    plane_cuts = cuts(steps, 4)
    slots = pairs - 1

    def middle_send(k):
        return send(middle_rows(field, order.token, *mid_cuts[k]), "space", swap)

    def outer_send(j):
        last = slots - j
        lo, hi = out_cuts[j]
        own_lo, own_hi = out_cuts[j + 1]
        first = out_cuts[(slots + 1) // 2][0]
        got, at = (relayed[0], lo) if lo < first else (relayed[1], lo - first)
        return send(
            picked_rows(order(device), field, got, last, at, own_lo, own_hi - own_lo), "space", swap
        )

    def outer_onward(parts):
        route = [(a, b) for a, b in onward if parts[-1] >= slots - rank(a ^ 1)]
        return send(y_out[parts[0]] if len(parts) == 1 else together, "space", route)

    def inner_send(k):
        return send(rows_of(order(device), INNER, field, *in_cuts[k]), "space", swap)

    def relay(lo, hi):
        return send(rows_of(order(device), OUTER, field, lo, hi), "space", outward)

    y_steps = [functools.partial(middle_send, k) for k in range(len(mid_cuts))]
    y_steps += [functools.partial(outer_send, j) for j in range(slots)]
    y_steps += [functools.partial(inner_send, k) for k in range(len(in_cuts))]
    sent = []

    def next_y():
        if len(sent) < len(y_steps):
            sent.append(y_steps[len(sent)]())

    scaled, mode_gain = mode_tables(mode_rates, mode_weights, steps * groups)
    next_y()
    next_y()
    first = out_cuts[(slots + 1) // 2][0]
    relayed = [relay(0, first)]
    head = send(head_of(order(device), field), "tm", back(1))
    sums = mode_sums(order(scaled), field)
    aways = [1]
    later = [send(sums, "tm", back(1))]

    def plane(k, image):
        return order(plane_terms(order.token, absorption, field, image, *plane_cuts[k]))

    image = plane(0, None)
    y_mid = [order(sent[0])]
    z_mid = [send(y_mid[0], "space", onward)]
    relayed[0] = order(relayed[0])
    next_y()
    head = order(head)
    later[0] = order(later[0])
    if first < out_cuts[slots][0]:
        relayed.append(relay(first, out_cuts[slots][0]))
    while 2 * aways[-1] < groups:
        if len(aways) > 1:
            later[-1] = order(later[-1])
        sums = carried(order(scaled), aways[-1] * steps, sums, later[-1])
        aways.append(2 * aways[-1])
        later.append(send(sums, "tm", back(aways[-1])))

    image = plane(1, image)
    y_mid.append(order(sent[1]))
    next_y()
    image = plane(2, image)

    def halo(q, image):
        lo, hi = out_cuts[q]
        over_z = y_out[0] if q == 0 else z_last if q == slots else z_most
        at_z = out_cuts[q - 1][0] if 0 < q < slots else 0
        over_y = (y_out[q], 0) if q < slots else (over_z, 0)
        if q == 0:
            over_z = jnp.zeros_like(over_z)
        for k, (start, end) in enumerate(mid_cuts):
            a, b = max(lo, start), min(hi, end)
            if a < b:
                image = add_halo(
                    order(device), (y_mid[k], a - start), (z_mid[k], a - start), (over_y[0], a - lo),
                    (over_z, at_z + a - lo), image, slots - q, a, b,
                )
        return order(image)

    y_out = []
    def inner(k, image):
        return order(add_inner(device, y_in[k], image, order.token, in_cuts[k][0]))

    for j in range(slots):
        y_out.append(order(sent[2 + j]))
        if j == 0:
            relayed[1:] = order(relayed[1:])
        if j < slots - 1:
            next_y()
        if j == 0:
            z_mid.append(send(y_mid[1], "space", onward))
            image = plane(3, image)
        if j == min(1, slots - 1):
            later[1:] = order(later[1:])
        if j == slots - 2:
            together = joined(order(device), y_out)
    z_mid[0] = order(z_mid[0])
    most = list(range(slots - 1))
    z_most = outer_onward(most) if most else None
    next_y()
    z_mid[1] = order(z_mid[1])
    z_last = outer_onward([slots - 1])
    image = halo(0, image)
    image = order(add_history(order(scaled), mode_gain, field, head, aways, later, image))
    y_in = []
    if most:
        z_most = order(z_most)
    for q in range(1, slots):
        image = halo(q, image)
    y_in.append(order(sent[2 + slots]))
    next_y()
    image = inner(0, image)
    z_last = order(z_last)
    image = halo(slots, image)
    for k in range(1, len(in_cuts)):
        y_in.append(order(sent[2 + slots + k]))
        next_y()
        image = inner(k, image)
    return image.transpose(1, 0, 2)


def solution(mesh):
    return jax.shard_map(
        per_device,
        mesh=mesh,
        in_specs=(P("tm", "space", None), P("space", None), P(), P()),
        out_specs=P("tm", "space", None),
        check_vma=False,
    )
```

time: 347 us -> 291 us (0.84)
  Pallas kernels: 110 us -> 162 us
  waiting for transfers between devices: 123 us -> 80.3 us
  local copies, waits for them, and re-layouts: 37.3 us -> 3.28 us
  other arithmetic: 27.6 us -> 0.01 us
    pallas_call x2 -> x23, Pallas kernels: 74.1 us -> 131 us  [the longest x4 41.5 us: plane_terms(): pl.pallas_call(functools.partial(plane_kernel, depth, shifts), grid=((end...]
    ppermute x19 -> x18, waiting for transfers between devices: 123 us -> 80.3 us  [send(): return lax.ppermute(order(value), axis, route)]
    squeeze x6 -> x0, local copies, waits for them, and re-layouts: 19.5 us -> none  [the longest x5 14.4 us: piece(): return lax.dynamic_slice(field, (at, lo, 0), (1, hi - lo, plane))[0]]
    select_n x10 -> x0, other arithmetic: 10.8 us -> none  [the longest x1 4.46 us: outer_send(): own = jnp.where(q < pairs - 1 - my_rank, relayed[lo:hi], own)]
    concatenate x3 -> x0, other arithmetic: 7.89 us -> none  [the longest x1 2.82 us: per_device(): near = jnp.concatenate([y_mid0, y_mid1], axis=0)]
    slice x5 -> x0, local copies, waits for them, and re-layouts: 6.03 us -> none  [the longest x4 3.23 us: history_tables(): return (own[:, :steps], ahead[:, steps:], projector, remote_gain)]
    pallas_call x3 -> x4, Pallas kernels: 23.7 us -> 19.5 us  [add_inner(): pl.pallas_call(inner_kernel, grid_spec=pltpu.PrefetchScalarGridSpec(num_s...]
    unnamed x36 -> x26, local copies, waits for them, and re-layouts: 6.58 us -> 2.52 us
  transfers between devices with their start and end apart: 19 -> 18, of which waited for: 7 -> 10; matrix products, arithmetic and copies ran while one was open for 17% -> 0% of each run, Pallas kernels for 31% -> 54%
where the time goes in v2:
time: 291 us; the launch traced here: 290 us
  Pallas kernels  162 us (56%)
  waiting for transfers between devices  80.3 us (28%)
  starting transfers between devices  43.2 us (15%)
  local copies, waits for them, and re-layouts  3.28 us (1%)
    ppermute x18, waiting for transfers between devices, send(): return lax.ppermute(order(value), axis, route)  80.3 us
    ppermute x18, starting transfers between devices, send(): return lax.ppermute(order(value), axis, route)  43.2 us
    pallas_call x4, Pallas kernels, plane_terms(): pl.pallas_call(functools.partial(plane_kernel, depth, shifts), grid=((end...  41.5 us
    pallas_call x11, Pallas kernels, staged(): pl.pallas_call(kernel, in_specs=[pl.BlockSpec(memory_space=pltpu.SMEM)] +...  33.2 us
    pallas_call x1, Pallas kernels, add_history(): pl.pallas_call(functools.partial(history_kernel, aways), grid=(depth, pla...  24.4 us
    pallas_call x4, Pallas kernels, add_halo(): pl.pallas_call(functools.partial(halo_kernel, last), grid_spec=pltpu.Pref...  21 us
    pallas_call x4, Pallas kernels, add_inner(): pl.pallas_call(inner_kernel, grid_spec=pltpu.PrefetchScalarGridSpec(num_s...  19.5 us
    pallas_call x1, Pallas kernels, mode_sums(): pl.pallas_call(sums_kernel, grid=(depth, plane // tile), in_specs=[pl.Blo...  12.3 us
  transfers between devices with their start and end apart: 18, of which 10 were waited for; matrix products, arithmetic and copies ran while one was open for 0% of the time, Pallas kernels for 54%

profile of v2, /device:TPU:0, one launch (start us, length us, event | category | flops | bytes accessed | tf_op | source)
XLA Modules:
  0.0 289.5 jit_solution(6858295451242262027)
XLA Ops:
  15.0 5.1 %head_of.1 = f32[3,16,9216]{2,1,0:T(8,128)} custom-call(s32[5]{0:T(128)} %stack.20.device, f32[3,128,9216]{2,1,0:T(8,128)} %bitcast.13), custom_call_target="tpu_custom_call" | custom-call | flops 1 | bytes 1 | tf_op jit(solution)/shard_map/head_of/pallas_call | solution.py:193
  21.4 12.3 %mode_sums.1.sums = f32[3,16,9216]{2,1,0:T(8,128)S(1)} custom-call(f32[16]{0:T(128)S(1)} %get-tuple-element.222.scaled, f32[3,128,9216]{2,1,0:T(8,128)} %bitcast.14), custom_call_target="tpu_custom_call" | custom-call | flops 1 | bytes 1 | tf_op jit(solution)/shard_map/mode_sums/pallas_call | solution.py:67
  39.3 10.4 %plane_terms.4.refs_1_ = f32[3,128,9216]{2,1,0:T(8,128)} custom-call(f32[3,9216]{1,0:T(4,128)S(1)} %copy-done.3, f32[3,128,9216]{2,1,0:T(8,128)} %bitcast.15, f32[16]{0:T(128)S(1)} %copy-done.9), custom_call_target="tpu_custom_call" | custom-call | flops 1 | bytes 1 | tf_op jit(solution)/shard_map/plane_terms/pallas_call | solution.py:311
  49.7 8.9 %collective-permute-done.3.near = f32[64,9216]{1,0:T(8,128)} collective-permute-done((f32[64,9216]{1,0:T(8,128)}, f32[64,9216]{1,0:T(8,128)}, u32[]{:S(2)}, u32[]{:S(2)}) %collective-permute-start.3) | collective-permute-done | bytes 2359328 | tf_op jit(solution)/shard_map/ppermute | solution.py:440
  58.6 10.0 %collective-permute-done.2.relayed = f32[64,9216]{1,0:T(8,128)} collective-permute-done((f32[64,9216]{1,0:T(8,128)}, f32[64,9216]{1,0:T(8,128)}, u32[]{:S(2)}, u32[]{:S(2)}) %collective-permute-start.2) | collective-permute-done | bytes 2359328 | tf_op jit(solution)/shard_map/ppermute | solution.py:440
  76.0 6.1 %collective-permute-start.9 = (f32[64,9216]{1,0:T(8,128)}, f32[64,9216]{1,0:T(8,128)}, u32[]{:S(2)}, u32[]{:S(2)}) collective-permute-start(f32[64,9216]{1,0:T(8,128)} %collective-permute-done.3.near), channel_id=1, source_target_pairs={{0,2},{2,4},{3,1},{4,6},{5,3},{7,5},{8,10},{10,12},{11,9},{12,14},... | collective-permute-start | bytes 7077896 | tf_op jit(solution)/shard_map/ppermute | solution.py:440
  87.6 10.4 %plane_terms.5.refs_1_ = f32[3,128,9216]{2,1,0:T(8,128)} custom-call(f32[3,9216]{1,0:T(4,128)S(1)} %copy-done.3, f32[3,128,9216]{2,1,0:T(8,128)} %bitcast.18, f32[16]{0:T(128)S(1)} %copy-done.9, f32[3,128,9216]{2,1,0:T(8,128)} %plane_terms.4.refs_1_), custom_call_target="tpu_custom_call", output_to_operand_aliasing={{}: (3, {})} | custom-call | flops 1 | bytes 1 | tf_op jit(solution)/shard_map/plane_terms/pallas_call | solution.py:311
  98.0 11.1 %collective-permute-done.5.near = f32[64,9216]{1,0:T(8,128)} collective-permute-done((f32[64,9216]{1,0:T(8,128)}, f32[64,9216]{1,0:T(8,128)}, u32[]{:S(2)}, u32[]{:S(2)}) %collective-permute-start.5) | collective-permute-done | bytes 2359328 | tf_op jit(solution)/shard_map/ppermute | solution.py:440
  114.3 10.4 %plane_terms.6.refs_1_ = f32[3,128,9216]{2,1,0:T(8,128)} custom-call(f32[3,9216]{1,0:T(4,128)S(1)} %copy-done.3, f32[3,128,9216]{2,1,0:T(8,128)} %bitcast.20, f32[16]{0:T(128)S(1)} %copy-done.9, f32[3,128,9216]{2,1,0:T(8,128)} %plane_terms.5.refs_1_), custom_call_target="tpu_custom_call", output_to_operand_aliasing={{}: (3, {})} | custom-call | flops 1 | bytes 1 | tf_op jit(solution)/shard_map/plane_terms/pallas_call | solution.py:311
  124.7 9.7 %collective-permute-done.8.refs_0_.over_y = f32[32,9216]{1,0:T(8,128)S(1)} collective-permute-done((f32[32,9216]{1,0:T(8,128)}, f32[32,9216]{1,0:T(8,128)S(1)}, u32[]{:S(2)}, u32[]{:S(2)}) %collective-permute-start.8) | collective-permute-done | bytes 1179680 | tf_op jit(solution)/shard_map/ppermute | solution.py:440
  139.4 4.9 %collective-permute-start.12 = (f32[64,9216]{1,0:T(8,128)}, f32[64,9216]{1,0:T(8,128)}, u32[]{:S(2)}, u32[]{:S(2)}) collective-permute-start(f32[64,9216]{1,0:T(8,128)} %collective-permute-done.5.near), channel_id=1, source_target_pairs={{0,2},{2,4},{3,1},{4,6},{5,3},{7,5},{8,10},{10,12},{11,9},{12,14},... | collective-permute-start | bytes 7077896 | tf_op jit(solution)/shard_map/ppermute | solution.py:440
  144.3 10.4 %plane_terms.7.before = f32[3,128,9216]{2,1,0:T(8,128)} custom-call(f32[3,9216]{1,0:T(4,128)S(1)} %copy-done.3, f32[3,128,9216]{2,1,0:T(8,128)} %bitcast.22, f32[16]{0:T(128)S(1)} %copy-done.9, f32[3,128,9216]{2,1,0:T(8,128)} %plane_terms.6.refs_1_), custom_call_target="tpu_custom_call", output_to_operand_aliasing={{}: (3, {})} | custom-call | flops 1 | bytes 1 | tf_op jit(solution)/shard_map/plane_terms/pallas_call | solution.py:311
  154.7 5.0 %collective-permute-done.6.refs_1_.over_y = f32[32,9216]{1,0:T(8,128)} collective-permute-done((f32[32,9216]{1,0:T(8,128)}, f32[32,9216]{1,0:T(8,128)}, u32[]{:S(2)}, u32[]{:S(2)}) %collective-permute-start.6) | collective-permute-done | bytes 1179680 | tf_op jit(solution)/shard_map/ppermute | solution.py:440
  170.5 14.5 %collective-permute-done.10.over_y = f32[32,9216]{1,0:T(8,128)} collective-permute-done((f32[32,9216]{1,0:T(8,128)}, f32[32,9216]{1,0:T(8,128)}, u32[]{:S(2)}, u32[]{:S(2)}) %collective-permute-start.10) | collective-permute-done | bytes 1179680 | tf_op jit(solution)/shard_map/ppermute | solution.py:440
  185.0 5.4 %collective-permute-start.15 = (f32[64,9216]{1,0:T(8,128)}, f32[64,9216]{1,0:T(8,128)}, u32[]{:S(2)}, u32[]{:S(2)}) collective-permute-start(f32[64,9216]{1,0:T(8,128)} %copy-done.4), channel_id=1, source_target_pairs={{0,2},{2,4},{5,3},{7,5},{8,10},{10,12},{13,11},{15,13},{16,18},{18... | collective-permute-start | bytes 7077896 | tf_op jit(solution)/shard_map/ppermute | solution.py:440
  194.9 4.4 %collective-permute-start.13 = (f32[32,9216]{1,0:T(8,128)}, f32[32,9216]{1,0:T(8,128)S(1)}, u32[]{:S(2)}, u32[]{:S(2)}) collective-permute-start(f32[32,9216]{1,0:T(8,128)} %collective-permute-done.10.over_y), channel_id=1, source_target_pairs={{0,2},{2,4},{3,1},{4,6},{5,3},{7,5},{8,10},{10,12},{11,9},{12,14},... | collective-permute-start | bytes 3538952 | tf_op jit(solution)/shard_map/ppermute | solution.py:440
  199.6 4.9 %add_halo.4.refs_3_ = f32[3,128,9216]{2,1,0:T(8,128)} custom-call(s32[5]{0:T(128)S(1)} %copy-done.6, f32[64,9216]{1,0:T(8,128)} %collective-permute-done.3.near, f32[64,9216]{1,0:T(8,128)} %collective-permute-done.9.out_side, f32[32,9216]{1,0:T(8,128)S(1)} %copy-done.2, f32[32,9216]{1,0:T(8,128)S(1)} %broadcast_in_dim.9.over_z, ...), custom_call_target="tpu_custom_call", output_to_operand_aliasing={{}: (5, {})} | custom-call | flops 1 | bytes 1 | tf_op jit(solution)/shard_map/add_halo/pallas_call | solution.py:342
  204.4 24.4 %add_history.1.before = f32[3,128,9216]{2,1,0:T(8,128)} custom-call(f32[16]{0:T(128)S(1)} %copy-done.11, f32[16]{0:T(128)S(1)} %get-tuple-element.269.mode_gain, f32[1,16]{1,0:T(1,128)S(1)} %bitcast.8, f32[1,16]{1,0:T(1,128)S(1)} %bitcast.9, f32[3,128,9216]{2,1,0:T(8,128)} %bitcast.25, ...), custom_call_target="tpu_custom_call", output_to_operand_aliasing={{}: (8, {})} | custom-call | flops 1 | bytes 1 | tf_op jit(solution)/shard_map/add_history/pallas_call | solution.py:161
  228.8 16.7 %collective-permute-done.15.over_z = f32[64,9216]{1,0:T(8,128)} collective-permute-done((f32[64,9216]{1,0:T(8,128)}, f32[64,9216]{1,0:T(8,128)}, u32[]{:S(2)}, u32[]{:S(2)}) %collective-permute-start.15) | collective-permute-done | bytes 2359328 | tf_op jit(solution)/shard_map/ppermute | solution.py:440
  245.5 5.6 %add_halo.5.before = f32[3,128,9216]{2,1,0:T(8,128)} custom-call(s32[5]{0:T(128)S(1)} %copy-done.6, f32[64,9216]{1,0:T(8,128)} %collective-permute-done.3.near, f32[64,9216]{1,0:T(8,128)} %collective-permute-done.9.out_side, f32[32,9216]{1,0:T(8,128)} %collective-permute-done.6.refs_1_.over_y, ...), custom_call_target="tpu_custom_call", output_to_operand_aliasing={{}: (5, {})} | custom-call | flops 1 | bytes 1 | tf_op jit(solution)/shard_map/add_halo/pallas_call | solution.py:342
  251.1 5.6 %add_halo.6.image = f32[3,128,9216]{2,1,0:T(8,128)} custom-call(s32[5]{0:T(128)S(1)} %copy-done.6, f32[64,9216]{1,0:T(8,128)} %collective-permute-done.5.near, f32[64,9216]{1,0:T(8,128)} %collective-permute-done.12.out_side, f32[32,9216]{1,0:T(8,128)} %collective-permute-done.10.over_y, ...), custom_call_target="tpu_custom_call", output_to_operand_aliasing={{}: (5, {})} | custom-call | flops 1 | bytes 1 | tf_op jit(solution)/shard_map/add_halo/pallas_call | solution.py:342
  258.4 10.0 %add_inner.4.before = f32[3,128,9216]{2,1,0:T(8,128)} custom-call(s32[5]{0:T(128)S(1)} %copy-done.7, f32[80,9216]{1,0:T(8,128)} %collective-permute-done.14.beside, f32[3,128,9216]{2,1,0:T(8,128)} %add_halo.6.image, f32[16]{0:T(128)S(1)} %copy-done.9), custom_call_target="tpu_custom_call", output_to_operand_aliasing={{}: (2, {})} | custom-call | flops 1 | bytes 1 | tf_op jit(solution)/shard_map/add_inner/pallas_call | solution.py:372
  268.5 4.9 %add_halo.7.image = f32[3,128,9216]{2,1,0:T(8,128)} custom-call(s32[5]{0:T(128)S(1)} %copy-done.7, f32[64,9216]{1,0:T(8,128)} %collective-permute-done.5.near, f32[64,9216]{1,0:T(8,128)} %collective-permute-done.12.out_side, f32[32,9216]{1,0:T(8,128)S(1)} %collective-permute-done.13.over_y.over_z, ...), custom_call_target="tpu_custom_call", output_to_operand_aliasing={{}: (5, {})} | custom-call | flops 1 | bytes 1 | tf_op jit(solution)/shard_map/add_halo/pallas_call | solution.py:342
  277.2 4.7 %add_inner.5.image = f32[3,128,9216]{2,1,0:T(8,128)} custom-call(s32[5]{0:T(128)S(1)} %copy-done.8, f32[32,9216]{1,0:T(8,128)} %collective-permute-done.11.beside, f32[3,128,9216]{2,1,0:T(8,128)} %add_halo.7.image, f32[16]{0:T(128)S(1)} %copy-done.9), custom_call_target="tpu_custom_call", output_to_operand_aliasing={{}: (2, {})} | custom-call | flops 1 | bytes 1 | tf_op jit(solution)/shard_map/add_inner/pallas_call | solution.py:372
  (69 shorter events, 73.5 us)
Async XLA Ops:
  3.2 55.4 %collective-permute-start.3 = (f32[64,9216]{1,0:T(8,128)}, f32[64,9216]{1,0:T(8,128)}, u32[]{:S(2)}, u32[]{:S(2)}) collective-permute-start(f32[64,9216]{1,0:T(8,128)} %middle_rows.2), channel_id=1, source_target_pairs={{0,1},{1,0},{2,3},{3,2},{4,5},{5,4},{6,7},{7,6},{8,9},{9,8},{10,11... | collective-permute-start | bytes 7077896 | tf_op jit(solution)/shard_map/ppermute | solution.py:440
  13.7 7.7 %copy-start.9 = (f32[16]{0:T(128)S(1)}, f32[16]{0:T(128)}, u32[]{:S(2)}) copy-start(f32[16]{0:T(128)} %token_.6) | copy-start | bytes 196
  13.7 54.9 %collective-permute-start.2 = (f32[64,9216]{1,0:T(8,128)}, f32[64,9216]{1,0:T(8,128)}, u32[]{:S(2)}, u32[]{:S(2)}) collective-permute-start(f32[64,9216]{1,0:T(8,128)} %rows_of.6), channel_id=1, source_target_pairs={{1,3},{2,0},{3,5},{4,2},{5,7},{6,4},{9,11},{10,8},{11,13},{12,10},... | collective-permute-start | bytes 7077896 | tf_op jit(solution)/shard_map/ppermute | solution.py:440
  20.1 51.5 %collective-permute-start.1 = (f32[3,16,9216]{2,1,0:T(8,128)}, f32[3,16,9216]{2,1,0:T(8,128)}, u32[]{:S(2)}, u32[]{:S(2)}) collective-permute-start(f32[3,16,9216]{2,1,0:T(8,128)} %head_of.1), channel_id=1, source_target_pairs={{8,0},{16,8},{24,16},{9,1},{17,9},{25,17},{10,2},{18,10},{26,18},{... | collective-permute-start | bytes 5308424 | tf_op jit(solution)/shard_map/ppermute | solution.py:440
  21.4 12.4 %copy-start.10 = (f32[16]{0:T(128)}, f32[16]{0:T(128)S(1)}, u32[]{:S(2)}) copy-start(f32[16]{0:T(128)S(1)} %get-tuple-element.222.scaled) | copy-start | bytes 196
  21.4 17.9 %copy-start.3 = (f32[3,9216]{1,0:T(4,128)S(1)}, f32[3,9216]{1,0:T(4,128)}, u32[]{:S(2)}) copy-start(f32[3,9216]{1,0:T(4,128)} %absorption.7) | copy-start | bytes 331780
  33.8 15.9 %copy-start = (f32[3,16,9216]{2,1,0:T(8,128)}, f32[3,16,9216]{2,1,0:T(8,128)S(1)}, u32[]{:S(2)}) copy-start(f32[3,16,9216]{2,1,0:T(8,128)S(1)} %mode_sums.1.sums) | copy-start | bytes 5308420
  33.8 37.8 %collective-permute-start = (f32[3,16,9216]{2,1,0:T(8,128)S(1)}, f32[3,16,9216]{2,1,0:T(8,128)}, u32[]{:S(2)}, u32[]{:S(2)}) collective-permute-start(f32[3,16,9216]{2,1,0:T(8,128)S(1)} %mode_sums.1.sums), channel_id=1, source_target_pairs={{8,0},{16,8},{24,16},{9,1},{17,9},{25,17},{10,2},{18,10},{26,18},{... | collective-permute-start | bytes 5308424 | tf_op jit(solution)/shard_map/ppermute | solution.py:440
  35.1 74.1 %collective-permute-start.5 = (f32[64,9216]{1,0:T(8,128)}, f32[64,9216]{1,0:T(8,128)}, u32[]{:S(2)}, u32[]{:S(2)}) collective-permute-start(f32[64,9216]{1,0:T(8,128)} %middle_rows.3), channel_id=1, source_target_pairs={{0,1},{1,0},{2,3},{3,2},{4,5},{5,4},{6,7},{7,6},{8,9},{9,8},{10,11... | collective-permute-start | bytes 7077896 | tf_op jit(solution)/shard_map/ppermute | solution.py:440
  74.6 59.8 %collective-permute-start.8 = (f32[32,9216]{1,0:T(8,128)}, f32[32,9216]{1,0:T(8,128)S(1)}, u32[]{:S(2)}, u32[]{:S(2)}) collective-permute-start(f32[32,9216]{1,0:T(8,128)} %picked_rows.3), channel_id=1, source_target_pairs={{0,1},{1,0},{2,3},{3,2},{4,5},{5,4},{6,7},{7,6},{8,9},{9,8},{10,11... | collective-permute-start | bytes 3538952 | tf_op jit(solution)/shard_map/ppermute | solution.py:440
  74.7 59.7 %collective-permute-start.7 = (f32[32,9216]{1,0:T(8,128)}, f32[32,9216]{1,0:T(8,128)}, u32[]{:S(2)}, u32[]{:S(2)}) collective-permute-start(f32[32,9216]{1,0:T(8,128)} %rows_of.7), channel_id=1, source_target_pairs={{1,3},{2,0},{3,5},{4,2},{5,7},{6,4},{9,11},{10,8},{11,13},{12,10},... | collective-permute-start | bytes 3538952 | tf_op jit(solution)/shard_map/ppermute | solution.py:440
  76.0 109.0 %collective-permute-start.9 = (f32[64,9216]{1,0:T(8,128)}, f32[64,9216]{1,0:T(8,128)}, u32[]{:S(2)}, u32[]{:S(2)}) collective-permute-start(f32[64,9216]{1,0:T(8,128)} %collective-permute-done.3.near), channel_id=1, source_target_pairs={{0,2},{2,4},{3,1},{4,6},{5,3},{7,5},{8,10},{10,12},{11,9},{12,14},... | collective-permute-start | bytes 7077896 | tf_op jit(solution)/shard_map/ppermute | solution.py:440
  86.3 79.6 %collective-permute-start.4 = (f32[3,16,9216]{2,1,0:T(8,128)}, f32[3,16,9216]{2,1,0:T(8,128)}, u32[]{:S(2)}, u32[]{:S(2)}) collective-permute-start(f32[3,16,9216]{2,1,0:T(8,128)} %carried.1), channel_id=1, source_target_pairs={{16,0},{24,8},{17,1},{25,9},{18,2},{26,10},{19,3},{27,11},{20,4},{... | collective-permute-start | bytes 5308424 | tf_op jit(solution)/shard_map/ppermute | solution.py:440
  112.2 47.6 %collective-permute-start.6 = (f32[32,9216]{1,0:T(8,128)}, f32[32,9216]{1,0:T(8,128)}, u32[]{:S(2)}, u32[]{:S(2)}) collective-permute-start(f32[32,9216]{1,0:T(8,128)} %picked_rows.4), channel_id=1, source_target_pairs={{0,1},{1,0},{2,3},{3,2},{4,5},{5,4},{6,7},{7,6},{8,9},{9,8},{10,11... | collective-permute-start | bytes 3538952 | tf_op jit(solution)/shard_map/ppermute | solution.py:440
  137.3 47.7 %collective-permute-start.10 = (f32[32,9216]{1,0:T(8,128)}, f32[32,9216]{1,0:T(8,128)}, u32[]{:S(2)}, u32[]{:S(2)}) collective-permute-start(f32[32,9216]{1,0:T(8,128)} %picked_rows.5), channel_id=1, source_target_pairs={{0,1},{1,0},{2,3},{3,2},{4,5},{5,4},{6,7},{7,6},{8,9},{9,8},{10,11... | collective-permute-start | bytes 3538952 | tf_op jit(solution)/shard_map/ppermute | solution.py:440
  139.4 55.5 %collective-permute-start.12 = (f32[64,9216]{1,0:T(8,128)}, f32[64,9216]{1,0:T(8,128)}, u32[]{:S(2)}, u32[]{:S(2)}) collective-permute-start(f32[64,9216]{1,0:T(8,128)} %collective-permute-done.5.near), channel_id=1, source_target_pairs={{0,2},{2,4},{3,1},{4,6},{5,3},{7,5},{8,10},{10,12},{11,9},{12,14},... | collective-permute-start | bytes 7077896 | tf_op jit(solution)/shard_map/ppermute | solution.py:440
  163.8 92.9 %collective-permute-start.14 = (f32[80,9216]{1,0:T(8,128)}, f32[80,9216]{1,0:T(8,128)}, u32[]{:S(2)}, u32[]{:S(2)}) collective-permute-start(f32[80,9216]{1,0:T(8,128)} %rows_of.8), channel_id=1, source_target_pairs={{0,1},{1,0},{2,3},{3,2},{4,5},{5,4},{6,7},{7,6},{8,9},{9,8},{10,11... | collective-permute-start | bytes 8847368 | tf_op jit(solution)/shard_map/ppermute | solution.py:440
  170.5 29.0 %copy-start.2 = (f32[32,9216]{1,0:T(8,128)S(1)}, f32[32,9216]{1,0:T(8,128)}, u32[]{:S(2)}) copy-start(f32[32,9216]{1,0:T(8,128)} %copy-done.1) | copy-start | bytes 3538948
  170.5 29.0 %copy-start.6 = (s32[5]{0:T(128)S(1)}, s32[5]{0:T(128)}, u32[]{:S(2)}) copy-start(s32[5]{0:T(128)} %stack.20.device) | copy-start | bytes 64
  185.0 60.5 %collective-permute-start.15 = (f32[64,9216]{1,0:T(8,128)}, f32[64,9216]{1,0:T(8,128)}, u32[]{:S(2)}, u32[]{:S(2)}) collective-permute-start(f32[64,9216]{1,0:T(8,128)} %copy-done.4), channel_id=1, source_target_pairs={{0,2},{2,4},{5,3},{7,5},{8,10},{10,12},{13,11},{15,13},{16,18},{18... | collective-permute-start | bytes 7077896 | tf_op jit(solution)/shard_map/ppermute | solution.py:440
  194.9 73.6 %collective-permute-start.13 = (f32[32,9216]{1,0:T(8,128)}, f32[32,9216]{1,0:T(8,128)S(1)}, u32[]{:S(2)}, u32[]{:S(2)}) collective-permute-start(f32[32,9216]{1,0:T(8,128)} %collective-permute-done.10.over_y), channel_id=1, source_target_pairs={{0,2},{2,4},{3,1},{4,6},{5,3},{7,5},{8,10},{10,12},{11,9},{12,14},... | collective-permute-start | bytes 3538952 | tf_op jit(solution)/shard_map/ppermute | solution.py:440
  199.4 74.0 %collective-permute-start.11 = (f32[32,9216]{1,0:T(8,128)}, f32[32,9216]{1,0:T(8,128)}, u32[]{:S(2)}, u32[]{:S(2)}) collective-permute-start(f32[32,9216]{1,0:T(8,128)} %copy-done.5), channel_id=1, source_target_pairs={{0,1},{1,0},{2,3},{3,2},{4,5},{5,4},{6,7},{7,6},{8,9},{9,8},{10,11... | collective-permute-start | bytes 3538952 | tf_op jit(solution)/shard_map/ppermute | solution.py:440
  273.4 10.0 %collective-permute-start.17 = (f32[8,9216]{1,0:T(8,128)S(1)}, f32[8,9216]{1,0:T(8,128)S(1)}, u32[]{:S(2)}, u32[]{:S(2)}) collective-permute-start(f32[8,9216]{1,0:T(8,128)S(1)} %rows_of.10), channel_id=1, source_target_pairs={{0,1},{1,0},{2,3},{3,2},{4,5},{5,4},{6,7},{7,6},{8,9},{9,8},{10,11... | collective-permute-start | bytes 884744 | tf_op jit(solution)/shard_map/ppermute | solution.py:440
  276.0 11.1 %collective-permute-start.16 = (f32[8,9216]{1,0:T(8,128)S(1)}, f32[8,9216]{1,0:T(8,128)S(1)}, u32[]{:S(2)}, u32[]{:S(2)}) collective-permute-start(f32[8,9216]{1,0:T(8,128)S(1)} %rows_of.11), channel_id=1, source_target_pairs={{0,1},{1,0},{2,3},{3,2},{4,5},{5,4},{6,7},{7,6},{8,9},{9,8},{10,11... | collective-permute-start | bytes 884744 | tf_op jit(solution)/shard_map/ppermute | solution.py:440
  (7 other events, 23.6 us)

commit v3 on v2

--- a/solution.py
+++ b/solution.py
@@ -178,100 +178,99 @@
     )(scaled, mode_gain, scaled[None], mode_gain[None], *operands, image)
 
 
-def copy_rows(source, out, sems):
+def copy_rows(source, out, held, sems):
     pieces = [pl.ds(k * ROWS, ROWS) for k in range(out.shape[0] // ROWS)]
-    copies = [
-        pltpu.make_async_copy(source.at[rows], out.at[rows], sems.at[k]) for k, rows in enumerate(pieces)
+    inward = [
+        pltpu.make_async_copy(source.at[rows], held.at[rows], sems.at[0, k]) for k, rows in enumerate(pieces)
     ]
-    for copy in copies:
+    outward = [
+        pltpu.make_async_copy(held.at[rows], out.at[rows], sems.at[1, k]) for k, rows in enumerate(pieces)
+    ]
+    for copy in inward:
         copy.start()
-    for copy in copies:
+    for copy, onward in zip(inward, outward):
+        copy.wait()
+        onward.start()
+    for copy in outward:
         copy.wait()
 
 
 def staged(kernel, name, shape, device, *arrays):
     return pl.pallas_call(
         kernel,
-        in_specs=[pl.BlockSpec(memory_space=pltpu.SMEM)]
+        in_specs=[pl.BlockSpec(memory_space=pltpu.SMEM)] * len(device)
         + [pl.BlockSpec(memory_space=pl.ANY)] * len(arrays),
-        out_specs=pl.BlockSpec(memory_space=pltpu.VMEM),
-        out_shape=pltpu.VMEM(shape, jnp.float32),
-        scratch_shapes=[pltpu.SemaphoreType.DMA((math.prod(shape[:-1]) // ROWS,))],
+        out_specs=pl.BlockSpec(memory_space=pl.ANY),
+        out_shape=jax.ShapeDtypeStruct(shape, jnp.float32),
+        scratch_shapes=[
+            pltpu.VMEM(shape, jnp.float32),
+            pltpu.SemaphoreType.DMA((2, math.prod(shape[:-1]) // ROWS)),
+        ],
+        compiler_params=pltpu.CompilerParams(vmem_limit_bytes=VMEM_LIMIT),
         cost_estimate=SHORT,
         name=name,
-    )(device, *arrays)
-
-
-def rows_kernel(which, lo, device, field, out, sems):
-    copy_rows(field.at[device[which], pl.ds(lo, out.shape[0])], out, sems)
-
-
-def middle_kernel(lo, field, token, out, sems):
-    copy_rows(field.at[1, pl.ds(lo, out.shape[0])], out, sems)
-
-
-def middle_rows(field, token, lo, hi):
-    shape = (hi - lo, field.shape[-1])
-    return pl.pallas_call(
-        functools.partial(middle_kernel, lo),
-        in_specs=[pl.BlockSpec(memory_space=pl.ANY)] * 2,
-        out_specs=pl.BlockSpec(memory_space=pltpu.VMEM),
-        out_shape=pltpu.VMEM(shape, jnp.float32),
-        scratch_shapes=[pltpu.SemaphoreType.DMA((shape[0] // ROWS,))],
-        cost_estimate=SHORT,
-        name="middle_rows",
-    )(field, token)
+    )(*device, *arrays)
+
+
+def rows_kernel(which, lo, device, field, out, held, sems):
+    copy_rows(field.at[device[which], pl.ds(lo, out.shape[0])], out, held, sems)
+
+
+def middle_kernel(lo, field, *refs):
+    out, held, sems = refs[-3:]
+    copy_rows(field.at[1, pl.ds(lo, out.shape[0])], out, held, sems)
+
+
+def middle_rows(field, lo, hi, *token):
+    kernel = functools.partial(middle_kernel, lo)
+    return staged(kernel, "middle_rows", (hi - lo, field.shape[-1]), [], field, *token)
 
 
 def rows_of(device, which, field, lo, hi):
     kernel = functools.partial(rows_kernel, which, lo)
-    return staged(kernel, "rows_of", (hi - lo, field.shape[-1]), device, field)
-
-
-def pick_kernel(last, relayed_lo, own_lo, device, field, relayed, out, sems):
+    return staged(kernel, "rows_of", (hi - lo, field.shape[-1]), [device], field)
+
+
+def pick_kernel(last, relayed_lo, own_lo, device, field, relayed, out, held, sems):
     count = out.shape[0]
 
     @pl.when(device[RANK] < last)
     def _():
-        copy_rows(relayed.at[pl.ds(relayed_lo, count)], out, sems)
+        copy_rows(relayed.at[pl.ds(relayed_lo, count)], out, held, sems)
 
     @pl.when(device[RANK] >= last)
     def _():
-        copy_rows(field.at[device[OUTER], pl.ds(own_lo, count)], out, sems)
+        copy_rows(field.at[device[OUTER], pl.ds(own_lo, count)], out, held, sems)
 
 
 def picked_rows(device, field, relayed, last, relayed_lo, own_lo, count):
     kernel = functools.partial(pick_kernel, last, relayed_lo, own_lo)
-    return staged(kernel, "picked_rows", (count, field.shape[-1]), device, field, relayed)
-
-
-def head_kernel(device, field, out, sems):
+    return staged(kernel, "picked_rows", (count, field.shape[-1]), [device], field, relayed)
+
+
+def head_kernel(field, out, held, sems):
     per_plane = BAND // ROWS
     for p in range(out.shape[0]):
-        copy_rows(field.at[p, pl.ds(0, BAND)], out.at[p], sems.at[pl.ds(p * per_plane, per_plane)])
-
-
-def head_of(device, field):
+        copy_rows(field.at[p, pl.ds(0, BAND)], out.at[p], held.at[p], sems.at[:, pl.ds(p * per_plane, per_plane)])
+
+
+def head_of(field):
     depth, _, plane = field.shape
-    return staged(head_kernel, "head_of", (depth, BAND, plane), device, field)
-
-
-def join_kernel(device, *refs):
-    arrays, (out, sems) = refs[:-2], refs[-2:]
+    return staged(head_kernel, "head_of", (depth, BAND, plane), [], field)
+
+
+def join_kernel(*refs):
+    arrays, (out, held, sems) = refs[:-3], refs[-3:]
     at = 0
     for array in arrays:
-        rows = array.shape[0]
-        copy_rows(array, out.at[pl.ds(at, rows)], sems.at[pl.ds(at // ROWS, rows // ROWS)])
-        at += rows
-
-
-def joined(device, arrays):
+        rows = pl.ds(at, array.shape[0])
+        copy_rows(array, out.at[rows], held.at[rows], sems.at[:, pl.ds(at // ROWS, array.shape[0] // ROWS)])
+        at += array.shape[0]
+
+
+def joined(arrays):
     shape = (sum(array.shape[0] for array in arrays), arrays[0].shape[1])
-    return staged(join_kernel, "joined", shape, device, *arrays)
-
-
-def block_rows(*edges):
-    return 2 * ROWS if all(edge % (2 * ROWS) == 0 for edge in edges) else ROWS
+    return staged(join_kernel, "joined", shape, [], *arrays)
 
 
 def plane_kernel(depth, shifts, absorption, field, *refs):
@@ -301,7 +300,7 @@
         image[p] = total
 
 
-def plane_terms(token, absorption, field, image, start, end):
+def plane_terms(absorption, field, image, start, end):
     depth, _, plane = field.shape
     shifts = tuple(OFFSETS) + tuple(offset * NY for offset in OFFSETS)
     first = start // ROWS
@@ -311,82 +310,109 @@
     return pl.pallas_call(
         functools.partial(plane_kernel, depth, shifts),
         grid=((end - start) // ROWS,),
-        in_specs=[pl.BlockSpec(absorption.shape, lambda t: (0, 0)), slab, in_any] + [in_any] * len(started),
+        in_specs=[pl.BlockSpec(absorption.shape, lambda t: (0, 0)), slab] + [in_any] * len(started),
         out_specs=slab,
         scratch_shapes=[pltpu.VMEM((len(shifts), plane), jnp.float32)],
         out_shape=jax.ShapeDtypeStruct(field.shape, jnp.float32),
-        input_output_aliases={3: 0} if started else {},
+        input_output_aliases={2: 0} if started else {},
         compiler_params=pltpu.CompilerParams(vmem_limit_bytes=VMEM_LIMIT),
         cost_estimate=SHORT,
         name="plane_terms",
-    )(absorption, field, token, *started)
-
-
-def halo_kernel(last, device, near, out_side, over_y, over_z, before, image):
-    beyond = jnp.where(device[PARTNER_RANK] < last, over_y[...], over_z[...])
-    outer, middle, inner = device[OUTER], device[MIDDLE], device[INNER]
-    image[outer] = before[outer] + NEAR * beyond + FAR * out_side[...]
-    image[middle] = before[middle] + FAR * beyond
-    image[inner] = before[inner] + FAR * near[...]
-
-
-def add_halo(device, near, out_side, over_y, over_z, image, last, start, end):
-    depth, _, plane = image.shape
-    beside = (near, out_side, over_y, over_z)
-    rows = block_rows(start, end, *[row for _, row in beside])
-    slab = pl.BlockSpec((depth, rows, plane), lambda t, s: (0, start // rows + t, 0))
-
-    def single(row):
-        return pl.BlockSpec((rows, plane), lambda t, s: (row // rows + t, 0))
-
+    )(absorption, field, *started)
+
+
+def update_kernel(change, planes_of, count, start, *refs):
+    pieces = count // ROWS
+    device, refs = refs[0], refs[1:]
+    arrays, (image, held, came, in_sems, came_sems, out_sems) = refs[:-6], refs[-6:]
+    beside, before = arrays[: len(change.firsts)], arrays[len(change.firsts)]
+    planes = planes_of(device)
+
+    def held_copy(p, k, out):
+        there = pl.ds(start + k * ROWS, ROWS)
+        here = held.at[p, pl.ds(k * ROWS, ROWS)]
+        if out:
+            return pltpu.make_async_copy(here, image.at[planes[p], there], out_sems.at[p, k])
+        return pltpu.make_async_copy(before.at[planes[p], there], here, in_sems.at[p, k])
+
+    def came_copy(i, k):
+        source = beside[i].at[pl.ds(firsts[i] + k * ROWS, ROWS)]
+        return pltpu.make_async_copy(source, came.at[i, pl.ds(k * ROWS, ROWS)], came_sems.at[i, k])
+
+    firsts = change.firsts
+    for k in range(pieces):
+        for i in range(len(beside)):
+            came_copy(i, k).start()
+        for p in range(len(planes)):
+            held_copy(p, k, False).start()
+    for k in range(pieces):
+        for i in range(len(beside)):
+            came_copy(i, k).wait()
+        for p in range(len(planes)):
+            held_copy(p, k, False).wait()
+        at = slice(k * ROWS, (k + 1) * ROWS)
+        for p, added in enumerate(change(device, [came[i, at] for i in range(len(beside))])):
+            held[p, at] += added
+            held_copy(p, k, True).start()
+    for k in range(pieces):
+        for p in range(len(planes)):
+            held_copy(p, k, True).wait()
+
+
+class Change:
+    def __init__(self, change, firsts):
+        self.change, self.firsts = change, firsts
+
+    def __call__(self, device, beside):
+        return self.change(device, beside)
+
+
+def update(name, change, planes_of, plane_count, device, arrays, image, start, count, token=()):
+    plane = image.shape[-1]
+    pieces = count // ROWS
+    in_any = pl.BlockSpec(memory_space=pl.ANY)
     return pl.pallas_call(
-        functools.partial(halo_kernel, last),
-        grid_spec=pltpu.PrefetchScalarGridSpec(
-            num_scalar_prefetch=1,
-            grid=((end - start) // rows,),
-            in_specs=[*[single(row) for _, row in beside], slab],
-            out_specs=slab,
-        ),
+        functools.partial(update_kernel, Change(change, [row for _, row in arrays]), planes_of, count, start),
+        in_specs=[pl.BlockSpec(memory_space=pltpu.SMEM)] + [in_any] * (len(arrays) + 1 + len(token)),
+        out_specs=in_any,
         out_shape=jax.ShapeDtypeStruct(image.shape, jnp.float32),
-        input_output_aliases={5: 0},
+        scratch_shapes=[
+            pltpu.VMEM((plane_count, count, plane), jnp.float32),
+            pltpu.VMEM((len(arrays), count, plane), jnp.float32),
+            pltpu.SemaphoreType.DMA((plane_count, pieces)),
+            pltpu.SemaphoreType.DMA((len(arrays), pieces)),
+            pltpu.SemaphoreType.DMA((plane_count, pieces)),
+        ],
+        input_output_aliases={1 + len(arrays): 0},
         compiler_params=pltpu.CompilerParams(vmem_limit_bytes=VMEM_LIMIT),
         cost_estimate=SHORT,
-        name="add_halo",
-    )(device, *[array for array, _ in beside], image)
-
-
-def inner_kernel(device, beside, image, token, out):
-    weight = jnp.where(pl.program_id(1) == 0, NEAR, FAR)
-    out[...] = image[...] + weight * beside[...]
-
-
-def add_inner(device, beside, image, token, start):
-    plane = image.shape[-1]
-    count = beside.shape[0]
-    rows = block_rows(start, count)
-
-    def place(t, g, s):
-        return jnp.where(g == 0, s[INNER], s[MIDDLE]), start // rows + t, 0
-
-    at = pl.BlockSpec((None, rows, plane), place)
-    return pl.pallas_call(
-        inner_kernel,
-        grid_spec=pltpu.PrefetchScalarGridSpec(
-            num_scalar_prefetch=1,
-            grid=(count // rows, 2),
-            in_specs=[
-                pl.BlockSpec((rows, plane), lambda t, g, s: (t, 0)),
-                at,
-                pl.BlockSpec(memory_space=pl.ANY),
-            ],
-            out_specs=at,
-        ),
-        out_shape=jax.ShapeDtypeStruct(image.shape, jnp.float32),
-        input_output_aliases={2: 0},
-        compiler_params=pltpu.CompilerParams(vmem_limit_bytes=VMEM_LIMIT),
-        cost_estimate=SHORT,
-        name="add_inner",
-    )(device, beside, image, token)
+        name=name,
+    )(device, *[array for array, _ in arrays], image, *token)
+
+
+def add_halo(device, near, out_side, over_y, over_z, image, last, start, end):
+
+    def change(device, beside):
+        near, out_side, over_y, over_z = beside
+        beyond = jnp.where(device[PARTNER_RANK] < last, over_y, over_z)
+        return NEAR * beyond + FAR * out_side, FAR * beyond, FAR * near
+
+    def planes_of(device):
+        return device[OUTER], device[MIDDLE], device[INNER]
+
+    arrays = (near, out_side, over_y, over_z)
+    return update("add_halo", change, planes_of, 3, device, arrays, image, start, end - start)
+
+
+def add_inner(device, beside, image, start, token):
+
+    def change(device, beside):
+        return NEAR * beside[0], FAR * beside[0]
+
+    def planes_of(device):
+        return device[INNER], device[MIDDLE]
+
+    return update("add_inner", change, planes_of, 2, device, [(beside, 0)], image, start, beside.shape[0], token)
 
 
 def cuts(steps, pieces):
@@ -447,12 +473,13 @@
 
     mid_cuts = between(0, whole_rows(1 / 2), steps)
     out_cuts = cuts(steps, pairs)
-    in_cuts = between(0, whole_rows(5 / 8), whole_rows(7 / 8), steps - ROWS, steps)
+    in_cuts = between(0, whole_rows(9 / 16), steps - ROWS, steps)
     plane_cuts = cuts(steps, 4)
     slots = pairs - 1
 
     def middle_send(k):
-        return send(middle_rows(field, order.token, *mid_cuts[k]), "space", swap)
+        token = [order.token] if k else []
+        return send(middle_rows(field, *mid_cuts[k], *token), "space", swap)
 
     def outer_send(j):
         last = slots - j
@@ -488,13 +515,13 @@
     next_y()
     first = out_cuts[(slots + 1) // 2][0]
     relayed = [relay(0, first)]
-    head = send(head_of(order(device), field), "tm", back(1))
+    head = send(head_of(order(field)), "tm", back(1))
     sums = mode_sums(order(scaled), field)
     aways = [1]
     later = [send(sums, "tm", back(1))]
 
     def plane(k, image):
-        return order(plane_terms(order.token, absorption, field, image, *plane_cuts[k]))
+        return order(plane_terms(order(absorption), field, image, *plane_cuts[k]))
 
     image = plane(0, None)
     y_mid = [order(sent[0])]
@@ -535,7 +562,8 @@
 
     y_out = []
     def inner(k, image):
-        return order(add_inner(device, y_in[k], image, order.token, in_cuts[k][0]))
+        token = [order.token] if k == len(in_cuts) - 1 else []
+        return order(add_inner(order(device), y_in[k], image, in_cuts[k][0], token))
 
     for j in range(slots):
         y_out.append(order(sent[2 + j]))
@@ -549,7 +577,7 @@
         if j == min(1, slots - 1):
             later[1:] = order(later[1:])
         if j == slots - 2:
-            together = joined(order(device), y_out)
+            together = joined(order(list(y_out)))
     z_mid[0] = order(z_mid[0])
     most = list(range(slots - 1))
     z_most = outer_onward(most) if most else None
@@ -558,19 +586,17 @@
     z_last = outer_onward([slots - 1])
     image = halo(0, image)
     image = order(add_history(order(scaled), mode_gain, field, head, aways, later, image))
-    y_in = []
+    y_in = [order(sent[2 + slots])]
+    next_y()
+    image = inner(0, image)
     if most:
         z_most = order(z_most)
     for q in range(1, slots):
         image = halo(q, image)
-    y_in.append(order(sent[2 + slots]))
-    next_y()
-    image = inner(0, image)
     z_last = order(z_last)
     image = halo(slots, image)
     for k in range(1, len(in_cuts)):
         y_in.append(order(sent[2 + slots + k]))
-        next_y()
         image = inner(k, image)
     return image.transpose(1, 0, 2)
 

time: 291 us -> 289 us (level)
  waiting for transfers between devices: 80.3 us -> 97 us
  Pallas kernels: 162 us -> 147 us
  local copies, waits for them, and re-layouts: 3.28 us -> 0.24 us
    ppermute x18 -> x17, waiting for transfers between devices: 80.3 us -> 97 us  [send(): return lax.ppermute(order(value), axis, route)]
    pallas_call x21 -> x19, Pallas kernels: 79.9 us -> 67.2 us  [the longest x7 34.5 us: update(): pl.pallas_call(functools.partial(update_kernel, Change(change, [row for _...]
    ppermute x18 -> x17, starting transfers between devices: 43.2 us -> 42.1 us  [send(): return lax.ppermute(order(value), axis, route)]
  transfers between devices with their start and end apart: 18 -> 17, of which waited for: 10 -> 11; matrix products, arithmetic and copies ran while one was open for 0% -> 0% of each run, Pallas kernels for 54% -> 49%
where the time goes in v3:
time: 289 us; the launch traced here: 287 us
  Pallas kernels  147 us (51%)
  waiting for transfers between devices  97 us (34%)
  starting transfers between devices  42.1 us (15%)
    ppermute x17, waiting for transfers between devices, send(): return lax.ppermute(order(value), axis, route)  97 us
    ppermute x17, starting transfers between devices, send(): return lax.ppermute(order(value), axis, route)  42.1 us
    pallas_call x4, Pallas kernels, plane_terms(): pl.pallas_call(functools.partial(plane_kernel, depth, shifts), grid=((end...  41.5 us
    pallas_call x7, Pallas kernels, update(): pl.pallas_call(functools.partial(update_kernel, Change(change, [row for _...  34.5 us
    pallas_call x12, Pallas kernels, staged(): pl.pallas_call(kernel, in_specs=[pl.BlockSpec(memory_space=pltpu.SMEM)] *...  32.7 us
    pallas_call x1, Pallas kernels, add_history(): pl.pallas_call(functools.partial(history_kernel, aways), grid=(depth, pla...  21.9 us
    pallas_call x1, Pallas kernels, mode_sums(): pl.pallas_call(sums_kernel, grid=(depth, plane // tile), in_specs=[pl.Blo...  12.3 us
  transfers between devices with their start and end apart: 17, of which 11 were waited for; matrix products, arithmetic and copies ran while one was open for 0% of the time, Pallas kernels for 49%

profile of v3, /device:TPU:0, one launch (start us, length us, event | category | flops | bytes accessed | tf_op | source)
XLA Modules:
  0.0 287.3 jit_solution(6221671681017061449)
XLA Ops:
  11.9 5.6 %head_of.1 = f32[3,16,9216]{2,1,0:T(8,128)} custom-call(f32[3,128,9216]{2,1,0:T(8,128)} %bitcast.13), custom_call_target="tpu_custom_call" | custom-call | flops 1 | bytes 1 | tf_op jit(solution)/shard_map/head_of/pallas_call | solution.py:199
  18.8 12.3 %mode_sums.1.sums = f32[3,16,9216]{2,1,0:T(8,128)S(1)} custom-call(f32[16]{0:T(128)S(1)} %get-tuple-element.233.scaled, f32[3,128,9216]{2,1,0:T(8,128)} %bitcast.14), custom_call_target="tpu_custom_call" | custom-call | flops 1 | bytes 1 | tf_op jit(solution)/shard_map/mode_sums/pallas_call | solution.py:67
  35.4 10.4 %plane_terms.4.refs_0_ = f32[3,128,9216]{2,1,0:T(8,128)} custom-call(f32[3,9216]{1,0:T(4,128)S(1)} %copy-done.5, f32[3,128,9216]{2,1,0:T(8,128)} %bitcast.15), custom_call_target="tpu_custom_call" | custom-call | flops 1 | bytes 1 | tf_op jit(solution)/shard_map/plane_terms/pallas_call | solution.py:310
  45.8 12.1 %collective-permute-done.4.refs_1_ = f32[64,9216]{1,0:T(8,128)S(1)} collective-permute-done((f32[64,9216]{1,0:T(8,128)}, f32[64,9216]{1,0:T(8,128)S(1)}, u32[]{:S(2)}, u32[]{:S(2)}) %collective-permute-start.4) | collective-permute-done | bytes 2359328 | tf_op jit(solution)/shard_map/ppermute | solution.py:466
  57.9 7.3 %collective-permute-done.3.relayed = f32[64,9216]{1,0:T(8,128)S(1)} collective-permute-done((f32[64,9216]{1,0:T(8,128)S(1)}, f32[64,9216]{1,0:T(8,128)S(1)}, u32[]{:S(2)}, u32[]{:S(2)}) %collective-permute-start.3) | collective-permute-done | bytes 2359328 | tf_op jit(solution)/shard_map/ppermute | solution.py:466
  72.3 6.0 %collective-permute-start.12 = (f32[64,9216]{1,0:T(8,128)S(1)}, f32[64,9216]{1,0:T(8,128)}, u32[]{:S(2)}, u32[]{:S(2)}) collective-permute-start(f32[64,9216]{1,0:T(8,128)S(1)} %collective-permute-done.4.refs_1_), channel_id=1, source_target_pairs={{0,2},{2,4},{3,1},{4,6},{5,3},{7,5},{8,10},{10,12},{11,9},{12,14},... | collective-permute-start | bytes 7077896 | tf_op jit(solution)/shard_map/ppermute | solution.py:466
  78.4 4.3 %carried.1 = f32[3,16,9216]{2,1,0:T(8,128)} custom-call(f32[16]{0:T(128)} %copy-done.11, f32[3,16,9216]{2,1,0:T(8,128)} %copy-done.2, f32[3,16,9216]{2,1,0:T(8,128)} %copy-done.3), custom_call_target="tpu_custom_call" | custom-call | flops 1 | bytes 1 | tf_op jit(solution)/shard_map/carried/pallas_call | solution.py:93
  84.0 10.4 %plane_terms.5.refs_0_ = f32[3,128,9216]{2,1,0:T(8,128)} custom-call(f32[3,9216]{1,0:T(4,128)S(1)} %copy-done.5, f32[3,128,9216]{2,1,0:T(8,128)} %bitcast.18, f32[3,128,9216]{2,1,0:T(8,128)} %plane_terms.4.refs_0_), custom_call_target="tpu_custom_call", output_to_operand_aliasing={{}: (2, {})} | custom-call | flops 1 | bytes 1 | tf_op jit(solution)/shard_map/plane_terms/pallas_call | solution.py:310
  94.4 14.1 %collective-permute-done.refs_1_ = f32[64,9216]{1,0:T(8,128)} collective-permute-done((f32[64,9216]{1,0:T(8,128)}, f32[64,9216]{1,0:T(8,128)}, u32[]{:S(2)}, u32[]{:S(2)}) %collective-permute-start) | collective-permute-done | bytes 2359328 | tf_op jit(solution)/shard_map/ppermute | solution.py:466
  112.6 10.4 %plane_terms.6.refs_0_ = f32[3,128,9216]{2,1,0:T(8,128)} custom-call(f32[3,9216]{1,0:T(4,128)S(1)} %copy-done.6, f32[3,128,9216]{2,1,0:T(8,128)} %bitcast.20, f32[3,128,9216]{2,1,0:T(8,128)} %plane_terms.5.refs_0_), custom_call_target="tpu_custom_call", output_to_operand_aliasing={{}: (2, {})} | custom-call | flops 1 | bytes 1 | tf_op jit(solution)/shard_map/plane_terms/pallas_call | solution.py:310
  123.0 10.9 %collective-permute-done.7.refs_0_.refs_3_ = f32[32,9216]{1,0:T(8,128)} collective-permute-done((f32[32,9216]{1,0:T(8,128)}, f32[32,9216]{1,0:T(8,128)}, u32[]{:S(2)}, u32[]{:S(2)}) %collective-permute-start.7) | collective-permute-done | bytes 1179680 | tf_op jit(solution)/shard_map/ppermute | solution.py:466
  141.7 10.4 %plane_terms.7.refs_5_ = f32[3,128,9216]{2,1,0:T(8,128)} custom-call(f32[3,9216]{1,0:T(4,128)S(1)} %copy-done.6, f32[3,128,9216]{2,1,0:T(8,128)} %bitcast.22, f32[3,128,9216]{2,1,0:T(8,128)} %plane_terms.6.refs_0_), custom_call_target="tpu_custom_call", output_to_operand_aliasing={{}: (2, {})} | custom-call | flops 1 | bytes 1 | tf_op jit(solution)/shard_map/plane_terms/pallas_call | solution.py:310
  152.1 6.9 %collective-permute-done.5.refs_1_.refs_3_ = f32[32,9216]{1,0:T(8,128)S(1)} collective-permute-done((f32[32,9216]{1,0:T(8,128)S(1)}, f32[32,9216]{1,0:T(8,128)S(1)}, u32[]{:S(2)}, u32[]{:S(2)}) %collective-permute-start.5) | collective-permute-done | bytes 1179680 | tf_op jit(solution)/shard_map/ppermute | solution.py:466
  168.3 16.1 %collective-permute-done.9.refs_3_ = f32[32,9216]{1,0:T(8,128)} collective-permute-done((f32[32,9216]{1,0:T(8,128)S(1)}, f32[32,9216]{1,0:T(8,128)}, u32[]{:S(2)}, u32[]{:S(2)}) %collective-permute-start.9) | collective-permute-done | bytes 1179680 | tf_op jit(solution)/shard_map/ppermute | solution.py:466
  184.4 5.4 %collective-permute-start.16 = (f32[64,9216]{1,0:T(8,128)}, f32[64,9216]{1,0:T(8,128)}, u32[]{:S(2)}, u32[]{:S(2)}) collective-permute-start(f32[64,9216]{1,0:T(8,128)} %joined.1), channel_id=1, source_target_pairs={{0,2},{2,4},{5,3},{7,5},{8,10},{10,12},{13,11},{15,13},{16,18},{18... | collective-permute-start | bytes 7077896 | tf_op jit(solution)/shard_map/ppermute | solution.py:466
  193.0 4.3 %collective-permute-start.15 = (f32[32,9216]{1,0:T(8,128)}, f32[32,9216]{1,0:T(8,128)S(1)}, u32[]{:S(2)}, u32[]{:S(2)}) collective-permute-start(f32[32,9216]{1,0:T(8,128)} %collective-permute-done.9.refs_3_), channel_id=1, source_target_pairs={{0,2},{2,4},{3,1},{4,6},{5,3},{7,5},{8,10},{10,12},{11,9},{12,14},... | collective-permute-start | bytes 3538952 | tf_op jit(solution)/shard_map/ppermute | solution.py:466
  197.5 5.8 %add_halo.4.refs_3_ = f32[3,128,9216]{2,1,0:T(8,128)} custom-call(s32[5]{0:T(128)S(1)} %stack.20.device.refs_0_, f32[64,9216]{1,0:T(8,128)S(1)} %collective-permute-done.4.refs_1_, f32[64,9216]{1,0:T(8,128)} %collective-permute-done.12.refs_2_, f32[32,9216]{1,0:T(8,128)} %collective-permute-done.7.refs_0_.refs_3_, ...), custom_call_target="tpu_custom_call", output_to_operand_aliasing={{}: (5, {})} | custom-call | flops 1 | bytes 1 | tf_op jit(solution)/shard_map/add_halo/pallas_call | solution.py:374
  203.4 21.9 %add_history.1.refs_2_ = f32[3,128,9216]{2,1,0:T(8,128)} custom-call(f32[16]{0:T(128)S(1)} %copy-done.12, f32[16]{0:T(128)S(1)} %get-tuple-element.279.mode_gain, f32[1,16]{1,0:T(1,128)S(1)} %bitcast.8, f32[1,16]{1,0:T(1,128)S(1)} %bitcast.9, f32[3,128,9216]{2,1,0:T(8,128)} %bitcast.25, ...), custom_call_target="tpu_custom_call", output_to_operand_aliasing={{}: (8, {})} | custom-call | flops 1 | bytes 1 | tf_op jit(solution)/shard_map/add_history/pallas_call | solution.py:161
  225.3 16.0 %collective-permute-done.8.refs_1_ = f32[72,9216]{1,0:T(8,128)} collective-permute-done((f32[72,9216]{1,0:T(8,128)}, f32[72,9216]{1,0:T(8,128)}, u32[]{:S(2)}, u32[]{:S(2)}) %collective-permute-start.8) | collective-permute-done | bytes 2654240 | tf_op jit(solution)/shard_map/ppermute | solution.py:466
  245.0 6.4 %add_inner.3.refs_5_ = f32[3,128,9216]{2,1,0:T(8,128)} custom-call(s32[5]{0:T(128)S(1)} %stack.20.device.refs_0_, f32[72,9216]{1,0:T(8,128)} %collective-permute-done.8.refs_1_, f32[3,128,9216]{2,1,0:T(8,128)} %add_history.1.refs_2_), custom_call_target="tpu_custom_call", output_to_operand_aliasing={{}: (2, {})} | custom-call | flops 1 | bytes 1 | tf_op jit(solution)/shard_map/add_inner/pallas_call | solution.py:374
  251.4 5.4 %add_halo.5.refs_5_ = f32[3,128,9216]{2,1,0:T(8,128)} custom-call(s32[5]{0:T(128)S(1)} %stack.20.device.refs_0_, f32[64,9216]{1,0:T(8,128)S(1)} %collective-permute-done.4.refs_1_, f32[64,9216]{1,0:T(8,128)} %collective-permute-done.12.refs_2_, f32[32,9216]{1,0:T(8,128)S(1)} %collective-permute-done.5.refs_1_.refs_3_, ...), custom_call_target="tpu_custom_call", output_to_operand_aliasing={{}: (5, {})} | custom-call | flops 1 | bytes 1 | tf_op jit(solution)/shard_map/add_halo/pallas_call | solution.py:374
  256.8 5.6 %add_halo.6.refs_5_ = f32[3,128,9216]{2,1,0:T(8,128)} custom-call(s32[5]{0:T(128)S(1)} %stack.20.device.refs_0_, f32[64,9216]{1,0:T(8,128)} %collective-permute-done.refs_1_, f32[64,9216]{1,0:T(8,128)S(1)} %collective-permute-done.11.refs_2_, f32[32,9216]{1,0:T(8,128)} %collective-permute-done.9.refs_3_, ...), custom_call_target="tpu_custom_call", output_to_operand_aliasing={{}: (5, {})} | custom-call | flops 1 | bytes 1 | tf_op jit(solution)/shard_map/add_halo/pallas_call | solution.py:374
  265.7 4.6 %add_halo.7.refs_2_ = f32[3,128,9216]{2,1,0:T(8,128)} custom-call(s32[5]{0:T(128)S(1)} %stack.20.device.refs_0_, f32[64,9216]{1,0:T(8,128)} %collective-permute-done.refs_1_, f32[64,9216]{1,0:T(8,128)S(1)} %collective-permute-done.11.refs_2_, f32[32,9216]{1,0:T(8,128)S(1)} %collective-permute-done.15.refs_3_.refs_4_, ...), custom_call_target="tpu_custom_call", output_to_operand_aliasing={{}: (5, {})} | custom-call | flops 1 | bytes 1 | tf_op jit(solution)/shard_map/add_halo/pallas_call | solution.py:374
  270.3 8.9 %collective-permute-done.14.refs_1_ = f32[48,9216]{1,0:T(8,128)} collective-permute-done((f32[48,9216]{1,0:T(8,128)}, f32[48,9216]{1,0:T(8,128)}, u32[]{:S(2)}, u32[]{:S(2)}) %collective-permute-start.14) | collective-permute-done | bytes 1769504 | tf_op jit(solution)/shard_map/ppermute | solution.py:466
  (71 shorter events, 65.3 us)
Async XLA Ops:
  2.6 55.3 %collective-permute-start.4 = (f32[64,9216]{1,0:T(8,128)}, f32[64,9216]{1,0:T(8,128)S(1)}, u32[]{:S(2)}, u32[]{:S(2)}) collective-permute-start(f32[64,9216]{1,0:T(8,128)} %middle_rows.2), channel_id=1, source_target_pairs={{0,1},{1,0},{2,3},{3,2},{4,5},{5,4},{6,7},{7,6},{8,9},{9,8},{10,11... | collective-permute-start | bytes 7077896 | tf_op jit(solution)/shard_map/ppermute | solution.py:466
  10.6 8.2 %copy-start.15 = (f32[16]{0:T(128)S(1)}, f32[16]{0:T(128)}, u32[]{:S(2)}) copy-start(f32[16]{0:T(128)} %param.7) | copy-start | bytes 196
  10.6 54.6 %collective-permute-start.3 = (f32[64,9216]{1,0:T(8,128)S(1)}, f32[64,9216]{1,0:T(8,128)S(1)}, u32[]{:S(2)}, u32[]{:S(2)}) collective-permute-start(f32[64,9216]{1,0:T(8,128)S(1)} %rows_of.5), channel_id=1, source_target_pairs={{1,3},{2,0},{3,5},{4,2},{5,7},{6,4},{9,11},{10,8},{11,13},{12,10},... | collective-permute-start | bytes 7077896 | tf_op jit(solution)/shard_map/ppermute | solution.py:466
  17.5 49.6 %collective-permute-start.2 = (f32[3,16,9216]{2,1,0:T(8,128)}, f32[3,16,9216]{2,1,0:T(8,128)S(1)}, u32[]{:S(2)}, u32[]{:S(2)}) collective-permute-start(f32[3,16,9216]{2,1,0:T(8,128)} %head_of.1), channel_id=1, source_target_pairs={{8,0},{16,8},{24,16},{9,1},{17,9},{25,17},{10,2},{18,10},{26,18},{... | collective-permute-start | bytes 5308424 | tf_op jit(solution)/shard_map/ppermute | solution.py:466
  18.8 12.4 %copy-start.11 = (f32[16]{0:T(128)}, f32[16]{0:T(128)S(1)}, u32[]{:S(2)}) copy-start(f32[16]{0:T(128)S(1)} %get-tuple-element.233.scaled) | copy-start | bytes 196
  18.8 16.6 %copy-start.5 = (f32[3,9216]{1,0:T(4,128)S(1)}, f32[3,9216]{1,0:T(4,128)}, u32[]{:S(2)}) copy-start(f32[3,9216]{1,0:T(4,128)} %absorption.3) | copy-start | bytes 331780
  31.2 14.6 %copy-start.2 = (f32[3,16,9216]{2,1,0:T(8,128)}, f32[3,16,9216]{2,1,0:T(8,128)S(1)}, u32[]{:S(2)}) copy-start(f32[3,16,9216]{2,1,0:T(8,128)S(1)} %mode_sums.1.sums) | copy-start | bytes 5308420
  31.2 35.9 %collective-permute-start.1 = (f32[3,16,9216]{2,1,0:T(8,128)S(1)}, f32[3,16,9216]{2,1,0:T(8,128)S(1)}, u32[]{:S(2)}, u32[]{:S(2)}) collective-permute-start(f32[3,16,9216]{2,1,0:T(8,128)S(1)} %mode_sums.1.sums), channel_id=1, source_target_pairs={{8,0},{16,8},{24,16},{9,1},{17,9},{25,17},{10,2},{18,10},{26,18},{... | collective-permute-start | bytes 5308424 | tf_op jit(solution)/shard_map/ppermute | solution.py:466
  32.5 76.1 %collective-permute-start = (f32[64,9216]{1,0:T(8,128)}, f32[64,9216]{1,0:T(8,128)}, u32[]{:S(2)}, u32[]{:S(2)}) collective-permute-start(f32[64,9216]{1,0:T(8,128)} %middle_rows.3), channel_id=1, source_target_pairs={{0,1},{1,0},{2,3},{3,2},{4,5},{5,4},{6,7},{7,6},{8,9},{9,8},{10,11... | collective-permute-start | bytes 7077896 | tf_op jit(solution)/shard_map/ppermute | solution.py:466
  70.4 63.5 %collective-permute-start.7 = (f32[32,9216]{1,0:T(8,128)}, f32[32,9216]{1,0:T(8,128)}, u32[]{:S(2)}, u32[]{:S(2)}) collective-permute-start(f32[32,9216]{1,0:T(8,128)} %picked_rows.3), channel_id=1, source_target_pairs={{0,1},{1,0},{2,3},{3,2},{4,5},{5,4},{6,7},{7,6},{8,9},{9,8},{10,11... | collective-permute-start | bytes 3538952 | tf_op jit(solution)/shard_map/ppermute | solution.py:466
  71.0 62.8 %collective-permute-start.6 = (f32[32,9216]{1,0:T(8,128)}, f32[32,9216]{1,0:T(8,128)}, u32[]{:S(2)}, u32[]{:S(2)}) collective-permute-start(f32[32,9216]{1,0:T(8,128)} %rows_of.6), channel_id=1, source_target_pairs={{1,3},{2,0},{3,5},{4,2},{5,7},{6,4},{9,11},{10,8},{11,13},{12,10},... | collective-permute-start | bytes 3538952 | tf_op jit(solution)/shard_map/ppermute | solution.py:466
  72.3 112.1 %collective-permute-start.12 = (f32[64,9216]{1,0:T(8,128)S(1)}, f32[64,9216]{1,0:T(8,128)}, u32[]{:S(2)}, u32[]{:S(2)}) collective-permute-start(f32[64,9216]{1,0:T(8,128)S(1)} %collective-permute-done.4.refs_1_), channel_id=1, source_target_pairs={{0,2},{2,4},{3,1},{4,6},{5,3},{7,5},{8,10},{10,12},{11,9},{12,14},... | collective-permute-start | bytes 7077896 | tf_op jit(solution)/shard_map/ppermute | solution.py:466
  82.6 25.9 %copy-start.1 = (f32[64,9216]{1,0:T(8,128)S(1)}, f32[64,9216]{1,0:T(8,128)}, u32[]{:S(2)}) copy-start(f32[64,9216]{1,0:T(8,128)} %copy-done) | copy-start | bytes 7077892
  82.6 81.7 %collective-permute-start.10 = (f32[3,16,9216]{2,1,0:T(8,128)}, f32[3,16,9216]{2,1,0:T(8,128)S(1)}, u32[]{:S(2)}, u32[]{:S(2)}) collective-permute-start(f32[3,16,9216]{2,1,0:T(8,128)} %carried.1), channel_id=1, source_target_pairs={{16,0},{24,8},{17,1},{25,9},{18,2},{26,10},{19,3},{27,11},{20,4},{... | collective-permute-start | bytes 5308424 | tf_op jit(solution)/shard_map/ppermute | solution.py:466
  94.4 18.2 %copy-start.6 = (f32[3,9216]{1,0:T(4,128)S(1)}, f32[3,9216]{1,0:T(4,128)}, u32[]{:S(2)}) copy-start(f32[3,9216]{1,0:T(4,128)} %absorption.3) | copy-start | bytes 331780
  109.7 49.3 %collective-permute-start.5 = (f32[32,9216]{1,0:T(8,128)S(1)}, f32[32,9216]{1,0:T(8,128)S(1)}, u32[]{:S(2)}, u32[]{:S(2)}) collective-permute-start(f32[32,9216]{1,0:T(8,128)S(1)} %picked_rows.4), channel_id=1, source_target_pairs={{0,1},{1,0},{2,3},{3,2},{4,5},{5,4},{6,7},{7,6},{8,9},{9,8},{10,11... | collective-permute-start | bytes 3538952 | tf_op jit(solution)/shard_map/ppermute | solution.py:466
  135.8 48.6 %collective-permute-start.9 = (f32[32,9216]{1,0:T(8,128)S(1)}, f32[32,9216]{1,0:T(8,128)}, u32[]{:S(2)}, u32[]{:S(2)}) collective-permute-start(f32[32,9216]{1,0:T(8,128)S(1)} %picked_rows.5), channel_id=1, source_target_pairs={{0,1},{1,0},{2,3},{3,2},{4,5},{5,4},{6,7},{7,6},{8,9},{9,8},{10,11... | collective-permute-start | bytes 3538952 | tf_op jit(solution)/shard_map/ppermute | solution.py:466
  137.9 55.1 %collective-permute-start.11 = (f32[64,9216]{1,0:T(8,128)}, f32[64,9216]{1,0:T(8,128)S(1)}, u32[]{:S(2)}, u32[]{:S(2)}) collective-permute-start(f32[64,9216]{1,0:T(8,128)} %collective-permute-done.refs_1_), channel_id=1, source_target_pairs={{0,2},{2,4},{3,1},{4,6},{5,3},{7,5},{8,10},{10,12},{11,9},{12,14},... | collective-permute-start | bytes 7077896 | tf_op jit(solution)/shard_map/ppermute | solution.py:466
  162.2 79.1 %collective-permute-start.8 = (f32[72,9216]{1,0:T(8,128)}, f32[72,9216]{1,0:T(8,128)}, u32[]{:S(2)}, u32[]{:S(2)}) collective-permute-start(f32[72,9216]{1,0:T(8,128)} %rows_of.7), channel_id=1, source_target_pairs={{0,1},{1,0},{2,3},{3,2},{4,5},{5,4},{6,7},{7,6},{8,9},{9,8},{10,11... | collective-permute-start | bytes 7962632 | tf_op jit(solution)/shard_map/ppermute | solution.py:466
  184.4 67.0 %collective-permute-start.16 = (f32[64,9216]{1,0:T(8,128)}, f32[64,9216]{1,0:T(8,128)}, u32[]{:S(2)}, u32[]{:S(2)}) collective-permute-start(f32[64,9216]{1,0:T(8,128)} %joined.1), channel_id=1, source_target_pairs={{0,2},{2,4},{5,3},{7,5},{8,10},{10,12},{13,11},{15,13},{16,18},{18... | collective-permute-start | bytes 7077896 | tf_op jit(solution)/shard_map/ppermute | solution.py:466
  192.7 86.5 %collective-permute-start.14 = (f32[48,9216]{1,0:T(8,128)}, f32[48,9216]{1,0:T(8,128)}, u32[]{:S(2)}, u32[]{:S(2)}) collective-permute-start(f32[48,9216]{1,0:T(8,128)} %rows_of.8), channel_id=1, source_target_pairs={{0,1},{1,0},{2,3},{3,2},{4,5},{5,4},{6,7},{7,6},{8,9},{9,8},{10,11... | collective-permute-start | bytes 5308424 | tf_op jit(solution)/shard_map/ppermute | solution.py:466
  193.0 72.7 %collective-permute-start.15 = (f32[32,9216]{1,0:T(8,128)}, f32[32,9216]{1,0:T(8,128)S(1)}, u32[]{:S(2)}, u32[]{:S(2)}) collective-permute-start(f32[32,9216]{1,0:T(8,128)} %collective-permute-done.9.refs_3_), channel_id=1, source_target_pairs={{0,2},{2,4},{3,1},{4,6},{5,3},{7,5},{8,10},{10,12},{11,9},{12,14},... | collective-permute-start | bytes 3538952 | tf_op jit(solution)/shard_map/ppermute | solution.py:466
  242.9 41.7 %collective-permute-start.13 = (f32[8,9216]{1,0:T(8,128)S(1)}, f32[8,9216]{1,0:T(8,128)S(1)}, u32[]{:S(2)}, u32[]{:S(2)}) collective-permute-start(f32[8,9216]{1,0:T(8,128)S(1)} %rows_of.9), channel_id=1, source_target_pairs={{0,1},{1,0},{2,3},{3,2},{4,5},{5,4},{6,7},{7,6},{8,9},{9,8},{10,11... | collective-permute-start | bytes 884744 | tf_op jit(solution)/shard_map/ppermute | solution.py:466
  270.3 14.3 %copy-start.14 = (f32[16]{0:T(128)S(1)}, f32[16]{0:T(128)}, u32[]{:S(2)}) copy-start(f32[16]{0:T(128)} %refs_3_) | copy-start | bytes 196
  (9 other events, 41.5 us)

commit v4 on v3

--- a/solution.py
+++ b/solution.py
@@ -212,6 +212,19 @@
     )(*device, *arrays)
 
 
+def place_of(me, slabs, depth):
+    odd = me % 2
+    half = me // 2
+    back = slabs // 2 - 1 - half
+    return [
+        jnp.where(odd == 0, 0, depth - 1),
+        jnp.where(odd == 0, depth - 1, 0),
+        jnp.where(odd == 0, depth - 2, 1),
+        jnp.where(odd == 0, half, back),
+        jnp.where(odd == 1, half, back),
+    ]
+
+
 def rows_kernel(which, lo, device, field, out, held, sems):
     copy_rows(field.at[device[which], pl.ds(lo, out.shape[0])], out, held, sems)
 
@@ -323,9 +336,9 @@
 
 def update_kernel(change, planes_of, count, start, *refs):
     pieces = count // ROWS
-    device, refs = refs[0], refs[1:]
     arrays, (image, held, came, in_sems, came_sems, out_sems) = refs[:-6], refs[-6:]
     beside, before = arrays[: len(change.firsts)], arrays[len(change.firsts)]
+    device = place_of(lax.axis_index("space"), lax.axis_size("space"), image.shape[0])
     planes = planes_of(device)
 
     def held_copy(p, k, out):
@@ -367,13 +380,13 @@
         return self.change(device, beside)
 
 
-def update(name, change, planes_of, plane_count, device, arrays, image, start, count, token=()):
+def update(name, change, planes_of, plane_count, arrays, image, start, count, token=()):
     plane = image.shape[-1]
     pieces = count // ROWS
     in_any = pl.BlockSpec(memory_space=pl.ANY)
     return pl.pallas_call(
         functools.partial(update_kernel, Change(change, [row for _, row in arrays]), planes_of, count, start),
-        in_specs=[pl.BlockSpec(memory_space=pltpu.SMEM)] + [in_any] * (len(arrays) + 1 + len(token)),
+        in_specs=[in_any] * (len(arrays) + 1 + len(token)),
         out_specs=in_any,
         out_shape=jax.ShapeDtypeStruct(image.shape, jnp.float32),
         scratch_shapes=[
@@ -383,14 +396,14 @@
             pltpu.SemaphoreType.DMA((len(arrays), pieces)),
             pltpu.SemaphoreType.DMA((plane_count, pieces)),
         ],
-        input_output_aliases={1 + len(arrays): 0},
+        input_output_aliases={len(arrays): 0},
         compiler_params=pltpu.CompilerParams(vmem_limit_bytes=VMEM_LIMIT),
         cost_estimate=SHORT,
         name=name,
-    )(device, *[array for array, _ in arrays], image, *token)
-
-
-def add_halo(device, near, out_side, over_y, over_z, image, last, start, end):
+    )(*[array for array, _ in arrays], image, *token)
+
+
+def add_halo(near, out_side, over_y, over_z, image, last, start, end):
 
     def change(device, beside):
         near, out_side, over_y, over_z = beside
@@ -401,10 +414,10 @@
         return device[OUTER], device[MIDDLE], device[INNER]
 
     arrays = (near, out_side, over_y, over_z)
-    return update("add_halo", change, planes_of, 3, device, arrays, image, start, end - start)
-
-
-def add_inner(device, beside, image, start, token):
+    return update("add_halo", change, planes_of, 3, arrays, image, start, end - start)
+
+
+def add_inner(beside, image, start, token):
 
     def change(device, beside):
         return NEAR * beside[0], FAR * beside[0]
@@ -412,7 +425,7 @@
     def planes_of(device):
         return device[INNER], device[MIDDLE]
 
-    return update("add_inner", change, planes_of, 2, device, [(beside, 0)], image, start, beside.shape[0], token)
+    return update("add_inner", change, planes_of, 2, [(beside, 0)], image, start, beside.shape[0], token)
 
 
 def cuts(steps, pieces):
@@ -435,7 +448,6 @@
     slabs = lax.axis_size("space")
     pairs = slabs // 2
     me = lax.axis_index("space")
-    odd = me % 2
     field = adjoint_field.transpose(1, 0, 2)
     order = Order(mode_rates)
 
@@ -452,15 +464,7 @@
     def rank(i):
         return i // 2 if i % 2 == 0 else pairs - 1 - i // 2
 
-    device = jnp.stack(
-        [
-            jnp.where(odd == 0, 0, depth - 1),
-            jnp.where(odd == 0, depth - 1, 0),
-            jnp.where(odd == 0, depth - 2, 1),
-            jnp.where(odd == 0, me // 2, pairs - 1 - me // 2),
-            jnp.where(odd == 1, me // 2, pairs - 1 - me // 2),
-        ]
-    ).astype(jnp.int32)
+    device = jnp.stack(place_of(me, slabs, depth)).astype(jnp.int32)
 
     def send(value, axis, route):
         return lax.ppermute(order(value), axis, route)
@@ -555,7 +559,7 @@
             a, b = max(lo, start), min(hi, end)
             if a < b:
                 image = add_halo(
-                    order(device), (y_mid[k], a - start), (z_mid[k], a - start), (over_y[0], a - lo),
+                    (y_mid[k], a - start), (z_mid[k], a - start), (over_y[0], a - lo),
                     (over_z, at_z + a - lo), image, slots - q, a, b,
                 )
         return order(image)
@@ -563,7 +567,7 @@
     y_out = []
     def inner(k, image):
         token = [order.token] if k == len(in_cuts) - 1 else []
-        return order(add_inner(order(device), y_in[k], image, in_cuts[k][0], token))
+        return order(add_inner(y_in[k], image, in_cuts[k][0], token))
 
     for j in range(slots):
         y_out.append(order(sent[2 + j]))

time: 289 us -> 288 us (level)
  Pallas kernels: 147 us -> 144 us
    pallas_call x7, Pallas kernels: 34.5 us -> 31.3 us  [update(): pl.pallas_call(functools.partial(update_kernel, Change(change, [row for _...]
where the time goes in v4:
time: 288 us; the launch traced here: 287 us
  Pallas kernels  144 us (50%)
  waiting for transfers between devices  99.3 us (34%)
  starting transfers between devices  42.1 us (15%)
    ppermute x17, waiting for transfers between devices, send(): return lax.ppermute(order(value), axis, route)  99.3 us
    ppermute x17, starting transfers between devices, send(): return lax.ppermute(order(value), axis, route)  42.1 us
    pallas_call x4, Pallas kernels, plane_terms(): pl.pallas_call(functools.partial(plane_kernel, depth, shifts), grid=((end...  41.5 us
    pallas_call x12, Pallas kernels, staged(): pl.pallas_call(kernel, in_specs=[pl.BlockSpec(memory_space=pltpu.SMEM)] *...  32.7 us
    pallas_call x7, Pallas kernels, update(): pl.pallas_call(functools.partial(update_kernel, Change(change, [row for _...  31.3 us
    pallas_call x1, Pallas kernels, add_history(): pl.pallas_call(functools.partial(history_kernel, aways), grid=(depth, pla...  21.9 us
    pallas_call x1, Pallas kernels, mode_sums(): pl.pallas_call(sums_kernel, grid=(depth, plane // tile), in_specs=[pl.Blo...  12.3 us
  transfers between devices with their start and end apart: 17, of which 11 were waited for; matrix products, arithmetic and copies ran while one was open for 0% of the time, Pallas kernels for 49%

profile of v4, /device:TPU:0, one launch (start us, length us, event | category | flops | bytes accessed | tf_op | source)
XLA Modules:
  0.0 286.7 jit_solution(13275690621102708707)
XLA Ops:
  11.9 5.6 %head_of.1 = f32[3,16,9216]{2,1,0:T(8,128)} custom-call(f32[3,128,9216]{2,1,0:T(8,128)} %bitcast.13), custom_call_target="tpu_custom_call" | custom-call | flops 1 | bytes 1 | tf_op jit(solution)/shard_map/head_of/pallas_call | solution.py:199
  18.8 12.3 %mode_sums.1.sums = f32[3,16,9216]{2,1,0:T(8,128)S(1)} custom-call(f32[16]{0:T(128)S(1)} %get-tuple-element.219.scaled, f32[3,128,9216]{2,1,0:T(8,128)} %bitcast.14), custom_call_target="tpu_custom_call" | custom-call | flops 1 | bytes 1 | tf_op jit(solution)/shard_map/mode_sums/pallas_call | solution.py:67
  35.4 10.4 %plane_terms.4.refs_0_ = f32[3,128,9216]{2,1,0:T(8,128)} custom-call(f32[3,9216]{1,0:T(4,128)S(1)} %copy-done.5, f32[3,128,9216]{2,1,0:T(8,128)} %bitcast.15), custom_call_target="tpu_custom_call" | custom-call | flops 1 | bytes 1 | tf_op jit(solution)/shard_map/plane_terms/pallas_call | solution.py:323
  45.8 12.1 %collective-permute-done.4.refs_0_ = f32[64,9216]{1,0:T(8,128)S(1)} collective-permute-done((f32[64,9216]{1,0:T(8,128)}, f32[64,9216]{1,0:T(8,128)S(1)}, u32[]{:S(2)}, u32[]{:S(2)}) %collective-permute-start.4) | collective-permute-done | bytes 2359328 | tf_op jit(solution)/shard_map/ppermute | solution.py:470
  57.9 7.3 %collective-permute-done.3.relayed = f32[64,9216]{1,0:T(8,128)S(1)} collective-permute-done((f32[64,9216]{1,0:T(8,128)S(1)}, f32[64,9216]{1,0:T(8,128)S(1)}, u32[]{:S(2)}, u32[]{:S(2)}) %collective-permute-start.3) | collective-permute-done | bytes 2359328 | tf_op jit(solution)/shard_map/ppermute | solution.py:470
  72.3 6.0 %collective-permute-start.9 = (f32[64,9216]{1,0:T(8,128)S(1)}, f32[64,9216]{1,0:T(8,128)}, u32[]{:S(2)}, u32[]{:S(2)}) collective-permute-start(f32[64,9216]{1,0:T(8,128)S(1)} %collective-permute-done.4.refs_0_), channel_id=1, source_target_pairs={{0,2},{2,4},{3,1},{4,6},{5,3},{7,5},{8,10},{10,12},{11,9},{12,14},... | collective-permute-start | bytes 7077896 | tf_op jit(solution)/shard_map/ppermute | solution.py:470
  84.0 10.4 %plane_terms.5.refs_0_ = f32[3,128,9216]{2,1,0:T(8,128)} custom-call(f32[3,9216]{1,0:T(4,128)S(1)} %copy-done.5, f32[3,128,9216]{2,1,0:T(8,128)} %bitcast.18, f32[3,128,9216]{2,1,0:T(8,128)} %plane_terms.4.refs_0_), custom_call_target="tpu_custom_call", output_to_operand_aliasing={{}: (2, {})} | custom-call | flops 1 | bytes 1 | tf_op jit(solution)/shard_map/plane_terms/pallas_call | solution.py:323
  94.4 14.1 %collective-permute-done.refs_0_ = f32[64,9216]{1,0:T(8,128)} collective-permute-done((f32[64,9216]{1,0:T(8,128)}, f32[64,9216]{1,0:T(8,128)}, u32[]{:S(2)}, u32[]{:S(2)}) %collective-permute-start) | collective-permute-done | bytes 2359328 | tf_op jit(solution)/shard_map/ppermute | solution.py:470
  112.6 10.4 %plane_terms.6.refs_0_ = f32[3,128,9216]{2,1,0:T(8,128)} custom-call(f32[3,9216]{1,0:T(4,128)S(1)} %copy-done.6, f32[3,128,9216]{2,1,0:T(8,128)} %bitcast.20, f32[3,128,9216]{2,1,0:T(8,128)} %plane_terms.5.refs_0_), custom_call_target="tpu_custom_call", output_to_operand_aliasing={{}: (2, {})} | custom-call | flops 1 | bytes 1 | tf_op jit(solution)/shard_map/plane_terms/pallas_call | solution.py:323
  123.0 10.9 %collective-permute-done.7.refs_2_.refs_0_ = f32[32,9216]{1,0:T(8,128)} collective-permute-done((f32[32,9216]{1,0:T(8,128)}, f32[32,9216]{1,0:T(8,128)}, u32[]{:S(2)}, u32[]{:S(2)}) %collective-permute-start.7) | collective-permute-done | bytes 1179680 | tf_op jit(solution)/shard_map/ppermute | solution.py:470
  141.7 10.4 %plane_terms.7.refs_4_ = f32[3,128,9216]{2,1,0:T(8,128)} custom-call(f32[3,9216]{1,0:T(4,128)S(1)} %copy-done.6, f32[3,128,9216]{2,1,0:T(8,128)} %bitcast.22, f32[3,128,9216]{2,1,0:T(8,128)} %plane_terms.6.refs_0_), custom_call_target="tpu_custom_call", output_to_operand_aliasing={{}: (2, {})} | custom-call | flops 1 | bytes 1 | tf_op jit(solution)/shard_map/plane_terms/pallas_call | solution.py:323
  152.1 6.9 %collective-permute-done.5.refs_1_.refs_2_ = f32[32,9216]{1,0:T(8,128)S(1)} collective-permute-done((f32[32,9216]{1,0:T(8,128)S(1)}, f32[32,9216]{1,0:T(8,128)S(1)}, u32[]{:S(2)}, u32[]{:S(2)}) %collective-permute-start.5) | collective-permute-done | bytes 1179680 | tf_op jit(solution)/shard_map/ppermute | solution.py:470
  168.3 16.1 %collective-permute-done.10.refs_2_ = f32[32,9216]{1,0:T(8,128)} collective-permute-done((f32[32,9216]{1,0:T(8,128)S(1)}, f32[32,9216]{1,0:T(8,128)}, u32[]{:S(2)}, u32[]{:S(2)}) %collective-permute-start.10) | collective-permute-done | bytes 1179680 | tf_op jit(solution)/shard_map/ppermute | solution.py:470
  184.4 5.4 %collective-permute-start.16 = (f32[64,9216]{1,0:T(8,128)}, f32[64,9216]{1,0:T(8,128)}, u32[]{:S(2)}, u32[]{:S(2)}) collective-permute-start(f32[64,9216]{1,0:T(8,128)} %joined.1), channel_id=1, source_target_pairs={{0,2},{2,4},{5,3},{7,5},{8,10},{10,12},{13,11},{15,13},{16,18},{18... | collective-permute-start | bytes 7077896 | tf_op jit(solution)/shard_map/ppermute | solution.py:470
  193.0 4.3 %collective-permute-start.15 = (f32[32,9216]{1,0:T(8,128)}, f32[32,9216]{1,0:T(8,128)S(1)}, u32[]{:S(2)}, u32[]{:S(2)}) collective-permute-start(f32[32,9216]{1,0:T(8,128)} %collective-permute-done.10.refs_2_), channel_id=1, source_target_pairs={{0,2},{2,4},{3,1},{4,6},{5,3},{7,5},{8,10},{10,12},{11,9},{12,14},... | collective-permute-start | bytes 3538952 | tf_op jit(solution)/shard_map/ppermute | solution.py:470
  197.5 5.1 %add_halo.4.refs_3_ = f32[3,128,9216]{2,1,0:T(8,128)} custom-call(f32[64,9216]{1,0:T(8,128)S(1)} %collective-permute-done.4.refs_0_, f32[64,9216]{1,0:T(8,128)} %collective-permute-done.9.refs_1_, f32[32,9216]{1,0:T(8,128)} %collective-permute-done.7.refs_2_.refs_0_, f32[32,9216]{1,0:T(8,128)S(1)} %broadcast_in_dim.9.refs_3_, ...), custom_call_target="tpu_custom_call", output_to_operand_aliasing={{}: (4, {})} | custom-call | flops 1 | bytes 1 | tf_op jit(solution)/shard_map/add_halo/pallas_call | solution.py:387
  203.1 21.9 %add_history.1.refs_1_ = f32[3,128,9216]{2,1,0:T(8,128)} custom-call(f32[16]{0:T(128)S(1)} %copy-done.12, f32[16]{0:T(128)S(1)} %get-tuple-element.255.mode_gain, f32[1,16]{1,0:T(1,128)S(1)} %bitcast.8, f32[1,16]{1,0:T(1,128)S(1)} %bitcast.9, f32[3,128,9216]{2,1,0:T(8,128)} %bitcast.25, ...), custom_call_target="tpu_custom_call", output_to_operand_aliasing={{}: (8, {})} | custom-call | flops 1 | bytes 1 | tf_op jit(solution)/shard_map/add_history/pallas_call | solution.py:161
  224.9 16.3 %collective-permute-done.8.refs_0_ = f32[72,9216]{1,0:T(8,128)} collective-permute-done((f32[72,9216]{1,0:T(8,128)}, f32[72,9216]{1,0:T(8,128)}, u32[]{:S(2)}, u32[]{:S(2)}) %collective-permute-start.8) | collective-permute-done | bytes 2654240 | tf_op jit(solution)/shard_map/ppermute | solution.py:470
  245.0 6.0 %add_inner.3.refs_4_ = f32[3,128,9216]{2,1,0:T(8,128)} custom-call(f32[72,9216]{1,0:T(8,128)} %collective-permute-done.8.refs_0_, f32[3,128,9216]{2,1,0:T(8,128)} %add_history.1.refs_1_), custom_call_target="tpu_custom_call", output_to_operand_aliasing={{}: (1, {})} | custom-call | flops 1 | bytes 1 | tf_op jit(solution)/shard_map/add_inner/pallas_call | solution.py:387
  251.0 4.9 %add_halo.5.refs_4_ = f32[3,128,9216]{2,1,0:T(8,128)} custom-call(f32[64,9216]{1,0:T(8,128)S(1)} %collective-permute-done.4.refs_0_, f32[64,9216]{1,0:T(8,128)} %collective-permute-done.9.refs_1_, f32[32,9216]{1,0:T(8,128)S(1)} %collective-permute-done.5.refs_1_.refs_2_, f32[64,9216]{1,0:T(8,128)} %collective-permute-done.16.refs_3_, ...), custom_call_target="tpu_custom_call", output_to_operand_aliasing={{}: (4, {})} | custom-call | flops 1 | bytes 1 | tf_op jit(solution)/shard_map/add_halo/pallas_call | solution.py:387
  255.9 5.0 %add_halo.6.refs_4_ = f32[3,128,9216]{2,1,0:T(8,128)} custom-call(f32[64,9216]{1,0:T(8,128)} %collective-permute-done.refs_0_, f32[64,9216]{1,0:T(8,128)S(1)} %collective-permute-done.12.refs_1_, f32[32,9216]{1,0:T(8,128)} %collective-permute-done.10.refs_2_, f32[64,9216]{1,0:T(8,128)} %collective-permute-done.16.refs_3_, ...), custom_call_target="tpu_custom_call", output_to_operand_aliasing={{}: (4, {})} | custom-call | flops 1 | bytes 1 | tf_op jit(solution)/shard_map/add_halo/pallas_call | solution.py:387
  260.9 4.8 %collective-permute-done.15.refs_2_.refs_3_ = f32[32,9216]{1,0:T(8,128)S(1)} collective-permute-done((f32[32,9216]{1,0:T(8,128)}, f32[32,9216]{1,0:T(8,128)S(1)}, u32[]{:S(2)}, u32[]{:S(2)}) %collective-permute-start.15) | collective-permute-done | bytes 1179680 | tf_op jit(solution)/shard_map/ppermute | solution.py:470
  269.8 9.4 %collective-permute-done.14.refs_0_ = f32[48,9216]{1,0:T(8,128)} collective-permute-done((f32[48,9216]{1,0:T(8,128)}, f32[48,9216]{1,0:T(8,128)}, u32[]{:S(2)}, u32[]{:S(2)}) %collective-permute-start.14) | collective-permute-done | bytes 1769504 | tf_op jit(solution)/shard_map/ppermute | solution.py:470
  279.2 4.3 %add_inner.4.refs_1_ = f32[3,128,9216]{2,1,0:T(8,128)} custom-call(f32[48,9216]{1,0:T(8,128)} %collective-permute-done.14.refs_0_, f32[3,128,9216]{2,1,0:T(8,128)} %add_halo.7.refs_1_), custom_call_target="tpu_custom_call", output_to_operand_aliasing={{}: (1, {})} | custom-call | flops 1 | bytes 1 | tf_op jit(solution)/shard_map/add_inner/pallas_call | solution.py:387
  (71 shorter events, 65.8 us)
Async XLA Ops:
  2.6 55.3 %collective-permute-start.4 = (f32[64,9216]{1,0:T(8,128)}, f32[64,9216]{1,0:T(8,128)S(1)}, u32[]{:S(2)}, u32[]{:S(2)}) collective-permute-start(f32[64,9216]{1,0:T(8,128)} %middle_rows.2), channel_id=1, source_target_pairs={{0,1},{1,0},{2,3},{3,2},{4,5},{5,4},{6,7},{7,6},{8,9},{9,8},{10,11... | collective-permute-start | bytes 7077896 | tf_op jit(solution)/shard_map/ppermute | solution.py:470
  10.6 8.2 %copy-start.15 = (f32[16]{0:T(128)S(1)}, f32[16]{0:T(128)}, u32[]{:S(2)}) copy-start(f32[16]{0:T(128)} %param.7) | copy-start | bytes 196
  10.6 54.6 %collective-permute-start.3 = (f32[64,9216]{1,0:T(8,128)S(1)}, f32[64,9216]{1,0:T(8,128)S(1)}, u32[]{:S(2)}, u32[]{:S(2)}) collective-permute-start(f32[64,9216]{1,0:T(8,128)S(1)} %rows_of.5), channel_id=1, source_target_pairs={{1,3},{2,0},{3,5},{4,2},{5,7},{6,4},{9,11},{10,8},{11,13},{12,10},... | collective-permute-start | bytes 7077896 | tf_op jit(solution)/shard_map/ppermute | solution.py:470
  17.5 49.6 %collective-permute-start.2 = (f32[3,16,9216]{2,1,0:T(8,128)}, f32[3,16,9216]{2,1,0:T(8,128)S(1)}, u32[]{:S(2)}, u32[]{:S(2)}) collective-permute-start(f32[3,16,9216]{2,1,0:T(8,128)} %head_of.1), channel_id=1, source_target_pairs={{8,0},{16,8},{24,16},{9,1},{17,9},{25,17},{10,2},{18,10},{26,18},{... | collective-permute-start | bytes 5308424 | tf_op jit(solution)/shard_map/ppermute | solution.py:470
  18.8 12.4 %copy-start.11 = (f32[16]{0:T(128)}, f32[16]{0:T(128)S(1)}, u32[]{:S(2)}) copy-start(f32[16]{0:T(128)S(1)} %get-tuple-element.219.scaled) | copy-start | bytes 196
  18.8 16.6 %copy-start.5 = (f32[3,9216]{1,0:T(4,128)S(1)}, f32[3,9216]{1,0:T(4,128)}, u32[]{:S(2)}) copy-start(f32[3,9216]{1,0:T(4,128)} %absorption.3) | copy-start | bytes 331780
  31.2 14.6 %copy-start.2 = (f32[3,16,9216]{2,1,0:T(8,128)}, f32[3,16,9216]{2,1,0:T(8,128)S(1)}, u32[]{:S(2)}) copy-start(f32[3,16,9216]{2,1,0:T(8,128)S(1)} %mode_sums.1.sums) | copy-start | bytes 5308420
  31.2 35.9 %collective-permute-start.1 = (f32[3,16,9216]{2,1,0:T(8,128)S(1)}, f32[3,16,9216]{2,1,0:T(8,128)S(1)}, u32[]{:S(2)}, u32[]{:S(2)}) collective-permute-start(f32[3,16,9216]{2,1,0:T(8,128)S(1)} %mode_sums.1.sums), channel_id=1, source_target_pairs={{8,0},{16,8},{24,16},{9,1},{17,9},{25,17},{10,2},{18,10},{26,18},{... | collective-permute-start | bytes 5308424 | tf_op jit(solution)/shard_map/ppermute | solution.py:470
  32.5 76.1 %collective-permute-start = (f32[64,9216]{1,0:T(8,128)}, f32[64,9216]{1,0:T(8,128)}, u32[]{:S(2)}, u32[]{:S(2)}) collective-permute-start(f32[64,9216]{1,0:T(8,128)} %middle_rows.3), channel_id=1, source_target_pairs={{0,1},{1,0},{2,3},{3,2},{4,5},{5,4},{6,7},{7,6},{8,9},{9,8},{10,11... | collective-permute-start | bytes 7077896 | tf_op jit(solution)/shard_map/ppermute | solution.py:470
  70.4 63.5 %collective-permute-start.7 = (f32[32,9216]{1,0:T(8,128)}, f32[32,9216]{1,0:T(8,128)}, u32[]{:S(2)}, u32[]{:S(2)}) collective-permute-start(f32[32,9216]{1,0:T(8,128)} %picked_rows.3), channel_id=1, source_target_pairs={{0,1},{1,0},{2,3},{3,2},{4,5},{5,4},{6,7},{7,6},{8,9},{9,8},{10,11... | collective-permute-start | bytes 3538952 | tf_op jit(solution)/shard_map/ppermute | solution.py:470
  71.0 62.8 %collective-permute-start.6 = (f32[32,9216]{1,0:T(8,128)}, f32[32,9216]{1,0:T(8,128)}, u32[]{:S(2)}, u32[]{:S(2)}) collective-permute-start(f32[32,9216]{1,0:T(8,128)} %rows_of.6), channel_id=1, source_target_pairs={{1,3},{2,0},{3,5},{4,2},{5,7},{6,4},{9,11},{10,8},{11,13},{12,10},... | collective-permute-start | bytes 3538952 | tf_op jit(solution)/shard_map/ppermute | solution.py:470
  72.3 112.1 %collective-permute-start.9 = (f32[64,9216]{1,0:T(8,128)S(1)}, f32[64,9216]{1,0:T(8,128)}, u32[]{:S(2)}, u32[]{:S(2)}) collective-permute-start(f32[64,9216]{1,0:T(8,128)S(1)} %collective-permute-done.4.refs_0_), channel_id=1, source_target_pairs={{0,2},{2,4},{3,1},{4,6},{5,3},{7,5},{8,10},{10,12},{11,9},{12,14},... | collective-permute-start | bytes 7077896 | tf_op jit(solution)/shard_map/ppermute | solution.py:470
  82.6 25.9 %copy-start.1 = (f32[64,9216]{1,0:T(8,128)S(1)}, f32[64,9216]{1,0:T(8,128)}, u32[]{:S(2)}) copy-start(f32[64,9216]{1,0:T(8,128)} %copy-done) | copy-start | bytes 7077892
  82.6 81.7 %collective-permute-start.11 = (f32[3,16,9216]{2,1,0:T(8,128)}, f32[3,16,9216]{2,1,0:T(8,128)S(1)}, u32[]{:S(2)}, u32[]{:S(2)}) collective-permute-start(f32[3,16,9216]{2,1,0:T(8,128)} %carried.1), channel_id=1, source_target_pairs={{16,0},{24,8},{17,1},{25,9},{18,2},{26,10},{19,3},{27,11},{20,4},{... | collective-permute-start | bytes 5308424 | tf_op jit(solution)/shard_map/ppermute | solution.py:470
  94.4 18.2 %copy-start.6 = (f32[3,9216]{1,0:T(4,128)S(1)}, f32[3,9216]{1,0:T(4,128)}, u32[]{:S(2)}) copy-start(f32[3,9216]{1,0:T(4,128)} %absorption.3) | copy-start | bytes 331780
  109.7 49.3 %collective-permute-start.5 = (f32[32,9216]{1,0:T(8,128)S(1)}, f32[32,9216]{1,0:T(8,128)S(1)}, u32[]{:S(2)}, u32[]{:S(2)}) collective-permute-start(f32[32,9216]{1,0:T(8,128)S(1)} %picked_rows.4), channel_id=1, source_target_pairs={{0,1},{1,0},{2,3},{3,2},{4,5},{5,4},{6,7},{7,6},{8,9},{9,8},{10,11... | collective-permute-start | bytes 3538952 | tf_op jit(solution)/shard_map/ppermute | solution.py:470
  135.8 48.6 %collective-permute-start.10 = (f32[32,9216]{1,0:T(8,128)S(1)}, f32[32,9216]{1,0:T(8,128)}, u32[]{:S(2)}, u32[]{:S(2)}) collective-permute-start(f32[32,9216]{1,0:T(8,128)S(1)} %picked_rows.5), channel_id=1, source_target_pairs={{0,1},{1,0},{2,3},{3,2},{4,5},{5,4},{6,7},{7,6},{8,9},{9,8},{10,11... | collective-permute-start | bytes 3538952 | tf_op jit(solution)/shard_map/ppermute | solution.py:470
  137.9 55.1 %collective-permute-start.12 = (f32[64,9216]{1,0:T(8,128)}, f32[64,9216]{1,0:T(8,128)S(1)}, u32[]{:S(2)}, u32[]{:S(2)}) collective-permute-start(f32[64,9216]{1,0:T(8,128)} %collective-permute-done.refs_0_), channel_id=1, source_target_pairs={{0,2},{2,4},{3,1},{4,6},{5,3},{7,5},{8,10},{10,12},{11,9},{12,14},... | collective-permute-start | bytes 7077896 | tf_op jit(solution)/shard_map/ppermute | solution.py:470
  162.2 79.1 %collective-permute-start.8 = (f32[72,9216]{1,0:T(8,128)}, f32[72,9216]{1,0:T(8,128)}, u32[]{:S(2)}, u32[]{:S(2)}) collective-permute-start(f32[72,9216]{1,0:T(8,128)} %rows_of.7), channel_id=1, source_target_pairs={{0,1},{1,0},{2,3},{3,2},{4,5},{5,4},{6,7},{7,6},{8,9},{9,8},{10,11... | collective-permute-start | bytes 7962632 | tf_op jit(solution)/shard_map/ppermute | solution.py:470
  184.4 66.6 %collective-permute-start.16 = (f32[64,9216]{1,0:T(8,128)}, f32[64,9216]{1,0:T(8,128)}, u32[]{:S(2)}, u32[]{:S(2)}) collective-permute-start(f32[64,9216]{1,0:T(8,128)} %joined.1), channel_id=1, source_target_pairs={{0,2},{2,4},{5,3},{7,5},{8,10},{10,12},{13,11},{15,13},{16,18},{18... | collective-permute-start | bytes 7077896 | tf_op jit(solution)/shard_map/ppermute | solution.py:470
  192.7 86.5 %collective-permute-start.14 = (f32[48,9216]{1,0:T(8,128)}, f32[48,9216]{1,0:T(8,128)}, u32[]{:S(2)}, u32[]{:S(2)}) collective-permute-start(f32[48,9216]{1,0:T(8,128)} %rows_of.8), channel_id=1, source_target_pairs={{0,1},{1,0},{2,3},{3,2},{4,5},{5,4},{6,7},{7,6},{8,9},{9,8},{10,11... | collective-permute-start | bytes 5308424 | tf_op jit(solution)/shard_map/ppermute | solution.py:470
  193.0 72.7 %collective-permute-start.15 = (f32[32,9216]{1,0:T(8,128)}, f32[32,9216]{1,0:T(8,128)S(1)}, u32[]{:S(2)}, u32[]{:S(2)}) collective-permute-start(f32[32,9216]{1,0:T(8,128)} %collective-permute-done.10.refs_2_), channel_id=1, source_target_pairs={{0,2},{2,4},{3,1},{4,6},{5,3},{7,5},{8,10},{10,12},{11,9},{12,14},... | collective-permute-start | bytes 3538952 | tf_op jit(solution)/shard_map/ppermute | solution.py:470
  242.9 41.7 %collective-permute-start.13 = (f32[8,9216]{1,0:T(8,128)S(1)}, f32[8,9216]{1,0:T(8,128)S(1)}, u32[]{:S(2)}, u32[]{:S(2)}) collective-permute-start(f32[8,9216]{1,0:T(8,128)S(1)} %rows_of.9), channel_id=1, source_target_pairs={{0,1},{1,0},{2,3},{3,2},{4,5},{5,4},{6,7},{7,6},{8,9},{9,8},{10,11... | collective-permute-start | bytes 884744 | tf_op jit(solution)/shard_map/ppermute | solution.py:470
  269.8 14.8 %copy-start.14 = (f32[16]{0:T(128)S(1)}, f32[16]{0:T(128)}, u32[]{:S(2)}) copy-start(f32[16]{0:T(128)} %refs_2_) | copy-start | bytes 196
  (9 other events, 39.4 us)

commit v5 on v4

--- a/solution.py
+++ b/solution.py
@@ -336,8 +336,7 @@
 
 def update_kernel(change, planes_of, count, start, *refs):
     pieces = count // ROWS
-    arrays, (image, held, came, in_sems, came_sems, out_sems) = refs[:-6], refs[-6:]
-    beside, before = arrays[: len(change.firsts)], arrays[len(change.firsts)]
+    beside, (before, image, held, came, in_sems, came_sems, out_sems) = refs[:-7], refs[-7:]
     device = place_of(lax.axis_index("space"), lax.axis_size("space"), image.shape[0])
     planes = planes_of(device)
 
@@ -380,13 +379,13 @@
         return self.change(device, beside)
 
 
-def update(name, change, planes_of, plane_count, arrays, image, start, count, token=()):
+def update(name, change, planes_of, plane_count, arrays, image, start, count):
     plane = image.shape[-1]
     pieces = count // ROWS
     in_any = pl.BlockSpec(memory_space=pl.ANY)
     return pl.pallas_call(
         functools.partial(update_kernel, Change(change, [row for _, row in arrays]), planes_of, count, start),
-        in_specs=[in_any] * (len(arrays) + 1 + len(token)),
+        in_specs=[in_any] * (len(arrays) + 1),
         out_specs=in_any,
         out_shape=jax.ShapeDtypeStruct(image.shape, jnp.float32),
         scratch_shapes=[
@@ -400,7 +399,7 @@
         compiler_params=pltpu.CompilerParams(vmem_limit_bytes=VMEM_LIMIT),
         cost_estimate=SHORT,
         name=name,
-    )(*[array for array, _ in arrays], image, *token)
+    )(*[array for array, _ in arrays], image)
 
 
 def add_halo(near, out_side, over_y, over_z, image, last, start, end):
@@ -417,7 +416,7 @@
     return update("add_halo", change, planes_of, 3, arrays, image, start, end - start)
 
 
-def add_inner(beside, image, start, token):
+def add_inner(beside, image, start):
 
     def change(device, beside):
         return NEAR * beside[0], FAR * beside[0]
@@ -425,7 +424,71 @@
     def planes_of(device):
         return device[INNER], device[MIDDLE]
 
-    return update("add_inner", change, planes_of, 2, [(beside, 0)], image, start, beside.shape[0], token)
+    return update("add_inner", change, planes_of, 2, [(beside, 0)], image, start, beside.shape[0])
+
+
+def ahead_kernel(start, image, out, sems):
+    depth = image.shape[0]
+    place = place_of(lax.axis_index("space"), lax.axis_size("space"), depth)
+    copies = [
+        pltpu.make_async_copy(image.at[plane, pl.ds(start, out.shape[1])], out.at[p], sems.at[p])
+        for p, plane in enumerate((place[INNER], place[MIDDLE]))
+    ]
+    for copy in copies:
+        copy.start()
+    for copy in copies:
+        copy.wait()
+
+
+def rows_ahead(image, start):
+    _, steps, plane = image.shape
+    shape = (2, steps - start, plane)
+    return pl.pallas_call(
+        functools.partial(ahead_kernel, start),
+        in_specs=[pl.BlockSpec(memory_space=pl.ANY)],
+        out_specs=pl.BlockSpec(memory_space=pltpu.VMEM),
+        out_shape=pltpu.VMEM(shape, jnp.float32),
+        scratch_shapes=[pltpu.SemaphoreType.DMA((2,))],
+        compiler_params=pltpu.CompilerParams(vmem_limit_bytes=VMEM_LIMIT),
+        cost_estimate=SHORT,
+        name="rows_ahead",
+    )(image)
+
+
+def last_kernel(start, parts, beside, ahead, image, token, out, held, sems):
+    depth, _, plane = out.shape
+    place = place_of(lax.axis_index("space"), lax.axis_size("space"), depth)
+    width = plane // parts
+    copies = []
+    for c in range(parts):
+        at = pl.ds(c * width, width)
+        for p, (row, weight) in enumerate(((place[INNER], NEAR), (place[MIDDLE], FAR))):
+            held[p, :, at] = ahead[p, :, at] + weight * beside[:, at]
+            copy = pltpu.make_async_copy(
+                held.at[p, :, at], out.at[row, pl.ds(start, held.shape[1]), at], sems.at[p, c]
+            )
+            copy.start()
+            copies.append(copy)
+    for copy in copies:
+        copy.wait()
+
+
+def add_last(beside, ahead, image, start, token):
+    plane = image.shape[-1]
+    parts = 4 if plane % 512 == 0 else 1
+    in_vmem = pl.BlockSpec(memory_space=pltpu.VMEM)
+    in_any = pl.BlockSpec(memory_space=pl.ANY)
+    return pl.pallas_call(
+        functools.partial(last_kernel, start, parts),
+        in_specs=[in_vmem, in_vmem, in_any, in_any],
+        out_specs=in_any,
+        out_shape=jax.ShapeDtypeStruct(image.shape, jnp.float32),
+        scratch_shapes=[pltpu.VMEM(ahead.shape, jnp.float32), pltpu.SemaphoreType.DMA((2, parts))],
+        input_output_aliases={2: 0},
+        compiler_params=pltpu.CompilerParams(vmem_limit_bytes=VMEM_LIMIT),
+        cost_estimate=SHORT,
+        name="add_last",
+    )(beside, ahead, image, token)
 
 
 def cuts(steps, pieces):
@@ -566,8 +629,7 @@
 
     y_out = []
     def inner(k, image):
-        token = [order.token] if k == len(in_cuts) - 1 else []
-        return order(add_inner(y_in[k], image, in_cuts[k][0], token))
+        return order(add_inner(y_in[k], image, in_cuts[k][0]))
 
     for j in range(slots):
         y_out.append(order(sent[2 + j]))
@@ -599,9 +661,12 @@
         image = halo(q, image)
     z_last = order(z_last)
     image = halo(slots, image)
-    for k in range(1, len(in_cuts)):
+    last = in_cuts[-1][0]
+    ahead = order(rows_ahead(image, last))
+    for k in range(1, len(in_cuts) - 1):
         y_in.append(order(sent[2 + slots + k]))
         image = inner(k, image)
+    image = add_last(order(sent[-1]), ahead, image, last, order.token)
     return image.transpose(1, 0, 2)
 
 

time: 288 us -> 287 us (level)
    pallas_call x7 -> x6, Pallas kernels: 31.3 us -> 29.3 us  [update(): pl.pallas_call(functools.partial(update_kernel, Change(change, [row for _...]
where the time goes in v5:
time: 287 us; the launch traced here: 286 us
  Pallas kernels  144 us (50%)
  waiting for transfers between devices  98.2 us (34%)
  starting transfers between devices  42.1 us (15%)
    ppermute x17, waiting for transfers between devices, send(): return lax.ppermute(order(value), axis, route)  98.2 us
    ppermute x17, starting transfers between devices, send(): return lax.ppermute(order(value), axis, route)  42.1 us
    pallas_call x4, Pallas kernels, plane_terms(): pl.pallas_call(functools.partial(plane_kernel, depth, shifts), grid=((end...  41.5 us
    pallas_call x12, Pallas kernels, staged(): pl.pallas_call(kernel, in_specs=[pl.BlockSpec(memory_space=pltpu.SMEM)] *...  32.7 us
    pallas_call x6, Pallas kernels, update(): pl.pallas_call(functools.partial(update_kernel, Change(change, [row for _...  29.3 us
    pallas_call x1, Pallas kernels, add_history(): pl.pallas_call(functools.partial(history_kernel, aways), grid=(depth, pla...  21.9 us
    pallas_call x1, Pallas kernels, mode_sums(): pl.pallas_call(sums_kernel, grid=(depth, plane // tile), in_specs=[pl.Blo...  12.3 us
  transfers between devices with their start and end apart: 17, of which 11 were waited for; matrix products, arithmetic and copies ran while one was open for 0% of the time, Pallas kernels for 49%

profile of v5, /device:TPU:0, one launch (start us, length us, event | category | flops | bytes accessed | tf_op | source)
XLA Modules:
  0.0 285.6 jit_solution(10842557803536894743)
XLA Ops:
  11.9 5.6 %head_of.1 = f32[3,16,9216]{2,1,0:T(8,128)} custom-call(f32[3,128,9216]{2,1,0:T(8,128)} %bitcast.13), custom_call_target="tpu_custom_call" | custom-call | flops 1 | bytes 1 | tf_op jit(solution)/shard_map/head_of/pallas_call | solution.py:199
  18.8 12.3 %mode_sums.1.sums = f32[3,16,9216]{2,1,0:T(8,128)S(1)} custom-call(f32[16]{0:T(128)S(1)} %get-tuple-element.220.scaled, f32[3,128,9216]{2,1,0:T(8,128)} %bitcast.14), custom_call_target="tpu_custom_call" | custom-call | flops 1 | bytes 1 | tf_op jit(solution)/shard_map/mode_sums/pallas_call | solution.py:67
  35.4 10.4 %plane_terms.4.refs_0_ = f32[3,128,9216]{2,1,0:T(8,128)} custom-call(f32[3,9216]{1,0:T(4,128)S(1)} %copy-done.5, f32[3,128,9216]{2,1,0:T(8,128)} %bitcast.15), custom_call_target="tpu_custom_call" | custom-call | flops 1 | bytes 1 | tf_op jit(solution)/shard_map/plane_terms/pallas_call | solution.py:323
  45.8 12.1 %collective-permute-done.4.refs_0_ = f32[64,9216]{1,0:T(8,128)S(1)} collective-permute-done((f32[64,9216]{1,0:T(8,128)}, f32[64,9216]{1,0:T(8,128)S(1)}, u32[]{:S(2)}, u32[]{:S(2)}) %collective-permute-start.4) | collective-permute-done | bytes 2359328 | tf_op jit(solution)/shard_map/ppermute | solution.py:533
  57.9 7.3 %collective-permute-done.3.relayed = f32[64,9216]{1,0:T(8,128)S(1)} collective-permute-done((f32[64,9216]{1,0:T(8,128)S(1)}, f32[64,9216]{1,0:T(8,128)S(1)}, u32[]{:S(2)}, u32[]{:S(2)}) %collective-permute-start.3) | collective-permute-done | bytes 2359328 | tf_op jit(solution)/shard_map/ppermute | solution.py:533
  72.3 6.0 %collective-permute-start.9 = (f32[64,9216]{1,0:T(8,128)S(1)}, f32[64,9216]{1,0:T(8,128)}, u32[]{:S(2)}, u32[]{:S(2)}) collective-permute-start(f32[64,9216]{1,0:T(8,128)S(1)} %collective-permute-done.4.refs_0_), channel_id=1, source_target_pairs={{0,2},{2,4},{3,1},{4,6},{5,3},{7,5},{8,10},{10,12},{11,9},{12,14},... | collective-permute-start | bytes 7077896 | tf_op jit(solution)/shard_map/ppermute | solution.py:533
  84.0 10.4 %plane_terms.5.refs_0_ = f32[3,128,9216]{2,1,0:T(8,128)} custom-call(f32[3,9216]{1,0:T(4,128)S(1)} %copy-done.5, f32[3,128,9216]{2,1,0:T(8,128)} %bitcast.18, f32[3,128,9216]{2,1,0:T(8,128)} %plane_terms.4.refs_0_), custom_call_target="tpu_custom_call", output_to_operand_aliasing={{}: (2, {})} | custom-call | flops 1 | bytes 1 | tf_op jit(solution)/shard_map/plane_terms/pallas_call | solution.py:323
  94.4 14.1 %collective-permute-done.refs_0_ = f32[64,9216]{1,0:T(8,128)} collective-permute-done((f32[64,9216]{1,0:T(8,128)}, f32[64,9216]{1,0:T(8,128)}, u32[]{:S(2)}, u32[]{:S(2)}) %collective-permute-start) | collective-permute-done | bytes 2359328 | tf_op jit(solution)/shard_map/ppermute | solution.py:533
  112.6 10.4 %plane_terms.6.refs_0_ = f32[3,128,9216]{2,1,0:T(8,128)} custom-call(f32[3,9216]{1,0:T(4,128)S(1)} %copy-done.6, f32[3,128,9216]{2,1,0:T(8,128)} %bitcast.20, f32[3,128,9216]{2,1,0:T(8,128)} %plane_terms.5.refs_0_), custom_call_target="tpu_custom_call", output_to_operand_aliasing={{}: (2, {})} | custom-call | flops 1 | bytes 1 | tf_op jit(solution)/shard_map/plane_terms/pallas_call | solution.py:323
  123.0 10.9 %collective-permute-done.7.refs_2_.refs_0_ = f32[32,9216]{1,0:T(8,128)} collective-permute-done((f32[32,9216]{1,0:T(8,128)}, f32[32,9216]{1,0:T(8,128)}, u32[]{:S(2)}, u32[]{:S(2)}) %collective-permute-start.7) | collective-permute-done | bytes 1179680 | tf_op jit(solution)/shard_map/ppermute | solution.py:533
  141.7 10.4 %plane_terms.7.refs_4_ = f32[3,128,9216]{2,1,0:T(8,128)} custom-call(f32[3,9216]{1,0:T(4,128)S(1)} %copy-done.6, f32[3,128,9216]{2,1,0:T(8,128)} %bitcast.22, f32[3,128,9216]{2,1,0:T(8,128)} %plane_terms.6.refs_0_), custom_call_target="tpu_custom_call", output_to_operand_aliasing={{}: (2, {})} | custom-call | flops 1 | bytes 1 | tf_op jit(solution)/shard_map/plane_terms/pallas_call | solution.py:323
  152.1 6.9 %collective-permute-done.5.refs_1_.refs_2_ = f32[32,9216]{1,0:T(8,128)S(1)} collective-permute-done((f32[32,9216]{1,0:T(8,128)S(1)}, f32[32,9216]{1,0:T(8,128)S(1)}, u32[]{:S(2)}, u32[]{:S(2)}) %collective-permute-start.5) | collective-permute-done | bytes 1179680 | tf_op jit(solution)/shard_map/ppermute | solution.py:533
  168.3 16.1 %collective-permute-done.10.refs_2_ = f32[32,9216]{1,0:T(8,128)} collective-permute-done((f32[32,9216]{1,0:T(8,128)S(1)}, f32[32,9216]{1,0:T(8,128)}, u32[]{:S(2)}, u32[]{:S(2)}) %collective-permute-start.10) | collective-permute-done | bytes 1179680 | tf_op jit(solution)/shard_map/ppermute | solution.py:533
  184.4 5.4 %collective-permute-start.16 = (f32[64,9216]{1,0:T(8,128)}, f32[64,9216]{1,0:T(8,128)}, u32[]{:S(2)}, u32[]{:S(2)}) collective-permute-start(f32[64,9216]{1,0:T(8,128)} %joined.1), channel_id=1, source_target_pairs={{0,2},{2,4},{5,3},{7,5},{8,10},{10,12},{13,11},{15,13},{16,18},{18... | collective-permute-start | bytes 7077896 | tf_op jit(solution)/shard_map/ppermute | solution.py:533
  193.0 4.3 %collective-permute-start.15 = (f32[32,9216]{1,0:T(8,128)}, f32[32,9216]{1,0:T(8,128)S(1)}, u32[]{:S(2)}, u32[]{:S(2)}) collective-permute-start(f32[32,9216]{1,0:T(8,128)} %collective-permute-done.10.refs_2_), channel_id=1, source_target_pairs={{0,2},{2,4},{3,1},{4,6},{5,3},{7,5},{8,10},{10,12},{11,9},{12,14},... | collective-permute-start | bytes 3538952 | tf_op jit(solution)/shard_map/ppermute | solution.py:533
  197.5 5.1 %add_halo.4.refs_3_ = f32[3,128,9216]{2,1,0:T(8,128)} custom-call(f32[64,9216]{1,0:T(8,128)S(1)} %collective-permute-done.4.refs_0_, f32[64,9216]{1,0:T(8,128)} %collective-permute-done.9.refs_1_, f32[32,9216]{1,0:T(8,128)} %collective-permute-done.7.refs_2_.refs_0_, f32[32,9216]{1,0:T(8,128)S(1)} %broadcast_in_dim.9.refs_3_, ...), custom_call_target="tpu_custom_call", output_to_operand_aliasing={{}: (4, {})} | custom-call | flops 1 | bytes 1 | tf_op jit(solution)/shard_map/add_halo/pallas_call | solution.py:386
  203.1 21.9 %add_history.1.refs_1_ = f32[3,128,9216]{2,1,0:T(8,128)} custom-call(f32[16]{0:T(128)S(1)} %copy-done.12, f32[16]{0:T(128)S(1)} %get-tuple-element.257.mode_gain, f32[1,16]{1,0:T(1,128)S(1)} %bitcast.8, f32[1,16]{1,0:T(1,128)S(1)} %bitcast.9, f32[3,128,9216]{2,1,0:T(8,128)} %bitcast.25, ...), custom_call_target="tpu_custom_call", output_to_operand_aliasing={{}: (8, {})} | custom-call | flops 1 | bytes 1 | tf_op jit(solution)/shard_map/add_history/pallas_call | solution.py:161
  224.9 16.3 %collective-permute-done.8.refs_0_ = f32[72,9216]{1,0:T(8,128)} collective-permute-done((f32[72,9216]{1,0:T(8,128)}, f32[72,9216]{1,0:T(8,128)}, u32[]{:S(2)}, u32[]{:S(2)}) %collective-permute-start.8) | collective-permute-done | bytes 2654240 | tf_op jit(solution)/shard_map/ppermute | solution.py:533
  245.0 6.0 %add_inner.2.refs_4_ = f32[3,128,9216]{2,1,0:T(8,128)} custom-call(f32[72,9216]{1,0:T(8,128)} %collective-permute-done.8.refs_0_, f32[3,128,9216]{2,1,0:T(8,128)} %add_history.1.refs_1_), custom_call_target="tpu_custom_call", output_to_operand_aliasing={{}: (1, {})} | custom-call | flops 1 | bytes 1 | tf_op jit(solution)/shard_map/add_inner/pallas_call | solution.py:386
  251.0 4.9 %add_halo.5.refs_4_ = f32[3,128,9216]{2,1,0:T(8,128)} custom-call(f32[64,9216]{1,0:T(8,128)S(1)} %collective-permute-done.4.refs_0_, f32[64,9216]{1,0:T(8,128)} %collective-permute-done.9.refs_1_, f32[32,9216]{1,0:T(8,128)S(1)} %collective-permute-done.5.refs_1_.refs_2_, f32[64,9216]{1,0:T(8,128)} %collective-permute-done.16.refs_3_, ...), custom_call_target="tpu_custom_call", output_to_operand_aliasing={{}: (4, {})} | custom-call | flops 1 | bytes 1 | tf_op jit(solution)/shard_map/add_halo/pallas_call | solution.py:386
  255.9 5.0 %add_halo.6.refs_4_ = f32[3,128,9216]{2,1,0:T(8,128)} custom-call(f32[64,9216]{1,0:T(8,128)} %collective-permute-done.refs_0_, f32[64,9216]{1,0:T(8,128)S(1)} %collective-permute-done.12.refs_1_, f32[32,9216]{1,0:T(8,128)} %collective-permute-done.10.refs_2_, f32[64,9216]{1,0:T(8,128)} %collective-permute-done.16.refs_3_, ...), custom_call_target="tpu_custom_call", output_to_operand_aliasing={{}: (4, {})} | custom-call | flops 1 | bytes 1 | tf_op jit(solution)/shard_map/add_halo/pallas_call | solution.py:386
  260.9 4.8 %collective-permute-done.15.refs_2_.refs_3_ = f32[32,9216]{1,0:T(8,128)S(1)} collective-permute-done((f32[32,9216]{1,0:T(8,128)}, f32[32,9216]{1,0:T(8,128)S(1)}, u32[]{:S(2)}, u32[]{:S(2)}) %collective-permute-start.15) | collective-permute-done | bytes 1179680 | tf_op jit(solution)/shard_map/ppermute | solution.py:533
  270.9 8.3 %collective-permute-done.14.refs_0_ = f32[48,9216]{1,0:T(8,128)} collective-permute-done((f32[48,9216]{1,0:T(8,128)}, f32[48,9216]{1,0:T(8,128)}, u32[]{:S(2)}, u32[]{:S(2)}) %collective-permute-start.14) | collective-permute-done | bytes 1769504 | tf_op jit(solution)/shard_map/ppermute | solution.py:533
  279.2 4.3 %add_inner.3.image = f32[3,128,9216]{2,1,0:T(8,128)} custom-call(f32[48,9216]{1,0:T(8,128)} %collective-permute-done.14.refs_0_, f32[3,128,9216]{2,1,0:T(8,128)} %add_halo.7.image.refs_1_), custom_call_target="tpu_custom_call", output_to_operand_aliasing={{}: (1, {})} | custom-call | flops 1 | bytes 1 | tf_op jit(solution)/shard_map/add_inner/pallas_call | solution.py:386
  (72 shorter events, 65.8 us)
Async XLA Ops:
  2.6 55.3 %collective-permute-start.4 = (f32[64,9216]{1,0:T(8,128)}, f32[64,9216]{1,0:T(8,128)S(1)}, u32[]{:S(2)}, u32[]{:S(2)}) collective-permute-start(f32[64,9216]{1,0:T(8,128)} %middle_rows.2), channel_id=1, source_target_pairs={{0,1},{1,0},{2,3},{3,2},{4,5},{5,4},{6,7},{7,6},{8,9},{9,8},{10,11... | collective-permute-start | bytes 7077896 | tf_op jit(solution)/shard_map/ppermute | solution.py:533
  10.6 8.2 %copy-start.15 = (f32[16]{0:T(128)S(1)}, f32[16]{0:T(128)}, u32[]{:S(2)}) copy-start(f32[16]{0:T(128)} %param.7) | copy-start | bytes 196
  10.6 54.6 %collective-permute-start.3 = (f32[64,9216]{1,0:T(8,128)S(1)}, f32[64,9216]{1,0:T(8,128)S(1)}, u32[]{:S(2)}, u32[]{:S(2)}) collective-permute-start(f32[64,9216]{1,0:T(8,128)S(1)} %rows_of.5), channel_id=1, source_target_pairs={{1,3},{2,0},{3,5},{4,2},{5,7},{6,4},{9,11},{10,8},{11,13},{12,10},... | collective-permute-start | bytes 7077896 | tf_op jit(solution)/shard_map/ppermute | solution.py:533
  17.5 49.6 %collective-permute-start.2 = (f32[3,16,9216]{2,1,0:T(8,128)}, f32[3,16,9216]{2,1,0:T(8,128)S(1)}, u32[]{:S(2)}, u32[]{:S(2)}) collective-permute-start(f32[3,16,9216]{2,1,0:T(8,128)} %head_of.1), channel_id=1, source_target_pairs={{8,0},{16,8},{24,16},{9,1},{17,9},{25,17},{10,2},{18,10},{26,18},{... | collective-permute-start | bytes 5308424 | tf_op jit(solution)/shard_map/ppermute | solution.py:533
  18.8 12.4 %copy-start.11 = (f32[16]{0:T(128)}, f32[16]{0:T(128)S(1)}, u32[]{:S(2)}) copy-start(f32[16]{0:T(128)S(1)} %get-tuple-element.220.scaled) | copy-start | bytes 196
  18.8 16.6 %copy-start.5 = (f32[3,9216]{1,0:T(4,128)S(1)}, f32[3,9216]{1,0:T(4,128)}, u32[]{:S(2)}) copy-start(f32[3,9216]{1,0:T(4,128)} %absorption.3) | copy-start | bytes 331780
  31.2 14.6 %copy-start.2 = (f32[3,16,9216]{2,1,0:T(8,128)}, f32[3,16,9216]{2,1,0:T(8,128)S(1)}, u32[]{:S(2)}) copy-start(f32[3,16,9216]{2,1,0:T(8,128)S(1)} %mode_sums.1.sums) | copy-start | bytes 5308420
  31.2 35.9 %collective-permute-start.1 = (f32[3,16,9216]{2,1,0:T(8,128)S(1)}, f32[3,16,9216]{2,1,0:T(8,128)S(1)}, u32[]{:S(2)}, u32[]{:S(2)}) collective-permute-start(f32[3,16,9216]{2,1,0:T(8,128)S(1)} %mode_sums.1.sums), channel_id=1, source_target_pairs={{8,0},{16,8},{24,16},{9,1},{17,9},{25,17},{10,2},{18,10},{26,18},{... | collective-permute-start | bytes 5308424 | tf_op jit(solution)/shard_map/ppermute | solution.py:533
  32.5 76.1 %collective-permute-start = (f32[64,9216]{1,0:T(8,128)}, f32[64,9216]{1,0:T(8,128)}, u32[]{:S(2)}, u32[]{:S(2)}) collective-permute-start(f32[64,9216]{1,0:T(8,128)} %middle_rows.3), channel_id=1, source_target_pairs={{0,1},{1,0},{2,3},{3,2},{4,5},{5,4},{6,7},{7,6},{8,9},{9,8},{10,11... | collective-permute-start | bytes 7077896 | tf_op jit(solution)/shard_map/ppermute | solution.py:533
  70.4 63.5 %collective-permute-start.7 = (f32[32,9216]{1,0:T(8,128)}, f32[32,9216]{1,0:T(8,128)}, u32[]{:S(2)}, u32[]{:S(2)}) collective-permute-start(f32[32,9216]{1,0:T(8,128)} %picked_rows.3), channel_id=1, source_target_pairs={{0,1},{1,0},{2,3},{3,2},{4,5},{5,4},{6,7},{7,6},{8,9},{9,8},{10,11... | collective-permute-start | bytes 3538952 | tf_op jit(solution)/shard_map/ppermute | solution.py:533
  71.0 62.8 %collective-permute-start.6 = (f32[32,9216]{1,0:T(8,128)}, f32[32,9216]{1,0:T(8,128)}, u32[]{:S(2)}, u32[]{:S(2)}) collective-permute-start(f32[32,9216]{1,0:T(8,128)} %rows_of.6), channel_id=1, source_target_pairs={{1,3},{2,0},{3,5},{4,2},{5,7},{6,4},{9,11},{10,8},{11,13},{12,10},... | collective-permute-start | bytes 3538952 | tf_op jit(solution)/shard_map/ppermute | solution.py:533
  72.3 112.1 %collective-permute-start.9 = (f32[64,9216]{1,0:T(8,128)S(1)}, f32[64,9216]{1,0:T(8,128)}, u32[]{:S(2)}, u32[]{:S(2)}) collective-permute-start(f32[64,9216]{1,0:T(8,128)S(1)} %collective-permute-done.4.refs_0_), channel_id=1, source_target_pairs={{0,2},{2,4},{3,1},{4,6},{5,3},{7,5},{8,10},{10,12},{11,9},{12,14},... | collective-permute-start | bytes 7077896 | tf_op jit(solution)/shard_map/ppermute | solution.py:533
  82.6 25.9 %copy-start.1 = (f32[64,9216]{1,0:T(8,128)S(1)}, f32[64,9216]{1,0:T(8,128)}, u32[]{:S(2)}) copy-start(f32[64,9216]{1,0:T(8,128)} %copy-done) | copy-start | bytes 7077892
  82.6 81.7 %collective-permute-start.11 = (f32[3,16,9216]{2,1,0:T(8,128)}, f32[3,16,9216]{2,1,0:T(8,128)S(1)}, u32[]{:S(2)}, u32[]{:S(2)}) collective-permute-start(f32[3,16,9216]{2,1,0:T(8,128)} %carried.1), channel_id=1, source_target_pairs={{16,0},{24,8},{17,1},{25,9},{18,2},{26,10},{19,3},{27,11},{20,4},{... | collective-permute-start | bytes 5308424 | tf_op jit(solution)/shard_map/ppermute | solution.py:533
  94.4 18.2 %copy-start.6 = (f32[3,9216]{1,0:T(4,128)S(1)}, f32[3,9216]{1,0:T(4,128)}, u32[]{:S(2)}) copy-start(f32[3,9216]{1,0:T(4,128)} %absorption.3) | copy-start | bytes 331780
  109.7 49.3 %collective-permute-start.5 = (f32[32,9216]{1,0:T(8,128)S(1)}, f32[32,9216]{1,0:T(8,128)S(1)}, u32[]{:S(2)}, u32[]{:S(2)}) collective-permute-start(f32[32,9216]{1,0:T(8,128)S(1)} %picked_rows.4), channel_id=1, source_target_pairs={{0,1},{1,0},{2,3},{3,2},{4,5},{5,4},{6,7},{7,6},{8,9},{9,8},{10,11... | collective-permute-start | bytes 3538952 | tf_op jit(solution)/shard_map/ppermute | solution.py:533
  135.8 48.6 %collective-permute-start.10 = (f32[32,9216]{1,0:T(8,128)S(1)}, f32[32,9216]{1,0:T(8,128)}, u32[]{:S(2)}, u32[]{:S(2)}) collective-permute-start(f32[32,9216]{1,0:T(8,128)S(1)} %picked_rows.5), channel_id=1, source_target_pairs={{0,1},{1,0},{2,3},{3,2},{4,5},{5,4},{6,7},{7,6},{8,9},{9,8},{10,11... | collective-permute-start | bytes 3538952 | tf_op jit(solution)/shard_map/ppermute | solution.py:533
  137.9 55.1 %collective-permute-start.12 = (f32[64,9216]{1,0:T(8,128)}, f32[64,9216]{1,0:T(8,128)S(1)}, u32[]{:S(2)}, u32[]{:S(2)}) collective-permute-start(f32[64,9216]{1,0:T(8,128)} %collective-permute-done.refs_0_), channel_id=1, source_target_pairs={{0,2},{2,4},{3,1},{4,6},{5,3},{7,5},{8,10},{10,12},{11,9},{12,14},... | collective-permute-start | bytes 7077896 | tf_op jit(solution)/shard_map/ppermute | solution.py:533
  162.2 79.1 %collective-permute-start.8 = (f32[72,9216]{1,0:T(8,128)}, f32[72,9216]{1,0:T(8,128)}, u32[]{:S(2)}, u32[]{:S(2)}) collective-permute-start(f32[72,9216]{1,0:T(8,128)} %rows_of.7), channel_id=1, source_target_pairs={{0,1},{1,0},{2,3},{3,2},{4,5},{5,4},{6,7},{7,6},{8,9},{9,8},{10,11... | collective-permute-start | bytes 7962632 | tf_op jit(solution)/shard_map/ppermute | solution.py:533
  184.4 66.6 %collective-permute-start.16 = (f32[64,9216]{1,0:T(8,128)}, f32[64,9216]{1,0:T(8,128)}, u32[]{:S(2)}, u32[]{:S(2)}) collective-permute-start(f32[64,9216]{1,0:T(8,128)} %joined.1), channel_id=1, source_target_pairs={{0,2},{2,4},{5,3},{7,5},{8,10},{10,12},{13,11},{15,13},{16,18},{18... | collective-permute-start | bytes 7077896 | tf_op jit(solution)/shard_map/ppermute | solution.py:533
  192.7 86.5 %collective-permute-start.14 = (f32[48,9216]{1,0:T(8,128)}, f32[48,9216]{1,0:T(8,128)}, u32[]{:S(2)}, u32[]{:S(2)}) collective-permute-start(f32[48,9216]{1,0:T(8,128)} %rows_of.8), channel_id=1, source_target_pairs={{0,1},{1,0},{2,3},{3,2},{4,5},{5,4},{6,7},{7,6},{8,9},{9,8},{10,11... | collective-permute-start | bytes 5308424 | tf_op jit(solution)/shard_map/ppermute | solution.py:533
  193.0 72.7 %collective-permute-start.15 = (f32[32,9216]{1,0:T(8,128)}, f32[32,9216]{1,0:T(8,128)S(1)}, u32[]{:S(2)}, u32[]{:S(2)}) collective-permute-start(f32[32,9216]{1,0:T(8,128)} %collective-permute-done.10.refs_2_), channel_id=1, source_target_pairs={{0,2},{2,4},{3,1},{4,6},{5,3},{7,5},{8,10},{10,12},{11,9},{12,14},... | collective-permute-start | bytes 3538952 | tf_op jit(solution)/shard_map/ppermute | solution.py:533
  242.9 41.7 %collective-permute-start.13 = (f32[8,9216]{1,0:T(8,128)S(1)}, f32[8,9216]{1,0:T(8,128)S(1)}, u32[]{:S(2)}, u32[]{:S(2)}) collective-permute-start(f32[8,9216]{1,0:T(8,128)S(1)} %rows_of.9), channel_id=1, source_target_pairs={{0,1},{1,0},{2,3},{3,2},{4,5},{5,4},{6,7},{7,6},{8,9},{9,8},{10,11... | collective-permute-start | bytes 884744 | tf_op jit(solution)/shard_map/ppermute | solution.py:533
  270.9 13.7 %copy-start.14 = (f32[16]{0:T(128)S(1)}, f32[16]{0:T(128)}, u32[]{:S(2)}) copy-start(f32[16]{0:T(128)} %token_) | copy-start | bytes 196
  (9 other events, 39.4 us)

commit v6 on v5

--- a/solution.py
+++ b/solution.py
@@ -540,7 +540,7 @@
 
     mid_cuts = between(0, whole_rows(1 / 2), steps)
     out_cuts = cuts(steps, pairs)
-    in_cuts = between(0, whole_rows(9 / 16), steps - ROWS, steps)
+    in_cuts = between(0, whole_rows(9 / 16), steps - 2 * ROWS, steps)
     plane_cuts = cuts(steps, 4)
     slots = pairs - 1
 

time: 287 us -> 287 us (level)
  no operation moved by 1% of the time
where the time goes in v6:
time: 287 us; the launch traced here: 286 us
  Pallas kernels  143 us (50%)
  waiting for transfers between devices  98.2 us (34%)
  starting transfers between devices  42 us (15%)
    ppermute x17, waiting for transfers between devices, send(): return lax.ppermute(order(value), axis, route)  98.2 us
    ppermute x17, starting transfers between devices, send(): return lax.ppermute(order(value), axis, route)  42 us
    pallas_call x4, Pallas kernels, plane_terms(): pl.pallas_call(functools.partial(plane_kernel, depth, shifts), grid=((end...  41.7 us
    pallas_call x12, Pallas kernels, staged(): pl.pallas_call(kernel, in_specs=[pl.BlockSpec(memory_space=pltpu.SMEM)] *...  32.2 us
    pallas_call x6, Pallas kernels, update(): pl.pallas_call(functools.partial(update_kernel, Change(change, [row for _...  28.4 us
    pallas_call x1, Pallas kernels, add_history(): pl.pallas_call(functools.partial(history_kernel, aways), grid=(depth, pla...  21.9 us
    pallas_call x1, Pallas kernels, mode_sums(): pl.pallas_call(sums_kernel, grid=(depth, plane // tile), in_specs=[pl.Blo...  12.3 us
  transfers between devices with their start and end apart: 17, of which 11 were waited for; matrix products, arithmetic and copies ran while one was open for 0% of the time, Pallas kernels for 49%

profile of v6, /device:TPU:0, one launch (start us, length us, event | category | flops | bytes accessed | tf_op | source)
XLA Modules:
  0.0 285.8 jit_solution(5999999704499118497)
XLA Ops:
  14.8 5.6 %head_of.1 = f32[3,16,9216]{2,1,0:T(8,128)} custom-call(f32[3,128,9216]{2,1,0:T(8,128)} %bitcast.13), custom_call_target="tpu_custom_call" | custom-call | flops 1 | bytes 1 | tf_op jit(solution)/shard_map/head_of/pallas_call | solution.py:199
  21.7 12.3 %mode_sums.1.sums = f32[3,16,9216]{2,1,0:T(8,128)S(1)} custom-call(f32[16]{0:T(128)S(1)} %get-tuple-element.220.scaled, f32[3,128,9216]{2,1,0:T(8,128)} %bitcast.14), custom_call_target="tpu_custom_call" | custom-call | flops 1 | bytes 1 | tf_op jit(solution)/shard_map/mode_sums/pallas_call | solution.py:67
  35.4 10.4 %plane_terms.4.refs_0_ = f32[3,128,9216]{2,1,0:T(8,128)} custom-call(f32[3,9216]{1,0:T(4,128)S(1)} %copy-done.5, f32[3,128,9216]{2,1,0:T(8,128)} %bitcast.15), custom_call_target="tpu_custom_call" | custom-call | flops 1 | bytes 1 | tf_op jit(solution)/shard_map/plane_terms/pallas_call | solution.py:323
  45.8 12.1 %collective-permute-done.4.refs_0_ = f32[64,9216]{1,0:T(8,128)S(1)} collective-permute-done((f32[64,9216]{1,0:T(8,128)}, f32[64,9216]{1,0:T(8,128)S(1)}, u32[]{:S(2)}, u32[]{:S(2)}) %collective-permute-start.4) | collective-permute-done | bytes 2359328 | tf_op jit(solution)/shard_map/ppermute | solution.py:533
  57.9 7.3 %collective-permute-done.3.relayed = f32[64,9216]{1,0:T(8,128)S(1)} collective-permute-done((f32[64,9216]{1,0:T(8,128)S(1)}, f32[64,9216]{1,0:T(8,128)S(1)}, u32[]{:S(2)}, u32[]{:S(2)}) %collective-permute-start.3) | collective-permute-done | bytes 2359328 | tf_op jit(solution)/shard_map/ppermute | solution.py:533
  72.3 6.0 %collective-permute-start.9 = (f32[64,9216]{1,0:T(8,128)S(1)}, f32[64,9216]{1,0:T(8,128)}, u32[]{:S(2)}, u32[]{:S(2)}) collective-permute-start(f32[64,9216]{1,0:T(8,128)S(1)} %collective-permute-done.4.refs_0_), channel_id=1, source_target_pairs={{0,2},{2,4},{3,1},{4,6},{5,3},{7,5},{8,10},{10,12},{11,9},{12,14},... | collective-permute-start | bytes 7077896 | tf_op jit(solution)/shard_map/ppermute | solution.py:533
  78.4 4.3 %carried.1 = f32[3,16,9216]{2,1,0:T(8,128)} custom-call(f32[16]{0:T(128)} %copy-done.11, f32[3,16,9216]{2,1,0:T(8,128)} %copy-done.2, f32[3,16,9216]{2,1,0:T(8,128)} %copy-done.3), custom_call_target="tpu_custom_call" | custom-call | flops 1 | bytes 1 | tf_op jit(solution)/shard_map/carried/pallas_call | solution.py:93
  82.6 10.5 %plane_terms.5.refs_0_ = f32[3,128,9216]{2,1,0:T(8,128)} custom-call(f32[3,9216]{1,0:T(4,128)S(1)} %copy-done.5, f32[3,128,9216]{2,1,0:T(8,128)} %bitcast.18, f32[3,128,9216]{2,1,0:T(8,128)} %plane_terms.4.refs_0_), custom_call_target="tpu_custom_call", output_to_operand_aliasing={{}: (2, {})} | custom-call | flops 1 | bytes 1 | tf_op jit(solution)/shard_map/plane_terms/pallas_call | solution.py:323
  93.2 15.4 %collective-permute-done.refs_0_ = f32[64,9216]{1,0:T(8,128)} collective-permute-done((f32[64,9216]{1,0:T(8,128)}, f32[64,9216]{1,0:T(8,128)}, u32[]{:S(2)}, u32[]{:S(2)}) %collective-permute-start) | collective-permute-done | bytes 2359328 | tf_op jit(solution)/shard_map/ppermute | solution.py:533
  113.9 10.4 %plane_terms.6.refs_0_ = f32[3,128,9216]{2,1,0:T(8,128)} custom-call(f32[3,9216]{1,0:T(4,128)S(1)} %copy-done.6, f32[3,128,9216]{2,1,0:T(8,128)} %bitcast.20, f32[3,128,9216]{2,1,0:T(8,128)} %plane_terms.5.refs_0_), custom_call_target="tpu_custom_call", output_to_operand_aliasing={{}: (2, {})} | custom-call | flops 1 | bytes 1 | tf_op jit(solution)/shard_map/plane_terms/pallas_call | solution.py:323
  124.3 9.5 %collective-permute-done.7.refs_2_.refs_0_ = f32[32,9216]{1,0:T(8,128)} collective-permute-done((f32[32,9216]{1,0:T(8,128)}, f32[32,9216]{1,0:T(8,128)}, u32[]{:S(2)}, u32[]{:S(2)}) %collective-permute-start.7) | collective-permute-done | bytes 1179680 | tf_op jit(solution)/shard_map/ppermute | solution.py:533
  141.7 10.4 %plane_terms.7.refs_4_ = f32[3,128,9216]{2,1,0:T(8,128)} custom-call(f32[3,9216]{1,0:T(4,128)S(1)} %copy-done.6, f32[3,128,9216]{2,1,0:T(8,128)} %bitcast.22, f32[3,128,9216]{2,1,0:T(8,128)} %plane_terms.6.refs_0_), custom_call_target="tpu_custom_call", output_to_operand_aliasing={{}: (2, {})} | custom-call | flops 1 | bytes 1 | tf_op jit(solution)/shard_map/plane_terms/pallas_call | solution.py:323
  152.1 6.9 %collective-permute-done.5.refs_1_.refs_2_ = f32[32,9216]{1,0:T(8,128)S(1)} collective-permute-done((f32[32,9216]{1,0:T(8,128)S(1)}, f32[32,9216]{1,0:T(8,128)S(1)}, u32[]{:S(2)}, u32[]{:S(2)}) %collective-permute-start.5) | collective-permute-done | bytes 1179680 | tf_op jit(solution)/shard_map/ppermute | solution.py:533
  169.0 15.4 %collective-permute-done.10.refs_2_ = f32[32,9216]{1,0:T(8,128)} collective-permute-done((f32[32,9216]{1,0:T(8,128)S(1)}, f32[32,9216]{1,0:T(8,128)}, u32[]{:S(2)}, u32[]{:S(2)}) %collective-permute-start.10) | collective-permute-done | bytes 1179680 | tf_op jit(solution)/shard_map/ppermute | solution.py:533
  184.4 5.4 %collective-permute-start.16 = (f32[64,9216]{1,0:T(8,128)}, f32[64,9216]{1,0:T(8,128)}, u32[]{:S(2)}, u32[]{:S(2)}) collective-permute-start(f32[64,9216]{1,0:T(8,128)} %joined.1), channel_id=1, source_target_pairs={{0,2},{2,4},{5,3},{7,5},{8,10},{10,12},{13,11},{15,13},{16,18},{18... | collective-permute-start | bytes 7077896 | tf_op jit(solution)/shard_map/ppermute | solution.py:533
  193.0 4.3 %collective-permute-start.15 = (f32[32,9216]{1,0:T(8,128)}, f32[32,9216]{1,0:T(8,128)S(1)}, u32[]{:S(2)}, u32[]{:S(2)}) collective-permute-start(f32[32,9216]{1,0:T(8,128)} %collective-permute-done.10.refs_2_), channel_id=1, source_target_pairs={{0,2},{2,4},{3,1},{4,6},{5,3},{7,5},{8,10},{10,12},{11,9},{12,14},... | collective-permute-start | bytes 3538952 | tf_op jit(solution)/shard_map/ppermute | solution.py:533
  197.5 5.1 %add_halo.4.refs_3_ = f32[3,128,9216]{2,1,0:T(8,128)} custom-call(f32[64,9216]{1,0:T(8,128)S(1)} %collective-permute-done.4.refs_0_, f32[64,9216]{1,0:T(8,128)} %collective-permute-done.9.refs_1_, f32[32,9216]{1,0:T(8,128)} %collective-permute-done.7.refs_2_.refs_0_, f32[32,9216]{1,0:T(8,128)S(1)} %broadcast_in_dim.9.refs_3_, ...), custom_call_target="tpu_custom_call", output_to_operand_aliasing={{}: (4, {})} | custom-call | flops 1 | bytes 1 | tf_op jit(solution)/shard_map/add_halo/pallas_call | solution.py:386
  203.0 21.9 %add_history.1.refs_1_ = f32[3,128,9216]{2,1,0:T(8,128)} custom-call(f32[16]{0:T(128)S(1)} %copy-done.12, f32[16]{0:T(128)S(1)} %get-tuple-element.257.mode_gain, f32[1,16]{1,0:T(1,128)S(1)} %bitcast.8, f32[1,16]{1,0:T(1,128)S(1)} %bitcast.9, f32[3,128,9216]{2,1,0:T(8,128)} %bitcast.25, ...), custom_call_target="tpu_custom_call", output_to_operand_aliasing={{}: (8, {})} | custom-call | flops 1 | bytes 1 | tf_op jit(solution)/shard_map/add_history/pallas_call | solution.py:161
  224.9 16.3 %collective-permute-done.8.refs_0_ = f32[72,9216]{1,0:T(8,128)} collective-permute-done((f32[72,9216]{1,0:T(8,128)}, f32[72,9216]{1,0:T(8,128)}, u32[]{:S(2)}, u32[]{:S(2)}) %collective-permute-start.8) | collective-permute-done | bytes 2654240 | tf_op jit(solution)/shard_map/ppermute | solution.py:533
  245.1 6.0 %add_inner.2.refs_4_ = f32[3,128,9216]{2,1,0:T(8,128)} custom-call(f32[72,9216]{1,0:T(8,128)} %collective-permute-done.8.refs_0_, f32[3,128,9216]{2,1,0:T(8,128)} %add_history.1.refs_1_), custom_call_target="tpu_custom_call", output_to_operand_aliasing={{}: (1, {})} | custom-call | flops 1 | bytes 1 | tf_op jit(solution)/shard_map/add_inner/pallas_call | solution.py:386
  251.1 4.9 %add_halo.5.refs_4_ = f32[3,128,9216]{2,1,0:T(8,128)} custom-call(f32[64,9216]{1,0:T(8,128)S(1)} %collective-permute-done.4.refs_0_, f32[64,9216]{1,0:T(8,128)} %collective-permute-done.9.refs_1_, f32[32,9216]{1,0:T(8,128)S(1)} %collective-permute-done.5.refs_1_.refs_2_, f32[64,9216]{1,0:T(8,128)} %collective-permute-done.16.refs_3_, ...), custom_call_target="tpu_custom_call", output_to_operand_aliasing={{}: (4, {})} | custom-call | flops 1 | bytes 1 | tf_op jit(solution)/shard_map/add_halo/pallas_call | solution.py:386
  256.0 5.0 %add_halo.6.refs_4_ = f32[3,128,9216]{2,1,0:T(8,128)} custom-call(f32[64,9216]{1,0:T(8,128)} %collective-permute-done.refs_0_, f32[64,9216]{1,0:T(8,128)S(1)} %collective-permute-done.12.refs_1_, f32[32,9216]{1,0:T(8,128)} %collective-permute-done.10.refs_2_, f32[64,9216]{1,0:T(8,128)} %collective-permute-done.16.refs_3_, ...), custom_call_target="tpu_custom_call", output_to_operand_aliasing={{}: (4, {})} | custom-call | flops 1 | bytes 1 | tf_op jit(solution)/shard_map/add_halo/pallas_call | solution.py:386
  261.0 4.7 %collective-permute-done.15.refs_2_.refs_3_ = f32[32,9216]{1,0:T(8,128)S(1)} collective-permute-done((f32[32,9216]{1,0:T(8,128)}, f32[32,9216]{1,0:T(8,128)S(1)}, u32[]{:S(2)}, u32[]{:S(2)}) %collective-permute-start.15) | collective-permute-done | bytes 1179680 | tf_op jit(solution)/shard_map/ppermute | solution.py:533
  276.3 8.3 %collective-permute-done.13.beside = f32[16,9216]{1,0:T(8,128)S(1)} collective-permute-done((f32[16,9216]{1,0:T(8,128)S(1)}, f32[16,9216]{1,0:T(8,128)S(1)}, u32[]{:S(2)}, u32[]{:S(2)}) %collective-permute-start.13) | collective-permute-done | bytes 589856 | tf_op jit(solution)/shard_map/ppermute | solution.py:533
  (74 shorter events, 66.7 us)
Async XLA Ops:
  2.6 55.3 %collective-permute-start.4 = (f32[64,9216]{1,0:T(8,128)}, f32[64,9216]{1,0:T(8,128)S(1)}, u32[]{:S(2)}, u32[]{:S(2)}) collective-permute-start(f32[64,9216]{1,0:T(8,128)} %middle_rows.2), channel_id=1, source_target_pairs={{0,1},{1,0},{2,3},{3,2},{4,5},{5,4},{6,7},{7,6},{8,9},{9,8},{10,11... | collective-permute-start | bytes 7077896 | tf_op jit(solution)/shard_map/ppermute | solution.py:533
  10.6 54.6 %collective-permute-start.3 = (f32[64,9216]{1,0:T(8,128)S(1)}, f32[64,9216]{1,0:T(8,128)S(1)}, u32[]{:S(2)}, u32[]{:S(2)}) collective-permute-start(f32[64,9216]{1,0:T(8,128)S(1)} %rows_of.5), channel_id=1, source_target_pairs={{1,3},{2,0},{3,5},{4,2},{5,7},{6,4},{9,11},{10,8},{11,13},{12,10},... | collective-permute-start | bytes 7077896 | tf_op jit(solution)/shard_map/ppermute | solution.py:533
  11.9 96.7 %collective-permute-start = (f32[64,9216]{1,0:T(8,128)}, f32[64,9216]{1,0:T(8,128)}, u32[]{:S(2)}, u32[]{:S(2)}) collective-permute-start(f32[64,9216]{1,0:T(8,128)} %middle_rows.3), channel_id=1, source_target_pairs={{0,1},{1,0},{2,3},{3,2},{4,5},{5,4},{6,7},{7,6},{8,9},{9,8},{10,11... | collective-permute-start | bytes 7077896 | tf_op jit(solution)/shard_map/ppermute | solution.py:533
  20.4 46.7 %collective-permute-start.2 = (f32[3,16,9216]{2,1,0:T(8,128)}, f32[3,16,9216]{2,1,0:T(8,128)S(1)}, u32[]{:S(2)}, u32[]{:S(2)}) collective-permute-start(f32[3,16,9216]{2,1,0:T(8,128)} %head_of.1), channel_id=1, source_target_pairs={{8,0},{16,8},{24,16},{9,1},{17,9},{25,17},{10,2},{18,10},{26,18},{... | collective-permute-start | bytes 5308424 | tf_op jit(solution)/shard_map/ppermute | solution.py:533
  21.7 12.4 %copy-start.11 = (f32[16]{0:T(128)}, f32[16]{0:T(128)S(1)}, u32[]{:S(2)}) copy-start(f32[16]{0:T(128)S(1)} %get-tuple-element.220.scaled) | copy-start | bytes 196
  21.7 13.7 %copy-start.5 = (f32[3,9216]{1,0:T(4,128)S(1)}, f32[3,9216]{1,0:T(4,128)}, u32[]{:S(2)}) copy-start(f32[3,9216]{1,0:T(4,128)} %absorption.3) | copy-start | bytes 331780
  34.1 11.7 %copy-start.2 = (f32[3,16,9216]{2,1,0:T(8,128)}, f32[3,16,9216]{2,1,0:T(8,128)S(1)}, u32[]{:S(2)}) copy-start(f32[3,16,9216]{2,1,0:T(8,128)S(1)} %mode_sums.1.sums) | copy-start | bytes 5308420
  34.1 33.0 %collective-permute-start.1 = (f32[3,16,9216]{2,1,0:T(8,128)S(1)}, f32[3,16,9216]{2,1,0:T(8,128)S(1)}, u32[]{:S(2)}, u32[]{:S(2)}) collective-permute-start(f32[3,16,9216]{2,1,0:T(8,128)S(1)} %mode_sums.1.sums), channel_id=1, source_target_pairs={{8,0},{16,8},{24,16},{9,1},{17,9},{25,17},{10,2},{18,10},{26,18},{... | collective-permute-start | bytes 5308424 | tf_op jit(solution)/shard_map/ppermute | solution.py:533
  70.4 63.4 %collective-permute-start.7 = (f32[32,9216]{1,0:T(8,128)}, f32[32,9216]{1,0:T(8,128)}, u32[]{:S(2)}, u32[]{:S(2)}) collective-permute-start(f32[32,9216]{1,0:T(8,128)} %picked_rows.3), channel_id=1, source_target_pairs={{0,1},{1,0},{2,3},{3,2},{4,5},{5,4},{6,7},{7,6},{8,9},{9,8},{10,11... | collective-permute-start | bytes 3538952 | tf_op jit(solution)/shard_map/ppermute | solution.py:533
  71.0 62.8 %collective-permute-start.6 = (f32[32,9216]{1,0:T(8,128)}, f32[32,9216]{1,0:T(8,128)}, u32[]{:S(2)}, u32[]{:S(2)}) collective-permute-start(f32[32,9216]{1,0:T(8,128)} %rows_of.6), channel_id=1, source_target_pairs={{1,3},{2,0},{3,5},{4,2},{5,7},{6,4},{9,11},{10,8},{11,13},{12,10},... | collective-permute-start | bytes 3538952 | tf_op jit(solution)/shard_map/ppermute | solution.py:533
  72.3 112.1 %collective-permute-start.9 = (f32[64,9216]{1,0:T(8,128)S(1)}, f32[64,9216]{1,0:T(8,128)}, u32[]{:S(2)}, u32[]{:S(2)}) collective-permute-start(f32[64,9216]{1,0:T(8,128)S(1)} %collective-permute-done.4.refs_0_), channel_id=1, source_target_pairs={{0,2},{2,4},{3,1},{4,6},{5,3},{7,5},{8,10},{10,12},{11,9},{12,14},... | collective-permute-start | bytes 7077896 | tf_op jit(solution)/shard_map/ppermute | solution.py:533
  82.6 25.9 %copy-start.1 = (f32[64,9216]{1,0:T(8,128)S(1)}, f32[64,9216]{1,0:T(8,128)}, u32[]{:S(2)}) copy-start(f32[64,9216]{1,0:T(8,128)} %copy-done) | copy-start | bytes 7077892
  93.2 19.4 %copy-start.15 = (f32[3,16,9216]{2,1,0:T(8,128)S(1)}, f32[3,16,9216]{2,1,0:T(8,128)}, u32[]{:S(2)}) copy-start(f32[3,16,9216]{2,1,0:T(8,128)} %carried.1) | copy-start | bytes 5308420
  93.2 20.7 %copy-start.6 = (f32[3,9216]{1,0:T(4,128)S(1)}, f32[3,9216]{1,0:T(4,128)}, u32[]{:S(2)}) copy-start(f32[3,9216]{1,0:T(4,128)} %absorption.3) | copy-start | bytes 331780
  109.7 49.3 %collective-permute-start.5 = (f32[32,9216]{1,0:T(8,128)S(1)}, f32[32,9216]{1,0:T(8,128)S(1)}, u32[]{:S(2)}, u32[]{:S(2)}) collective-permute-start(f32[32,9216]{1,0:T(8,128)S(1)} %picked_rows.4), channel_id=1, source_target_pairs={{0,1},{1,0},{2,3},{3,2},{4,5},{5,4},{6,7},{7,6},{8,9},{9,8},{10,11... | collective-permute-start | bytes 3538952 | tf_op jit(solution)/shard_map/ppermute | solution.py:533
  112.6 51.7 %collective-permute-start.11 = (f32[3,16,9216]{2,1,0:T(8,128)S(1)}, f32[3,16,9216]{2,1,0:T(8,128)S(1)}, u32[]{:S(2)}, u32[]{:S(2)}) collective-permute-start(f32[3,16,9216]{2,1,0:T(8,128)S(1)} %copy-done.15), channel_id=1, source_target_pairs={{16,0},{24,8},{17,1},{25,9},{18,2},{26,10},{19,3},{27,11},{20,4},{... | collective-permute-start | bytes 5308424 | tf_op jit(solution)/shard_map/ppermute | solution.py:533
  135.7 48.6 %collective-permute-start.10 = (f32[32,9216]{1,0:T(8,128)S(1)}, f32[32,9216]{1,0:T(8,128)}, u32[]{:S(2)}, u32[]{:S(2)}) collective-permute-start(f32[32,9216]{1,0:T(8,128)S(1)} %picked_rows.5), channel_id=1, source_target_pairs={{0,1},{1,0},{2,3},{3,2},{4,5},{5,4},{6,7},{7,6},{8,9},{9,8},{10,11... | collective-permute-start | bytes 3538952 | tf_op jit(solution)/shard_map/ppermute | solution.py:533
  137.9 55.1 %collective-permute-start.12 = (f32[64,9216]{1,0:T(8,128)}, f32[64,9216]{1,0:T(8,128)S(1)}, u32[]{:S(2)}, u32[]{:S(2)}) collective-permute-start(f32[64,9216]{1,0:T(8,128)} %collective-permute-done.refs_0_), channel_id=1, source_target_pairs={{0,2},{2,4},{3,1},{4,6},{5,3},{7,5},{8,10},{10,12},{11,9},{12,14},... | collective-permute-start | bytes 7077896 | tf_op jit(solution)/shard_map/ppermute | solution.py:533
  162.2 79.1 %collective-permute-start.8 = (f32[72,9216]{1,0:T(8,128)}, f32[72,9216]{1,0:T(8,128)}, u32[]{:S(2)}, u32[]{:S(2)}) collective-permute-start(f32[72,9216]{1,0:T(8,128)} %rows_of.7), channel_id=1, source_target_pairs={{0,1},{1,0},{2,3},{3,2},{4,5},{5,4},{6,7},{7,6},{8,9},{9,8},{10,11... | collective-permute-start | bytes 7962632 | tf_op jit(solution)/shard_map/ppermute | solution.py:533
  184.4 66.7 %collective-permute-start.16 = (f32[64,9216]{1,0:T(8,128)}, f32[64,9216]{1,0:T(8,128)}, u32[]{:S(2)}, u32[]{:S(2)}) collective-permute-start(f32[64,9216]{1,0:T(8,128)} %joined.1), channel_id=1, source_target_pairs={{0,2},{2,4},{5,3},{7,5},{8,10},{10,12},{13,11},{15,13},{16,18},{18... | collective-permute-start | bytes 7077896 | tf_op jit(solution)/shard_map/ppermute | solution.py:533
  192.5 80.3 %collective-permute-start.14 = (f32[40,9216]{1,0:T(8,128)}, f32[40,9216]{1,0:T(8,128)}, u32[]{:S(2)}, u32[]{:S(2)}) collective-permute-start(f32[40,9216]{1,0:T(8,128)} %rows_of.8), channel_id=1, source_target_pairs={{0,1},{1,0},{2,3},{3,2},{4,5},{5,4},{6,7},{7,6},{8,9},{9,8},{10,11... | collective-permute-start | bytes 4423688 | tf_op jit(solution)/shard_map/ppermute | solution.py:533
  193.0 72.7 %collective-permute-start.15 = (f32[32,9216]{1,0:T(8,128)}, f32[32,9216]{1,0:T(8,128)S(1)}, u32[]{:S(2)}, u32[]{:S(2)}) collective-permute-start(f32[32,9216]{1,0:T(8,128)} %collective-permute-done.10.refs_2_), channel_id=1, source_target_pairs={{0,2},{2,4},{3,1},{4,6},{5,3},{7,5},{8,10},{10,12},{11,9},{12,14},... | collective-permute-start | bytes 3538952 | tf_op jit(solution)/shard_map/ppermute | solution.py:533
  243.0 41.6 %collective-permute-start.13 = (f32[16,9216]{1,0:T(8,128)S(1)}, f32[16,9216]{1,0:T(8,128)S(1)}, u32[]{:S(2)}, u32[]{:S(2)}) collective-permute-start(f32[16,9216]{1,0:T(8,128)S(1)} %rows_of.9), channel_id=1, source_target_pairs={{0,1},{1,0},{2,3},{3,2},{4,5},{5,4},{6,7},{7,6},{8,9},{9,8},{10,11... | collective-permute-start | bytes 1769480 | tf_op jit(solution)/shard_map/ppermute | solution.py:533
  271.1 13.5 %copy-start.14 = (f32[16]{0:T(128)S(1)}, f32[16]{0:T(128)}, u32[]{:S(2)}) copy-start(f32[16]{0:T(128)} %token_) | copy-start | bytes 196
  (10 other events, 47.9 us)
